TPU v7x, 32 devices: a whole 2x2x4 slice. The times are simulated.
32 devices in a mesh: wide: 8 (over z, x), narrow: 4 (over y, core).
Axes of the slice: x: 2, y: 2, z: 4, core: 2. Of those that a mesh axis runs over, the one named last changes fastest.
Arguments:
- tokens: bfloat16 [8192, 2048], P(('wide', 'narrow')), may hold values from -6 to 6
- documents: int32 [8, 1024], P('wide'), may hold values from 0 to 3, never falling along the last dimension, each value on 1 to 512 neighbouring positions
- head_level: int32 [8192], P(('wide', 'narrow')), may hold values from 0 to 3
- width_level: int32 [8192], P(('wide', 'narrow')), may hold values from 0 to 3
- mixer_gain: float32 [2048], replicated, may hold values from 0.5 to 1.5
- mixer_bias: float32 [2048], replicated, may hold values from -1.5 to 1.5
- input_weight: bfloat16 [2048, 6144], P(('wide', 'narrow')), may hold values from -0.125 to 0.125
- output_weight: bfloat16 [2048, 2048], P(('wide', 'narrow')), may hold values from -0.75 to 0.75
- mixer_router: float32 [2048, 4], replicated, may hold values from -0.125 to 0.125
- feed_gain: float32 [2048], replicated, may hold values from 0.5 to 1.5
- feed_bias: float32 [2048], replicated, may hold values from -1.5 to 1.5
- up_weight: bfloat16 [2048, 8192], P(('wide', 'narrow')), may hold values from -0.125 to 0.125
- down_weight: bfloat16 [8192, 2048], P(('wide', 'narrow')), may hold values from -0.0625 to 0.0625
- feed_router: float32 [2048, 4], replicated, may hold values from -0.125 to 0.125
- cotangent: bfloat16 [8192, 2048], P(('wide', 'narrow')), may hold values from -6 to 6
Outputs:
- outputs: bfloat16 [8192, 2048], P(('wide', 'narrow'))
- grad_tokens: float32 [8192, 2048], P(('wide', 'narrow'))
- grad_mixer_gain: float32 [2048], replicated
- grad_mixer_bias: float32 [2048], replicated
- grad_input_weight: float32 [2048, 6144], P(('wide', 'narrow'))
- grad_output_weight: float32 [2048, 2048], P(('wide', 'narrow'))
- grad_mixer_router: float32 [2048, 4], replicated
- grad_feed_gain: float32 [2048], replicated
- grad_feed_bias: float32 [2048], replicated
- grad_up_weight: float32 [2048, 8192], P(('wide', 'narrow'))
- grad_down_weight: float32 [8192, 2048], P(('wide', 'narrow'))
- grad_feed_router: float32 [2048, 4], replicated
- usage_counts: float32 [2, 4], replicated
Inputs may be any that keep to these rules, and one draw needn't show every extreme that they name: `documents`: along each sequence the document id never falls; a document has at most 512 positions, and one has exactly that many.
All inputs are finite; a program needn't handle non-finite values.
Results may differ from a plain program's by a relative error of at most 0.013.
Values may be sent and summed in bfloat16 or wider, within the bound.
No kernel may reach another device: no remote copies, remote signals or barrier semaphores. Data moves between devices by JAX's collectives and lax.ppermute only.
A program may use at most 448 MiB of HBM per device.

v0:
```python
import jax
import jax.numpy as jnp
from jax import lax
from jax.sharding import PartitionSpec as P

D = 2048
H = 16
HD = 128
FF = 8192
OPTIONS = 4


highest = lax.Precision.HIGHEST
epsilon = 1e-05
masked_score = -1e30


def normalize(values, gain_vec, shift_vec):
    centre = values - jnp.mean(values, axis=1, keepdims=True)
    inv_scale = lax.rsqrt(jnp.mean(centre * centre, axis=1, keepdims=True) + epsilon)
    normed = centre * inv_scale
    return (normed * gain_vec + shift_vec, normed, inv_scale)


def normalize_back(grad_hidden, normed, inv_scale, gain_vec):
    grad_normed = grad_hidden * gain_vec
    inner = (
        grad_normed
        - jnp.mean(grad_normed, axis=1, keepdims=True)
        - normed * jnp.mean(grad_normed * normed, axis=1, keepdims=True)
    )
    return (inv_scale * inner, jnp.sum(grad_hidden * normed, axis=0), jnp.sum(grad_hidden, axis=0))


def route(hidden, router, picked):
    logits = jnp.dot(hidden, router, precision=highest)
    shifted = jnp.exp(logits - jnp.max(logits, axis=1, keepdims=True))
    prob_rows = shifted / jnp.sum(shifted, axis=1, keepdims=True)
    chosen = (jnp.arange(router.shape[1])[None, :] == picked[:, None]).astype(jnp.float32)
    return (router.shape[1] * jnp.sum(prob_rows * chosen, axis=1), prob_rows, chosen)


def route_back(grad_gate, prob_rows, chosen, hidden, router):
    grad_prob = router.shape[1] * grad_gate[:, None] * chosen
    grad_logits = prob_rows * (grad_prob - jnp.sum(grad_prob * prob_rows, axis=1, keepdims=True))
    grad_router = jnp.dot(hidden.T, grad_logits, precision=highest)
    grad_hidden = jnp.dot(grad_logits, router.T, precision=highest)
    return (grad_router, grad_hidden)


def rope_tables(positions):
    half_width = HD // 2
    exponent = jnp.arange(half_width).astype(jnp.float32) * (-2.0 / HD)
    frequency = jnp.power(10000.0, exponent)
    angles = positions[:, None] * frequency[None, :]
    return (jnp.cos(angles), jnp.sin(angles))


def rotate(values, cos_table, sin_table):
    row_count = values.shape[0]
    by_heads = values.reshape(row_count, values.shape[1] // HD, HD)
    half_width = HD // 2
    lower_part = by_heads[:, :, :half_width]
    upper_part = by_heads[:, :, half_width:]
    cos_rows = cos_table[:, None, :]
    sin_rows = sin_table[:, None, :]
    rotated = jnp.concatenate(
        [
            lower_part * cos_rows - upper_part * sin_rows,
            upper_part * cos_rows + lower_part * sin_rows,
        ],
        axis=2,
    )
    return rotated.reshape(row_count, values.shape[1])


def grouped(matrix):
    return matrix.reshape(matrix.shape[0], H // 2, 2, HD).transpose(1, 0, 2, 3)


def ungrouped(stacked):
    return stacked.transpose(1, 0, 2, 3).reshape(stacked.shape[1], D)


def contract_last(left, right):
    return lax.dot_general(
        left, right, (((1,), (1,)), ((), ())), preferred_element_type=jnp.float32
    )


def contract_first(left, right):
    return lax.dot_general(
        left, right, (((0,), (0,)), ((), ())), preferred_element_type=jnp.float32
    )


def local(
    tokens,
    documents,
    head_level,
    width_level,
    mixer_gain,
    mixer_bias,
    input_weight,
    output_weight,
    mixer_router,
    feed_gain,
    feed_bias,
    up_weight,
    down_weight,
    feed_router,
    cotangent,
):
    local_rows = tokens.shape[0]
    seq_rows = documents.shape[1]
    narrow_rank = lax.axis_index("narrow")
    start_row = narrow_rank * local_rows
    positions = (start_row + jnp.arange(local_rows)).astype(jnp.float32)
    key_positions = jnp.arange(seq_rows).astype(jnp.float32)
    document_row = documents[0]
    query_docs = lax.dynamic_slice_in_dim(document_row, start_row, local_rows)
    visible = (query_docs[:, None] == document_row[None, :]) & (
        positions[:, None] >= key_positions[None, :]
    )
    scale_factor = HD ** (-0.5)
    level_range = jnp.arange(OPTIONS)
    head_counts = jnp.sum((head_level[:, None] == level_range[None, :]).astype(jnp.float32), axis=0)
    width_counts = jnp.sum(
        (width_level[:, None] == level_range[None, :]).astype(jnp.float32), axis=0
    )
    counts_local = jnp.stack([head_counts, width_counts])
    token_values = tokens.astype(jnp.float32)
    mixer_hidden, mixer_normed, mixer_scale = normalize(token_values, mixer_gain, mixer_bias)
    mixer_gate, mixer_probs, mixer_chosen = route(mixer_hidden, mixer_router, head_level)
    mixer_input = mixer_hidden.astype(jnp.bfloat16)
    input_full, output_full = (
        lax.all_gather(input_weight, ("wide", "narrow"), axis=0, tiled=True),
        lax.all_gather(output_weight, ("wide", "narrow"), axis=0, tiled=True),
    )
    projected = jnp.dot(mixer_input, input_full, preferred_element_type=jnp.float32)
    cos_table, sin_table = rope_tables(positions)
    queries = rotate(projected[:, :D], cos_table, sin_table).astype(jnp.bfloat16)
    keys_local = rotate(projected[:, D : 2 * D], cos_table, sin_table).astype(jnp.bfloat16)
    values_local = projected[:, 2 * D :].astype(jnp.bfloat16)
    keys_all, values_all = (
        lax.all_gather(keys_local, "narrow", axis=0, tiled=True),
        lax.all_gather(values_local, "narrow", axis=0, tiled=True),
    )

    def attend(pieces):
        query_part, key_part, value_part = pieces
        scores = (
            jnp.einsum("qhd,khd->hqk", query_part, key_part, preferred_element_type=jnp.float32)
            * scale_factor
        )
        scores = jnp.where(visible[None], scores, masked_score)
        top_score = jnp.max(scores, axis=2, keepdims=True)
        weights_exp = jnp.exp(scores - top_score)
        totals = jnp.sum(weights_exp, axis=2, keepdims=True)
        probs_low = (weights_exp / totals).astype(jnp.bfloat16)
        attended_part = jnp.einsum(
            "hqk,khd->qhd", probs_low, value_part, preferred_element_type=jnp.float32
        )
        return (attended_part, top_score[..., 0], totals[..., 0])

    attended_groups, top_groups, total_groups = lax.map(
        attend, (grouped(queries), grouped(keys_all), grouped(values_all))
    )
    attended = ungrouped(attended_groups)
    head_mask = (
        (jnp.arange(D) // HD)[None, :] < ((head_level + 1) * (H // OPTIONS))[:, None]
    ).astype(jnp.float32)
    mixed_input = (attended * head_mask).astype(jnp.bfloat16)
    mixer_branch = jnp.dot(mixed_input, output_full, preferred_element_type=jnp.float32)
    middle = token_values + mixer_gate[:, None] * mixer_branch
    feed_hidden, feed_normed, feed_scale = normalize(middle, feed_gain, feed_bias)
    feed_gate, feed_probs, feed_chosen = route(feed_hidden, feed_router, width_level)
    feed_input = feed_hidden.astype(jnp.bfloat16)
    up_full, down_full = (
        lax.all_gather(up_weight, ("wide", "narrow"), axis=0, tiled=True),
        lax.all_gather(down_weight, ("wide", "narrow"), axis=0, tiled=True),
    )
    lifted = jnp.dot(feed_input, up_full, preferred_element_type=jnp.float32)
    width_mask = (jnp.arange(FF)[None, :] < ((width_level + 1) * (FF // OPTIONS))[:, None]).astype(
        jnp.float32
    )
    rectified = jnp.maximum(lifted, 0.0)
    activated = (rectified * rectified * width_mask).astype(jnp.bfloat16)
    feed_branch = jnp.dot(activated, down_full, preferred_element_type=jnp.float32)
    outputs = (middle + feed_gate[:, None] * feed_branch).astype(jnp.bfloat16)
    upstream = cotangent.astype(jnp.float32)
    grad_feed_gate = jnp.sum(feed_branch * upstream, axis=1)
    grad_feed_branch = (feed_gate[:, None] * upstream).astype(jnp.bfloat16)
    grad_activated = contract_last(grad_feed_branch, down_full)
    grad_down_weight = lax.psum_scatter(
        contract_first(activated, grad_feed_branch),
        ("wide", "narrow"),
        scatter_dimension=0,
        tiled=True,
    )
    grad_lifted = (grad_activated * width_mask * 2.0 * rectified).astype(jnp.bfloat16)
    grad_feed_input = contract_last(grad_lifted, up_full)
    grad_up_weight = lax.psum_scatter(
        contract_first(feed_input, grad_lifted), ("wide", "narrow"), scatter_dimension=0, tiled=True
    )
    feed_router_term, grad_feed_routed = route_back(
        grad_feed_gate, feed_probs, feed_chosen, feed_hidden, feed_router
    )
    grad_middle_norm, feed_gain_term, feed_bias_term = normalize_back(
        grad_feed_input + grad_feed_routed, feed_normed, feed_scale, feed_gain
    )
    grad_middle = upstream + grad_middle_norm
    grad_mixer_gate = jnp.sum(mixer_branch * grad_middle, axis=1)
    grad_mixer_branch = (mixer_gate[:, None] * grad_middle).astype(jnp.bfloat16)
    grad_mixed = contract_last(grad_mixer_branch, output_full)
    grad_attended = (grad_mixed * head_mask).astype(jnp.bfloat16)

    def attend_back(pieces):
        query_part, key_part, value_part, grad_part, top_part, total_part = pieces
        scores = (
            jnp.einsum("qhd,khd->hqk", query_part, key_part, preferred_element_type=jnp.float32)
            * scale_factor
        )
        scores = jnp.where(visible[None], scores, masked_score)
        prob_block = jnp.exp(scores - top_part[..., None]) / total_part[..., None]
        probs_low = prob_block.astype(jnp.bfloat16)
        grad_prob = jnp.einsum(
            "qhd,khd->hqk", grad_part, value_part, preferred_element_type=jnp.float32
        )
        inner = jnp.sum(grad_prob * prob_block, axis=2, keepdims=True)
        grad_scores = (prob_block * (grad_prob - inner)).astype(jnp.bfloat16)
        grad_query = (
            jnp.einsum("hqk,khd->qhd", grad_scores, key_part, preferred_element_type=jnp.float32)
            * scale_factor
        )
        grad_key = (
            jnp.einsum("hqk,qhd->khd", grad_scores, query_part, preferred_element_type=jnp.float32)
            * scale_factor
        )
        grad_value = jnp.einsum(
            "hqk,qhd->khd", probs_low, grad_part, preferred_element_type=jnp.float32
        )
        return (grad_query, grad_key, grad_value)

    query_grads, key_grads, value_grads = lax.map(
        attend_back,
        (
            grouped(queries),
            grouped(keys_all),
            grouped(values_all),
            grouped(grad_attended),
            top_groups,
            total_groups,
        ),
    )
    key_sum, value_sum = (
        lax.psum_scatter(
            ungrouped(key_grads).astype(jnp.bfloat16), "narrow", scatter_dimension=0, tiled=True
        ).astype(jnp.float32),
        lax.psum_scatter(
            ungrouped(value_grads).astype(jnp.bfloat16), "narrow", scatter_dimension=0, tiled=True
        ).astype(jnp.float32),
    )
    grad_projected = jnp.concatenate(
        [
            rotate(ungrouped(query_grads), cos_table, -sin_table),
            rotate(key_sum, cos_table, -sin_table),
            value_sum,
        ],
        axis=1,
    ).astype(jnp.bfloat16)
    grad_mixer_input = contract_last(grad_projected, input_full)
    input_part = contract_first(mixer_input, grad_projected)
    output_part = contract_first(mixed_input, grad_mixer_branch)
    mixer_summed = lax.psum_scatter(
        jnp.concatenate([input_part, output_part], axis=1),
        ("wide", "narrow"),
        scatter_dimension=0,
        tiled=True,
    )
    grad_input_weight = mixer_summed[:, : 3 * D]
    grad_output_weight = mixer_summed[:, 3 * D :]
    mixer_router_term, grad_mixer_routed = route_back(
        grad_mixer_gate, mixer_probs, mixer_chosen, mixer_hidden, mixer_router
    )
    grad_token_norm, mixer_gain_term, mixer_bias_term = normalize_back(
        grad_mixer_input + grad_mixer_routed, mixer_normed, mixer_scale, mixer_gain
    )
    grad_tokens = grad_middle + grad_token_norm
    summed = lax.psum(
        (
            mixer_gain_term,
            mixer_bias_term,
            mixer_router_term,
            feed_gain_term,
            feed_bias_term,
            feed_router_term,
            counts_local,
        ),
        ("wide", "narrow"),
    )
    return (
        outputs,
        grad_tokens,
        summed[0],
        summed[1],
        grad_input_weight,
        grad_output_weight,
        summed[2],
        summed[3],
        summed[4],
        grad_up_weight,
        grad_down_weight,
        summed[5],
        summed[6],
    )


def solution(mesh):
    in_specs = (
        P(("wide", "narrow"), None),
        P("wide", None),
        P(("wide", "narrow")),
        P(("wide", "narrow")),
        P(),
        P(),
        P(("wide", "narrow"), None),
        P(("wide", "narrow"), None),
        P(),
        P(),
        P(),
        P(("wide", "narrow"), None),
        P(("wide", "narrow"), None),
        P(),
        P(("wide", "narrow"), None),
    )
    out_specs = (
        P(("wide", "narrow"), None),
        P(("wide", "narrow"), None),
        P(),
        P(),
        P(("wide", "narrow"), None),
        P(("wide", "narrow"), None),
        P(),
        P(),
        P(),
        P(("wide", "narrow"), None),
        P(("wide", "narrow"), None),
        P(),
        P(),
    )
    return jax.shard_map(local, mesh=mesh, in_specs=in_specs, out_specs=out_specs, check_vma=False)
```

profile of v0, /device:TPU:0, one launch (start us, length us, event | category | flops | bytes accessed | tf_op | source)
XLA Modules:
  0.0 3307.9 jit_solution(7561931648706109577)
XLA Ops:
  9.9 158.4 %all-gather.7.cloned.1.call-done = bf16[2048,6144]{1,0:T(8,128)(2,1)} async-done(((bf16[64,6144]{1,0:T(8,128)(2,1)}), bf16[2048,6144]{1,0:T(8,128)(2,1)}) %all-gather.7.cloned.1.call-update) | async-done | bytes 25165840 | tf_op jit(solution)/shard_map/all_gather | solution.py:137
  168.3 11.7 fusion.141
  180.1 2.6 copy-done.9
  185.2 2.8 slice_bitcast_fusion
  200.3 16.3 all-gather.9.cloned.1.call-done
  216.7 7.9 reshape.249
  224.6 11.3 copy.63
  235.9 5.2 copy.76
  241.1 12.8 all-gather.11.cloned.1.call-done
  253.9 6.5 copy.49
  260.4 36.1 %while.32 = (s32[]{:T(128)}, bf16[8,256,2,128]{1,3,2,0:T(8,128)(2,1)S(1)}, f32[8,2,256]{2,1,0:T(2,128)S(1)}, f32[8,2,256]{2,1,0:T(2,128)S(1)}, bf16[8,1024,2,128...) while((s32[]{:T(128)}, ...), condition=%wide.region_8.9_spmd.clone.clone, body=%wide.region_5.8_spmd.clone.sunk.clone | while | flops 275512320 | bytes 8812665 | solution.py:166
  299.0 35.2 %all-gather.13.cloned.1.call-done = bf16[2048,2048]{1,0:T(8,128)(2,1)} async-done(((bf16[64,2048]{1,0:T(8,128)(2,1)}), bf16[2048,2048]{1,0:T(8,128)(2,1)}) %all-gather.13.cloned.1.call-update) | async-done | bytes 8388624 | tf_op jit(solution)/shard_map/all_gather | solution.py:138
  334.2 5.9 fusion.144
  343.3 187.0 %all-gather.15.cloned.1.call-done = bf16[2048,8192]{1,0:T(8,128)(2,1)} async-done(((bf16[64,8192]{1,0:T(8,128)(2,1)}), bf16[2048,8192]{1,0:T(8,128)(2,1)}) %all-gather.15.cloned.1.call-update) | async-done | bytes 33554448 | tf_op jit(solution)/shard_map/all_gather | solution.py:180
  530.3 17.8 convolution_maximum_fusion
  548.1 177.9 %all-gather.17.cloned.1.call-done = bf16[8192,2048]{1,0:T(8,128)(2,1)} async-done(((bf16[256,2048]{1,0:T(8,128)(2,1)}), bf16[8192,2048]{1,0:T(8,128)(2,1)}) %all-gather.17.cloned.1.call-update) | async-done | bytes 33554448 | tf_op jit(solution)/shard_map/all_gather | solution.py:181
  726.0 19.2 fusion.74
  745.8 18.8 fusion.52
  764.6 17.0 fusion.151
  781.7 4.8 multiply_reduce_fusion.1
  790.1 6.7 fusion.53
  796.8 2.6 reshape.254
  799.4 2.5 copy.77
  801.9 83.8 %while.33 = (s32[]{:T(128)}, f32[8,256,2,128]{1,3,2,0:T(8,128)}, bf16[8,1024,2,128]{1,3,2,0:T(8,128)(2,1)}, bf16[8,1024,2,128]{1,3,2,0:T(8,128)(2,1)}, bf16[8,10...) while((s32[]{:T(128)}, f32[8,256,2,128]{1,3,2,0:T(8,128)}, ...), condition=%wide.region_20.21_spmd.clone.clone, body=%wide.region_18.20_spmd.clone.sunk.clone | while | flops 677445120 | bytes 20741264 | solution.py:245
  886.7 3.2 fusion.147
  889.8 3.7 copy.69
  893.5 3.8 copy.68
  897.3 10.6 fusion.136
  907.9 20.6 reduce-scatter.6.cloned.1.call-done
  928.5 2.8 fusion.148
  931.3 3.7 copy.71
  935.0 3.7 copy.70
  938.7 7.0 subtract_convert_fusion.1
  949.7 3.4 pad_maximum_fusion.7
  953.1 2.4 copy.67
  955.5 20.2 reduce-scatter.8.cloned.1.call-done
  975.7 19.6 fusion.78
  995.3 43.4 %pad_maximum_fusion = f32[2048,8192]{1,0:T(8,128)} fusion(f32[2048,2048]{1,0:T(8,128)} %fusion.136, f32[2048,6144]{1,0:T(8,128)} %fusion.78), kind=kLoop, calls=%fused_computation.64 | loop fusion | flops 16777216 | bytes 134217728 | tf_op jit(solution)/shard_map/concatenate | solution.py:276
  1044.3 14.0 fusion.79
  1058.3 6.1 fusion.70
  1064.8 27.9 fusion.92
  1092.8 26.0 fusion.95
  1120.4 3.7 fusion.69
  1124.1 617.2 %reduce-scatter.10.cloned.1.call-done = f32[64,8192]{1,0:T(8,128)} async-done(((f32[2048,8192]{1,0:T(8,128)}), f32[64,8192]{1,0:T(8,128)}) %reduce-scatter.10.cloned.1.call-update) | async-done | bytes 2097168 | tf_op jit(solution)/shard_map/reduce_scatter | solution.py:275
  1743.2 2.7 slice.64
  1745.8 130.2 %all-reduce.3.cloned.1.call-done = (f32[2048]{0:T(1024)}, f32[2048]{0:T(1024)}, f32[2048,4]{0,1:T(4,128)}, f32[2048]{0:T(1024)}, f32[2048]{0:T(1024)}, /*index=5*/f32[2048,4]{0,1:T(4,128)}, f32[2,4]{1,0:T(2,128)}) async-done(((f32[2048]{0:T(1024)}, f32[2048]{0:T(1024)}, f32[2048,4]{0,1:T(4,128)}, f32[2048]{0:T(1024)}, f32[2048]{0:T(1024)}, /*index=5*/f32[2048,4]{0,1:T(4,128)}, f32[2,4]{1,0:T(2,128)}), ...) | async-done | bytes 98352 | tf_op jit(solution)/shard_map/psum | solution.py:290
  1876.1 706.5 %reduce-scatter.14.cloned.1.call-done = f32[256,2048]{1,0:T(8,128)} async-done(((f32[8192,2048]{1,0:T(8,128)}), f32[256,2048]{1,0:T(8,128)}) %reduce-scatter.14.cloned.1.call-update) | async-done | bytes 2097168 | tf_op jit(solution)/shard_map/reduce_scatter | solution.py:195
  2582.6 708.8 %reduce-scatter.12.cloned.1.call-done = f32[64,8192]{1,0:T(8,128)} async-done(((f32[2048,8192]{1,0:T(8,128)}), f32[64,8192]{1,0:T(8,128)}) %reduce-scatter.12.cloned.1.call-update) | async-done | bytes 2097168 | tf_op jit(solution)/shard_map/reduce_scatter | solution.py:203
  (264 shorter events, 170.0 us)
Async XLA Ops:
  7.2 334.3 %copy-start = (f32[2048,4]{0,1:T(4,128)S(1)}, f32[2048,4]{0,1:T(4,128)}, u32[]{:S(2)}) copy-start(f32[2048,4]{0,1:T(4,128)} %param.32) | copy-start | bytes 98308
  7.2 2.3 copy-start.2
  7.2 161.1 %copy-start.16 = (f32[2048]{0:T(1024)S(1)}, f32[2048]{0:T(1024)}, u32[]{:S(2)}) copy-start(f32[2048]{0:T(1024)} %param.23) | copy-start | bytes 24580
  7.2 161.1 %copy-start.18 = (f32[2048]{0:T(1024)S(1)}, f32[2048]{0:T(1024)}, u32[]{:S(2)}) copy-start(f32[2048]{0:T(1024)} %param.24) | copy-start | bytes 24580
  7.2 161.1 %all-gather.7.cloned.1.call-start = ((), (), s32[]{:S(2)}) async-start(), calls=%async_computation.5 | async-start | bytes 25952256 | tf_op jit(solution)/shard_map/all_gather | solution.py:137
  8.0 208.7 %all-gather.9.cloned.1.call-start = ((), (), s32[]{:S(2)}) async-start(), calls=%async_computation.6 | async-start | bytes 5242880 | tf_op jit(solution)/shard_map/all_gather | solution.py:147
  9.5 186.5 %copy-start.24 = (f32[256]{0:T(256)}, f32[256]{0:T(256)S(1)}, u32[]{:S(2)}) copy-start(f32[256]{0:T(256)S(1)} %broadcast_multiply_fusion.9) | copy-start | bytes 3076
  9.9 186.0 %copy-start.26 = (f32[256]{0:T(256)}, f32[256]{0:T(256)S(1)}, u32[]{:S(2)}) copy-start(f32[256]{0:T(256)S(1)} %add_rsqrt_fusion.1) | copy-start | bytes 3076
  180.1 2.7 copy-start.9
  183.9 70.0 %all-gather.11.cloned.1.call-start = ((), (), s32[]{:S(2)}) async-start(), calls=%async_computation.7 | async-start | bytes 5242880 | tf_op jit(solution)/shard_map/all_gather | solution.py:146
  185.2 3.5 copy-start.13
  194.0 1.9 copy-start.23
  194.0 2.0 copy-start.37
  194.0 140.2 %all-gather.13.cloned.1.call-start = ((), (), s32[]{:S(2)}) async-start(), calls=%async_computation.8 | async-start | bytes 8650752 | tf_op jit(solution)/shard_map/all_gather | solution.py:138
  194.6 335.7 %all-gather.15.cloned.1.call-start = ((), (), s32[]{:S(2)}) async-start(), calls=%async_computation.9 | async-start | bytes 34603008 | tf_op jit(solution)/shard_map/all_gather | solution.py:180
  195.2 3.0 copy-start.31
  195.2 3.0 copy-start.34
  195.2 530.8 %all-gather.17.cloned.1.call-start = ((), (), s32[]{:S(2)}) async-start(), calls=%async_computation.10 | async-start | bytes 34603008 | tf_op jit(solution)/shard_map/all_gather | solution.py:181
  195.8 732.7 %reduce-scatter.6.cloned.1.call-start = ((), (), s32[]{:S(2)}) async-start(), calls=%async_computation.11 | async-start | bytes 5242880 | tf_op jit(solution)/shard_map/reduce_scatter | solution.py:257
  198.2 547.7 %copy-start.28 = (s32[256]{0:T(256)}, s32[256]{0:T(256)S(1)}, u32[]{:S(2)}) copy-start(s32[256]{0:T(256)S(1)} %add_multiply_fusion) | copy-start | bytes 3076
  296.5 1.0 copy-start.11
  296.5 43.6 %copy-start.7 = (bf16[8,256,2,128]{3,1,2,0:T(8,128)(2,1)}, bf16[8,256,2,128]{3,1,2,0:T(8,128)(2,1)S(1)}, u32[]{:S(2)}) copy-start(bf16[8,256,2,128]{3,1,2,0:T(8,128)(2,1)S(1)} %get-tuple-element.681) | copy-start | bytes 3145732
  299.0 41.2 %copy-start.8 = (bf16[256,2048]{1,0:T(8,128)(2,1)}, bf16[256,2048]{1,0:T(8,128)(2,1)S(1)}, u32[]{:S(2)}) copy-start(bf16[256,2048]{1,0:T(8,128)(2,1)S(1)} %copy.64) | copy-start | bytes 3145732
  340.1 1.3 copy-start.5
  340.7 0.8 copy-start.20
  745.8 40.6 %copy-start.32 = (f32[256]{0:T(256)}, f32[256]{0:T(256)S(1)}, u32[]{:S(2)}) copy-start(f32[256]{0:T(256)S(1)} %broadcast_multiply_fusion.2) | copy-start | bytes 3076
  781.6 4.8 copy-start.6
  781.6 4.8 copy-start.10
  781.7 4.8 copy-start.12
  788.8 1.3 copy-start.3
  885.6 90.1 %reduce-scatter.8.cloned.1.call-start = ((), (), s32[]{:S(2)}) async-start(), calls=%async_computation.12 | async-start | bytes 5242880 | tf_op jit(solution)/shard_map/reduce_scatter | solution.py:260
  886.4 854.9 %reduce-scatter.10.cloned.1.call-start = ((), (), s32[]{:S(2)}) async-start(), calls=%async_computation.13 | async-start | bytes 69206016 | tf_op jit(solution)/shard_map/reduce_scatter | solution.py:275
  935.0 3.7 copy-start.14
  935.0 3.7 copy-start.22
  949.7 26.0 copy-start.17
  949.7 26.0 copy-start.19
  949.7 26.0 copy-start.25
  949.7 26.0 copy-start.27
  1038.8 0.8 copy-start.36
  1038.8 3.5 copy-start.21
  1038.8 837.2 %all-reduce.3.cloned.1.call-start = ((), (), s32[]{:S(2)}) async-start(), calls=%async_computation.16 | async-start | bytes 198656 | tf_op jit(solution)/shard_map/psum | solution.py:290
  1044.3 14.0 copy-start.38
  1058.3 6.5 copy-start.29
  1058.3 6.5 copy-start.33
  1064.5 1518.1 %reduce-scatter.14.cloned.1.call-start = ((), (), s32[]{:S(2)}) async-start(), calls=%async_computation.15 | async-start | bytes 69206016 | tf_op jit(solution)/shard_map/reduce_scatter | solution.py:195
  1092.7 2198.7 %reduce-scatter.12.cloned.1.call-start = ((), (), s32[]{:S(2)}) async-start(), calls=%async_computation.14 | async-start | bytes 69206016 | tf_op jit(solution)/shard_map/reduce_scatter | solution.py:203
  1118.8 1.6 copy-start.4
  1120.4 2180.2 %copy-start.1 = (f32[2048,4]{0,1:T(4,128)S(1)}, f32[2048,4]{0,1:T(4,128)}, u32[]{:S(2)}) copy-start(f32[2048,4]{0,1:T(4,128)} %param.32) | copy-start | bytes 98308
  (3 other events, 2.1 us)
Sparse Core Ops, SparseCore 0:
  11.0 157.3 all-gather.6
  184.0 32.6 all-gather.8
  218.8 35.0 all-gather.10
  256.6 77.5 all-gather.12
  336.9 193.3 all-gather.14
  533.0 192.9 all-gather.16
  885.8 42.6 reduce-scatter.5
  931.2 44.5 reduce-scatter.7
  1038.9 702.3 reduce-scatter.9
  1748.7 127.3 all-reduce.2
  1879.1 703.4 reduce-scatter.13
  2585.5 705.8 reduce-scatter.11
where the time goes:
time: 3320 us; the launch traced here: 3310 us
  waiting for transfers between devices  2790 us (84%)
  matrix products  322 us (10%)
  local copies, waits for them, and re-layouts  91.9 us (3%)
  other arithmetic  82.9 us (2%)
    reduce_scatter x1, waiting for transfers between devices, local(): lax.psum_scatter(contract_first(feed_input, grad_lifted), ('wide', 'narro...  709 us
    reduce_scatter x1, waiting for transfers between devices, local(): lax.psum_scatter(contract_first(activated, grad_feed_branch), ('wide', 'n...  707 us
    reduce_scatter x1, waiting for transfers between devices, local(): lax.psum_scatter(jnp.concatenate([input_part, output_part], axis=1), ('wi...  617 us
    all_gather x1, waiting for transfers between devices, local(): lax.all_gather(up_weight, ('wide', 'narrow'), axis=0, tiled=True)  187 us
    all_gather x1, waiting for transfers between devices, local(): lax.all_gather(down_weight, ('wide', 'narrow'), axis=0, tiled=True)  178 us
    all_gather x1, waiting for transfers between devices, local(): lax.all_gather(input_weight, ('wide', 'narrow'), axis=0, tiled=True)  158 us
    psum x1, waiting for transfers between devices, local(): lax.psum((mixer_gain_term, mixer_bias_term, mixer_router_term, feed_gain_...  130 us
    dot_general x4, matrix products, contract_first(): lax.dot_general(left, right, (((0,), (0,)), ((), ())), preferred_element_...  84.1 us
  transfers between devices with their start and end apart: 12, of which 12 were waited for; matrix products, arithmetic and copies ran while one was open for 7% of the time, Pallas kernels for 0%

commit v1 on v0

v1 whole, which is shorter than its diff:
```python
import functools

import jax
import jax.numpy as jnp
from jax import lax
from jax.experimental import pallas as pl
from jax.experimental.pallas import tpu as pltpu
from jax.sharding import Mesh, PartitionSpec as P

D = 2048
H = 16
HD = 128
FF = 8192
OPTIONS = 4
LONGEST = 512

PLANE = ("x", "y", "c")
ALL = ("z", "x", "y", "c")
GROUP = 8
SHARE = D // GROUP

highest = lax.Precision.HIGHEST
epsilon = 1e-05
masked_score = -1e30
f32 = jnp.float32
bf16 = jnp.bfloat16


def normalize(values, gain_vec, shift_vec):
    centre = values - jnp.mean(values, axis=1, keepdims=True)
    inv_scale = lax.rsqrt(jnp.mean(centre * centre, axis=1, keepdims=True) + epsilon)
    normed = centre * inv_scale
    return (normed * gain_vec + shift_vec, normed, inv_scale)


def normalize_back(grad_hidden, normed, inv_scale, gain_vec):
    grad_normed = grad_hidden * gain_vec
    inner = (
        grad_normed
        - jnp.mean(grad_normed, axis=1, keepdims=True)
        - normed * jnp.mean(grad_normed * normed, axis=1, keepdims=True)
    )
    return (inv_scale * inner, jnp.sum(grad_hidden * normed, axis=0), jnp.sum(grad_hidden, axis=0))


def route(hidden, router, picked):
    logits = jnp.dot(hidden, router, precision=highest)
    shifted = jnp.exp(logits - jnp.max(logits, axis=1, keepdims=True))
    prob_rows = shifted / jnp.sum(shifted, axis=1, keepdims=True)
    chosen = (jnp.arange(router.shape[1])[None, :] == picked[:, None]).astype(f32)
    return (router.shape[1] * jnp.sum(prob_rows * chosen, axis=1), prob_rows, chosen)


def route_back(grad_gate, prob_rows, chosen, hidden, router):
    grad_prob = router.shape[1] * grad_gate[:, None] * chosen
    grad_logits = prob_rows * (grad_prob - jnp.sum(grad_prob * prob_rows, axis=1, keepdims=True))
    grad_router = lax.dot_general(
        grad_logits, hidden, (((0,), (0,)), ((), ())), precision=highest
    )
    grad_hidden = jnp.dot(grad_logits, router.T, precision=highest)
    return (grad_router, grad_hidden)


def rope_tables(positions):
    half_width = HD // 2
    exponent = jnp.arange(half_width).astype(f32) * (-2.0 / HD)
    frequency = jnp.power(10000.0, exponent)
    angles = positions[:, None] * frequency[None, :]
    cos_half, sin_half = jnp.cos(angles), jnp.sin(angles)
    return (
        jnp.concatenate([cos_half, cos_half], axis=1),
        jnp.concatenate([-sin_half, sin_half], axis=1),
    )


def dot_plain(left, right):
    return jnp.dot(left, right, preferred_element_type=f32)


def contract_last(left, right):
    return lax.dot_general(left, right, (((1,), (1,)), ((), ())), preferred_element_type=f32)


def contract_first(left, right):
    return lax.dot_general(left, right, (((0,), (0,)), ((), ())), preferred_element_type=f32)


def flip(values, axis):
    return lax.ppermute(values, axis, [(0, 1), (1, 0)])


def plane_gather(values):
    half = values.shape[0] // 2
    from_x, from_y, from_c = flip(values, "x"), flip(values, "y"), flip(values, "c")
    diagonal = jnp.concatenate([flip(from_y[:half], "x"), flip(from_x[half:], "y")], axis=0)
    return [
        values,
        from_c,
        from_y,
        flip(from_y, "c"),
        from_x,
        flip(from_x, "c"),
        diagonal,
        flip(diagonal, "c"),
    ]


def plane_scatter(parts):
    sums = {}
    for dx in (1, 0):
        for dy in (1, 0):
            at = dx * 4 + dy * 2
            sums[dx, dy] = parts[at].astype(f32) + flip(parts[at + 1].astype(bf16), "c").astype(f32)
    half = sums[1, 1].shape[0] // 2
    diagonal = sums[1, 1].astype(bf16)
    by_x, by_y = flip(diagonal[:half], "x"), flip(diagonal[half:], "y")
    to_y = jnp.concatenate([sums[0, 1][:half] + by_x.astype(f32), sums[0, 1][half:]], axis=0)
    to_x = jnp.concatenate([sums[1, 0][:half], sums[1, 0][half:] + by_y.astype(f32)], axis=0)
    return (
        sums[0, 0]
        + flip(to_x.astype(bf16), "x").astype(f32)
        + flip(to_y.astype(bf16), "y").astype(f32)
    )


def sum_everywhere(values, planes):
    for axis in ("c", "y", "x"):
        values = values + flip(values, axis)
    if planes & (planes - 1):
        return lax.psum(values, "z")
    step = 1
    while step < planes:
        values = values + lax.ppermute(values, "z", [(i, i ^ step) for i in range(planes)])
        step *= 2
    return values


def swap_plane(values):
    return lax.all_to_all(values, PLANE, 0, 0, tiled=True)


def key_blocks(block, rows):
    return range(max(0, (block * rows - (LONGEST - 1)) // rows), block + 1)


def visible(start_col, block, key_block, rows):
    key_pos = key_block * rows + lax.broadcasted_iota(jnp.int32, (rows, rows), 1)
    seen = key_pos >= start_col
    if key_block == block:
        seen &= key_pos <= block * rows + lax.broadcasted_iota(jnp.int32, (rows, rows), 0)
    return seen


def softmax_blocks(query, rot_ref, start_col, block, rows, key_at):
    scores = []
    for key_block in key_blocks(block, rows):
        keys = rot_ref[key_block * rows : (key_block + 1) * rows, key_at : key_at + HD]
        piece = contract_last(query, keys) * HD ** (-0.5)
        scores.append(
            jnp.where(visible(start_col, block, key_block, rows), piece, masked_score)
        )
    top = functools.reduce(
        jnp.maximum, [jnp.max(piece, axis=1, keepdims=True) for piece in scores]
    )
    weights = [jnp.exp(piece - top) for piece in scores]
    total = functools.reduce(
        jnp.add, [jnp.sum(piece, axis=1, keepdims=True) for piece in weights]
    )
    inverse = 1.0 / total
    return [piece * inverse for piece in weights]


def attend_kernel(rows, blocks, place_ref, start_ref, cos_ref, sin_ref, proj_ref, rot_ref, out_ref):
    quarter = place_ref[1]
    for block in range(blocks):
        here = slice(block * rows, (block + 1) * rows)
        there = pl.ds(pl.multiple_of((block ^ quarter) * rows, rows), rows)
        cos_rows, sin_rows = cos_ref[here, :], sin_ref[here, :]
        for col in range(0, 2 * SHARE, HD):
            piece = proj_ref[there, col : col + HD]
            turned = piece * cos_rows + pltpu.roll(piece, HD // 2, 1) * sin_rows
            rot_ref[here, col : col + HD] = turned.astype(bf16)
        rot_ref[here, 2 * SHARE :] = proj_ref[there, 2 * SHARE :].astype(bf16)
    for head in range(0, SHARE, HD):
        for block in range(blocks):
            here = slice(block * rows, (block + 1) * rows)
            query = rot_ref[here, head : head + HD]
            probs = softmax_blocks(query, rot_ref, start_ref[here, :], block, rows, SHARE + head)
            total = None
            for key_block, piece in zip(key_blocks(block, rows), probs):
                values = rot_ref[
                    key_block * rows : (key_block + 1) * rows,
                    2 * SHARE + head : 2 * SHARE + head + HD,
                ]
                term = dot_plain(piece.astype(bf16), values)
                total = term if total is None else total + term
            out_ref[here, head : head + HD] = total.astype(bf16)


def attend_back_kernel(
    rows, blocks, place_ref, start_ref, cos_ref, sin_ref, rot_ref, grad_ref, out_ref, key_acc, value_acc
):
    quarter = place_ref[1]
    scale = HD ** (-0.5)

    def turn_back(piece, here):
        return piece * cos_ref[here, :] - pltpu.roll(piece, HD // 2, 1) * sin_ref[here, :]

    for head in range(0, SHARE, HD):
        key_at, value_at = SHARE + head, 2 * SHARE + head
        key_acc[...] = jnp.zeros_like(key_acc)
        value_acc[...] = jnp.zeros_like(value_acc)
        for block in range(blocks):
            here = slice(block * rows, (block + 1) * rows)
            there = pl.ds(pl.multiple_of((block ^ quarter) * rows, rows), rows)
            query = rot_ref[here, head : head + HD]
            grad = grad_ref[here, head : head + HD]
            probs = softmax_blocks(query, rot_ref, start_ref[here, :], block, rows, key_at)
            grad_probs, inner = [], None
            for key_block, piece in zip(key_blocks(block, rows), probs):
                keys_at = slice(key_block * rows, (key_block + 1) * rows)
                grad_piece = contract_last(grad, rot_ref[keys_at, value_at : value_at + HD])
                grad_probs.append(grad_piece)
                term = jnp.sum(grad_piece * piece, axis=1, keepdims=True)
                inner = term if inner is None else inner + term
            query_grad = None
            for key_block, piece, grad_piece in zip(key_blocks(block, rows), probs, grad_probs):
                keys_at = slice(key_block * rows, (key_block + 1) * rows)
                grad_scores = (piece * (grad_piece - inner)).astype(bf16)
                term = dot_plain(grad_scores, rot_ref[keys_at, key_at : key_at + HD])
                query_grad = term if query_grad is None else query_grad + term
                key_acc[keys_at, :] += contract_first(grad_scores, query)
                value_acc[keys_at, :] += contract_first(piece.astype(bf16), grad)
            out_ref[there, head : head + HD] = turn_back(query_grad * scale, here).astype(bf16)
        for block in range(blocks):
            here = slice(block * rows, (block + 1) * rows)
            there = pl.ds(pl.multiple_of((block ^ quarter) * rows, rows), rows)
            out_ref[there, key_at : key_at + HD] = turn_back(
                key_acc[here, :] * scale, here
            ).astype(bf16)
            out_ref[there, value_at : value_at + HD] = value_acc[here, :].astype(bf16)


def attend(place, starts, cos_table, sin_table, projected, rows):
    seq_rows = cos_table.shape[0]
    body = functools.partial(attend_kernel, rows, seq_rows // rows)
    return pl.pallas_call(
        body,
        grid_spec=pltpu.PrefetchScalarGridSpec(
            num_scalar_prefetch=1,
            grid=(2,),
            in_specs=[
                pl.BlockSpec((None, seq_rows, 1), lambda s, place: (s ^ place[0], 0, 0)),
                pl.BlockSpec((seq_rows, HD), lambda s, place: (0, 0)),
                pl.BlockSpec((seq_rows, HD), lambda s, place: (0, 0)),
                pl.BlockSpec((seq_rows, 3 * SHARE), lambda s, place: (s, 0)),
            ],
            out_specs=[
                pl.BlockSpec((seq_rows, 3 * SHARE), lambda s, place: (s, 0)),
                pl.BlockSpec((seq_rows, SHARE), lambda s, place: (s ^ place[0], 0)),
            ],
        ),
        out_shape=[
            jax.ShapeDtypeStruct((2 * seq_rows, 3 * SHARE), bf16),
            jax.ShapeDtypeStruct((2 * seq_rows, SHARE), bf16),
        ],
        compiler_params=pltpu.CompilerParams(vmem_limit_bytes=48 * 1024 * 1024),
        cost_estimate=pl.CostEstimate(
            flops=4 * 4 * seq_rows * seq_rows * HD, bytes_accessed=16 * 2**20, transcendentals=2**21
        ),
    )(place, starts, cos_table, sin_table, projected)


def attend_back(place, starts, cos_table, sin_table, rotated, grad, rows):
    seq_rows = cos_table.shape[0]
    body = functools.partial(attend_back_kernel, rows, seq_rows // rows)
    return pl.pallas_call(
        body,
        grid_spec=pltpu.PrefetchScalarGridSpec(
            num_scalar_prefetch=1,
            grid=(2,),
            in_specs=[
                pl.BlockSpec((None, seq_rows, 1), lambda s, place: (s ^ place[0], 0, 0)),
                pl.BlockSpec((seq_rows, HD), lambda s, place: (0, 0)),
                pl.BlockSpec((seq_rows, HD), lambda s, place: (0, 0)),
                pl.BlockSpec((seq_rows, 3 * SHARE), lambda s, place: (s, 0)),
                pl.BlockSpec((seq_rows, SHARE), lambda s, place: (s ^ place[0], 0)),
            ],
            out_specs=pl.BlockSpec((seq_rows, 3 * SHARE), lambda s, place: (s, 0)),
            scratch_shapes=[pltpu.VMEM((seq_rows, HD), f32), pltpu.VMEM((seq_rows, HD), f32)],
        ),
        out_shape=jax.ShapeDtypeStruct((2 * seq_rows, 3 * SHARE), bf16),
        compiler_params=pltpu.CompilerParams(vmem_limit_bytes=48 * 1024 * 1024),
        cost_estimate=pl.CostEstimate(
            flops=10 * 4 * seq_rows * seq_rows * HD, bytes_accessed=16 * 2**20, transcendentals=2**21
        ),
    )(place, starts, cos_table, sin_table, rotated, grad)


def local(
    planes,
    tokens,
    documents,
    head_level,
    width_level,
    mixer_gain,
    mixer_bias,
    input_weight,
    output_weight,
    mixer_router,
    feed_gain,
    feed_bias,
    up_weight,
    down_weight,
    feed_router,
    cotangent,
):
    rows = tokens.shape[0]
    seq_rows = documents.shape[1]
    quarters = seq_rows // rows
    weight_rows = input_weight.shape[0]
    unit_rows = down_weight.shape[0]
    at_x = lax.axis_index("x")
    quarter = lax.axis_index("y") * 2 + lax.axis_index("c")
    at_plane = at_x * quarters + quarter
    place = jnp.stack([at_x, quarter]).astype(jnp.int32)
    chunk_order = at_plane ^ jnp.arange(GROUP)

    whole = lax.all_gather(
        jnp.concatenate([documents[0], width_level])[None], PLANE, axis=0, tiled=True
    )
    plane_docs = jnp.stack([whole[0, :seq_rows], whole[quarters, :seq_rows]])
    width_all = whole[:, seq_rows:][chunk_order].reshape(GROUP * rows)
    starts = jnp.sum(
        (plane_docs[:, None, :] < plane_docs[:, :, None]).astype(jnp.int32), axis=2
    )[:, :, None]
    level_range = jnp.arange(OPTIONS)
    head_counts = jnp.sum((head_level[:, None] == level_range[None, :]).astype(f32), axis=0)
    width_counts = jnp.sum((width_level[:, None] == level_range[None, :]).astype(f32), axis=0)

    input_share = swap_plane(
        input_weight.reshape(weight_rows, 3, GROUP, SHARE)
        .transpose(2, 0, 1, 3)
        .reshape(GROUP * weight_rows, 3 * SHARE)
    )
    input_share = lax.all_gather(input_share, "z", axis=0, tiled=True)
    output_full = lax.all_gather(output_weight, ALL, axis=0, tiled=True)
    up_share = swap_plane(
        up_weight.reshape(weight_rows, planes, GROUP, unit_rows)
        .transpose(2, 0, 1, 3)
        .reshape(GROUP * weight_rows, planes * unit_rows)
    )
    up_share = lax.all_gather(up_share, "z", axis=0, tiled=True)
    down_share = lax.all_gather(down_weight, "z", axis=0, tiled=True)

    token_values = tokens.astype(f32)
    mixer_hidden, mixer_normed, mixer_scale = normalize(token_values, mixer_gain, mixer_bias)
    mixer_gate, mixer_probs, mixer_chosen = route(mixer_hidden, mixer_router, head_level)
    mixer_all = jnp.concatenate(plane_gather(mixer_hidden.astype(bf16)), axis=0)
    projected = dot_plain(mixer_all, input_share)
    cos_table, sin_table = rope_tables(jnp.arange(seq_rows).astype(f32))
    rotated, attended = attend(place, starts, cos_table, sin_table, projected, rows)

    def by_token(values):
        return (
            swap_plane(values).reshape(GROUP, rows, SHARE).transpose(1, 0, 2).reshape(rows, D)
        )

    def by_head(values):
        return swap_plane(
            values.reshape(rows, GROUP, SHARE).transpose(1, 0, 2).reshape(GROUP * rows, SHARE)
        )

    head_mask = (
        (jnp.arange(D) // HD)[None, :] < ((head_level + 1) * (H // OPTIONS))[:, None]
    ).astype(bf16)
    mixed_input = by_token(attended) * head_mask
    mixer_branch = dot_plain(mixed_input, output_full)
    middle = token_values + mixer_gate[:, None] * mixer_branch
    feed_hidden, feed_normed, feed_scale = normalize(middle, feed_gain, feed_bias)
    feed_gate, feed_probs, feed_chosen = route(feed_hidden, feed_router, width_level)
    upstream = cotangent.astype(f32)

    feed_all = jnp.concatenate(plane_gather(feed_hidden.astype(bf16)), axis=0)
    upstream_all = jnp.concatenate(plane_gather(cotangent), axis=0)
    gate_all = jnp.concatenate(plane_gather(feed_gate.reshape(2, rows // 2)), axis=0).reshape(
        GROUP * rows
    )
    lifted = dot_plain(feed_all, up_share)
    unit = jnp.arange(planes * unit_rows)
    unit = (unit // unit_rows * GROUP + at_plane) * unit_rows + unit % unit_rows
    width_mask = (unit[None, :] < ((width_all + 1) * (FF // OPTIONS))[:, None]).astype(f32)
    rectified = jnp.maximum(lifted, 0.0)
    activated = (rectified * rectified * width_mask).astype(bf16)

    def pieces(values):
        return [values[d * rows : (d + 1) * rows] for d in range(GROUP)]

    feed_branch = plane_scatter(pieces(dot_plain(activated, down_share).astype(bf16)))
    grad_branch_all = (gate_all[:, None] * upstream_all.astype(f32)).astype(bf16)
    grad_activated = contract_last(grad_branch_all, down_share)
    grad_lifted = (grad_activated * width_mask * 2.0 * rectified).astype(bf16)
    grad_feed_input = plane_scatter(pieces(contract_last(grad_lifted, up_share).astype(bf16)))
    grad_down_weight = lax.psum_scatter(
        contract_first(activated, grad_branch_all).astype(bf16),
        "z",
        scatter_dimension=0,
        tiled=True,
    ).astype(f32)
    up_part = swap_plane(
        lax.psum_scatter(
            contract_first(feed_all, grad_lifted).astype(bf16),
            "z",
            scatter_dimension=0,
            tiled=True,
        )
    )
    grad_up_weight = (
        up_part.reshape(GROUP, weight_rows, planes, unit_rows)
        .transpose(1, 2, 0, 3)
        .reshape(weight_rows, FF)
        .astype(f32)
    )

    outputs = (middle + feed_gate[:, None] * feed_branch).astype(bf16)
    grad_feed_gate = jnp.sum(feed_branch * upstream, axis=1)
    feed_router_term, grad_feed_routed = route_back(
        grad_feed_gate, feed_probs, feed_chosen, feed_hidden, feed_router
    )
    grad_middle_norm, feed_gain_term, feed_bias_term = normalize_back(
        grad_feed_input + grad_feed_routed, feed_normed, feed_scale, feed_gain
    )
    grad_middle = upstream + grad_middle_norm
    grad_mixer_gate = jnp.sum(mixer_branch * grad_middle, axis=1)
    grad_mixer_branch = (mixer_gate[:, None] * grad_middle).astype(bf16)
    grad_attended = contract_last(grad_mixer_branch, output_full).astype(bf16) * head_mask
    grad_output_weight = lax.psum_scatter(
        contract_first(mixed_input, grad_mixer_branch).astype(bf16),
        ALL,
        scatter_dimension=0,
        tiled=True,
    ).astype(f32)
    grad_projected = attend_back(
        place, starts, cos_table, sin_table, rotated, by_head(grad_attended), rows
    )
    grad_mixer_input = plane_scatter(
        pieces(contract_last(grad_projected, input_share).astype(bf16))
    )
    input_part = swap_plane(
        lax.psum_scatter(
            contract_first(mixer_all, grad_projected).astype(bf16),
            "z",
            scatter_dimension=0,
            tiled=True,
        )
    )
    grad_input_weight = (
        input_part.reshape(GROUP, weight_rows, 3, SHARE)
        .transpose(1, 2, 0, 3)
        .reshape(weight_rows, 3 * D)
        .astype(f32)
    )
    mixer_router_term, grad_mixer_routed = route_back(
        grad_mixer_gate, mixer_probs, mixer_chosen, mixer_hidden, mixer_router
    )
    grad_token_norm, mixer_gain_term, mixer_bias_term = normalize_back(
        grad_mixer_input + grad_mixer_routed, mixer_normed, mixer_scale, mixer_gain
    )
    grad_tokens = grad_middle + grad_token_norm

    counts = jnp.pad(jnp.concatenate([head_counts, width_counts]), (0, D - 2 * OPTIONS))
    feed_sums = sum_everywhere(
        jnp.concatenate(
            [feed_gain_term[None], feed_bias_term[None], feed_router_term, counts[None]], axis=0
        ),
        planes,
    )
    mixer_sums = sum_everywhere(
        jnp.concatenate(
            [mixer_gain_term[None], mixer_bias_term[None], mixer_router_term], axis=0
        ),
        planes,
    )
    return (
        outputs,
        grad_tokens,
        mixer_sums[0],
        mixer_sums[1],
        grad_input_weight,
        grad_output_weight,
        mixer_sums[2:6].T,
        feed_sums[0],
        feed_sums[1],
        grad_up_weight,
        grad_down_weight,
        feed_sums[2:6].T,
        feed_sums[6, : 2 * OPTIONS].reshape(2, OPTIONS),
    )


def solution(mesh):
    wide, narrow = mesh.shape["wide"], mesh.shape["narrow"]
    planes = wide // 2
    inner = Mesh(mesh.devices.reshape(planes, 2, narrow // 2, 2), ALL)
    rowwise = P(ALL, None)
    in_specs = (
        rowwise,
        P(("z", "x"), None),
        P(ALL),
        P(ALL),
        P(),
        P(),
        rowwise,
        rowwise,
        P(),
        P(),
        P(),
        rowwise,
        rowwise,
        P(),
        rowwise,
    )
    out_specs = (
        rowwise,
        rowwise,
        P(),
        P(),
        rowwise,
        rowwise,
        P(),
        P(),
        P(),
        rowwise,
        rowwise,
        P(),
        P(),
    )
    return jax.shard_map(
        functools.partial(local, planes),
        mesh=inner,
        in_specs=in_specs,
        out_specs=out_specs,
        check_vma=False,
    )
```

time: 3320 us -> 895 us (0.27)
  waiting for transfers between devices: 2790 us -> 450 us
  matrix products: 322 us -> 143 us
  blocking collectives: 0 us -> 79.4 us
  starting transfers between devices: 1.23 us -> 57.6 us
  other arithmetic: 82.9 us -> 34.8 us
  Pallas kernels: 0 us -> 34.3 us
    reduce_scatter x5 -> x4, waiting for transfers between devices: 2070 us -> 131 us  [the longest x1 131 us: local(): lax.psum_scatter(contract_first(mixed_input, grad_mixer_branch).astype(bf...]
    all_gather x6 -> x4, waiting for transfers between devices: 588 us -> 80.3 us  [the longest x1 66.4 us: local(): down_share = lax.all_gather(down_weight, 'z', axis=0, tiled=True)]
    ppermute x0 -> x66, waiting for transfers between devices: none -> 210 us  [the longest x62 179 us: flip(): return lax.ppermute(values, axis, [(0, 1), (1, 0)])]
    psum x1 -> x0, waiting for transfers between devices: 130 us -> none  [local(): lax.psum((mixer_gain_term, mixer_bias_term, mixer_router_term, feed_gain_...]
    dot_general x62 -> x6, matrix products: 166 us -> 47.7 us  [the longest x4 45 us: dot_plain(): return jnp.dot(left, right, preferred_element_type=f32)]
    all_to_all x0 -> x3, blocking collectives: none -> 52 us  [swap_plane(): return lax.all_to_all(values, PLANE, 0, 0, tiled=True)]
    concatenate x4 -> x15, other arithmetic: 50.5 us -> 2.47 us  [the longest x4 1.5 us: plane_gather(): jnp.concatenate([flip(from_y[:half], 'x'), flip(from_x[half:], 'y')], axi...]
    ppermute x0 -> x66, starting transfers between devices: none -> 43.9 us  [the longest x62 43.7 us: flip(): return lax.ppermute(values, axis, [(0, 1), (1, 0)])]
  transfers between devices with their start and end apart: 12 -> 77, of which waited for: 12 -> 41; matrix products, arithmetic and copies ran while one was open for 7% -> 24% of each run, Pallas kernels for 0% -> 4%
where the time goes in v1:
time: 895 us; the launch traced here: 890 us
  waiting for transfers between devices  450 us (50%)
  matrix products  143 us (16%)
  blocking collectives  79.4 us (9%)
  local copies, waits for them, and re-layouts  75.5 us (8%)
  starting transfers between devices  57.6 us (6%)
  other arithmetic  34.8 us (4%)
  Pallas kernels  34.3 us (4%)
  between operations  15.7 us (2%)
    ppermute x62, waiting for transfers between devices, flip(): return lax.ppermute(values, axis, [(0, 1), (1, 0)])  179 us
    reduce_scatter x1, waiting for transfers between devices, local(): lax.psum_scatter(contract_first(mixed_input, grad_mixer_branch).astype(bf...  131 us
    all_gather x1, waiting for transfers between devices, local(): down_share = lax.all_gather(down_weight, 'z', axis=0, tiled=True)  66.4 us
    all_to_all x3, blocking collectives, swap_plane(): return lax.all_to_all(values, PLANE, 0, 0, tiled=True)  52 us
    dot_general x4, matrix products, dot_plain(): return jnp.dot(left, right, preferred_element_type=f32)  45 us
    dot_general x4, matrix products, contract_first(): lax.dot_general(left, right, (((0,), (0,)), ((), ())), preferred_element_...  45 us
    unnamed x121, local copies, waits for them, and re-layouts  44.8 us
    ppermute x62, starting transfers between devices, flip(): return lax.ppermute(values, axis, [(0, 1), (1, 0)])  43.7 us
  transfers between devices with their start and end apart: 77, of which 41 were waited for; matrix products, arithmetic and copies ran while one was open for 24% of the time, Pallas kernels for 4%

profile of v1, /device:TPU:0, one launch (start us, length us, event | category | flops | bytes accessed | tf_op | source)
XLA Modules:
  0.0 890.1 jit_solution(9618525012931597404)
XLA Ops:
  9.9 16.8 %all_to_all.59 = bf16[8,64,768]{2,1,0:T(8,128)(2,1)} all-to-all(bf16[8,64,768]{2,1,0:T(8,128)(2,1)S(1)} %all_to_all.39), channel_id=1, replica_groups=mesh['z'=4,'x'=2,'y'=2,'c'=2] {'x','y','c'}, dimensions={0} | all-to-all | bytes 1572864 | tf_op jit(solution)/shard_map/all_to_all | solution.py:139
  29.0 17.8 %all_to_all.60 = bf16[8,64,1024]{2,1,0:T(8,128)(2,1)} all-to-all(bf16[8,64,1024]{2,1,0:T(8,128)(2,1)S(1)} %all_to_all.44), channel_id=1, replica_groups=mesh['z'=4,'x'=2,'y'=2,'c'=2] {'x','y','c'}, dimensions={0} | all-to-all | bytes 2097152 | tf_op jit(solution)/shard_map/all_to_all | solution.py:139
  51.6 27.4 %all-gather.1 = s32[8,1,1280]{2,1,0:T(1,128)S(1)} all-gather(s32[1,1,1280]{2,1,0:T(1,128)S(1)} %reshape.237), channel_id=2, replica_groups=mesh['z'=4,'x'=2,'y'=2,'c'=2] {'x','y','c'}, dimensions={0}, use_global_device_ids=true | all-gather | bytes 46080 | tf_op jit(solution)/shard_map/all_gather | solution.py:329
  93.0 5.2 collective-permute-done.6
  98.2 3.1 collective-permute-done.5
  112.0 11.6 %fusion.120.proj_ref = f32[2048,768]{1,0:T(8,128)} fusion(bf16[2048,2048]{1,0:T(8,128)(2,1)} %constant_dynamic-update-slice_fusion, bf16[2048,768]{1,0:T(8,128)(2,1)} %all-gather.7.cloned.1.call-done), kind=kOutput, calls=%fused_computation.255 | convolution fusion | flops 6442450944 | bytes 17825792 | tf_op jit(solution)/shard_map/dot_general | solution.py:77
  123.7 13.8 %shard_map.246 = (bf16[2048,768]{1,0:T(8,128)(2,1)}, bf16[2048,256]{1,0:T(8,128)(2,1)}) custom-call(s32[2]{0:T(128)S(1)} %pad_add_fusion.2.place_ref, s32[2,1024,1]{2,1,0:T(8,128)S(1)} %copy.56.start_ref, f32[1024,128]{1,0:T(8,128)S(1)} %get-tuple-element.87.cos_ref, f32[1024,128]{1,0:T(8,128)S(1)} %get-tuple-element.88.sin_ref, f32[2048,768]{1,0:T(8,128)} %fusion.120.proj_ref), custom_call_target="tpu_custom_call" | custom-call | flops 2147483648 | bytes 16777216 | tf_op jit(solution)/shard_map/pallas_call | solution.py:247
  137.4 4.4 all-to-all-start.1
  145.2 22.7 %all-to-all-done.1 = bf16[8,256,256]{2,1,0:T(8,128)(2,1)} async-done(((bf16[8,256,256]{2,1,0:T(8,128)(2,1)}), bf16[8,256,256]{2,1,0:T(8,128)(2,1)}, u32[]{:S(2)}, u32[]{:S(2)}) %all-to-all-start.1) | async-done | bytes 1048608 | tf_op jit(solution)/shard_map/all_to_all | solution.py:139
  170.2 10.9 %all-gather.9.cloned.1.call-done = bf16[2048,2048]{1,0:T(8,128)(2,1)} async-done(((bf16[64,2048]{1,0:T(8,128)(2,1)}), bf16[2048,2048]{1,0:T(8,128)(2,1)}) %all-gather.9.cloned.1.call-update) | async-done | bytes 8388624 | tf_op jit(solution)/shard_map/all_gather | solution.py:347
  181.1 6.2 fusion.102
  194.9 22.3 %collective-permute-done.9 = bf16[256,2048]{1,0:T(8,128)(2,1)} collective-permute-done((bf16[256,2048]{1,0:T(8,128)(2,1)}, bf16[256,2048]{1,0:T(8,128)(2,1)}, u32[]{:S(2)}, u32[]{:S(2)}) %collective-permute-start.9) | collective-permute-done | bytes 1048608 | tf_op jit(solution)/shard_map/ppermute | solution.py:89
  226.6 23.4 %collective-permute-done.14 = bf16[128,2048]{1,0:T(8,128)(2,1)S(1)} collective-permute-done((bf16[128,2048]{1,0:T(8,128)(2,1)S(1)}, bf16[128,2048]{1,0:T(8,128)(2,1)S(1)}, u32[]{:S(2)}, u32[]{:S(2)}) %collective-permute-start.14) | collective-permute-done | bytes 524320 | tf_op jit(solution)/shard_map/ppermute | solution.py:89
  259.0 3.0 all-gather.11.cloned.1.call-done
  262.0 14.4 %fusion.121 = f32[2048,1024]{1,0:T(8,128)} fusion(bf16[2048,2048]{1,0:T(8,128)(2,1)} %constant_dynamic-update-slice_fusion.9, bf16[2048,1024]{1,0:T(8,128)(2,1)} %all-gather.11.cloned.1.call-done), kind=kOutput, calls=%fused_computation.256 | convolution fusion | flops 8589934592 | bytes 20971520 | tf_op jit(solution)/shard_map/dot_general | solution.py:77
  276.4 66.4 %all-gather.13.cloned.1.call-done = bf16[1024,2048]{1,0:T(8,128)(2,1)} async-done(((bf16[256,2048]{1,0:T(8,128)(2,1)}), bf16[1024,2048]{1,0:T(8,128)(2,1)}) %all-gather.13.cloned.1.call-update) | async-done | bytes 4194320 | tf_op jit(solution)/shard_map/all_gather | solution.py:354
  342.8 12.8 %convolution_convert_fusion.3 = bf16[2048,2048]{1,0:T(8,128)(2,1)S(1)} fusion(bf16[1024,2048]{1,0:T(8,128)(2,1)} %all-gather.13.cloned.1.call-done, f32[2048,1024]{1,0:T(8,128)} %fusion.121, s32[1024]{0:T(1024)S(1)} %fusion.62, s32[2048]{0:T(1024)S(1)} %bitcast.121), kind=kOutput, calls=%fused_computation.12 | convolution fusion | flops 8604614656 | bytes 20983808 | tf_op jit(solution)/shard_map/dot_general | solution.py:77
  356.8 3.1 constant_dynamic-update-slice_fusion.26
  371.6 4.7 collective-permute-done.37
  378.6 8.1 collective-permute-done.22
  388.4 11.3 %collective-permute-done.19 = bf16[128,2048]{1,0:T(8,128)(2,1)S(1)} collective-permute-done((bf16[128,2048]{1,0:T(8,128)(2,1)S(1)}, bf16[128,2048]{1,0:T(8,128)(2,1)S(1)}, u32[]{:S(2)}, u32[]{:S(2)}) %collective-permute-start.19) | collective-permute-done | bytes 524320 | tf_op jit(solution)/shard_map/ppermute | solution.py:89
  409.5 13.6 %collective-permute-done.23 = bf16[256,2048]{1,0:T(8,128)(2,1)S(1)} collective-permute-done((bf16[256,2048]{1,0:T(8,128)(2,1)S(1)}, bf16[256,2048]{1,0:T(8,128)(2,1)S(1)}, u32[]{:S(2)}, u32[]{:S(2)}) %collective-permute-start.23) | collective-permute-done | bytes 1048608 | tf_op jit(solution)/shard_map/ppermute | solution.py:89
  437.0 15.5 %fusion.3 = bf16[2048,1024]{1,0:T(8,128)(2,1)S(1)} fusion(f32[2048,1024]{1,0:T(8,128)} %fusion.121, s32[1024]{0:T(1024)S(1)} %fusion.62, s32[2048]{0:T(1024)S(1)} %bitcast.122, bf16[1024,2048]{1,0:T(8,128)(2,1)} %all-gather.13.cloned.1.call-done, bf16[2048,2048]{1,0:T(8,128)(2,1)} %constant_dynamic-update-slice_fusion.18, f32[2048]{0:T(1024)S(1)} %bitcast.124), kind=kOutput, calls=%fused_computation.7 | convolution fusion | flops 8615100416 | bytes 25186304 | tf_op jit(solution)/shard_map/dot_general | solution.py:81
  452.5 9.8 %convolution_convert_fusion.2 = bf16[2048,2048]{1,0:T(8,128)(2,1)S(1)} fusion(bf16[2048,1024]{1,0:T(8,128)(2,1)S(1)} %fusion.3, bf16[2048,1024]{1,0:T(8,128)(2,1)S(1)} %copy-done.37), kind=kOutput, calls=%fused_computation.11 | convolution fusion | flops 8594128896 | bytes 16777216 | tf_op jit(solution)/shard_map/dot_general | solution.py:81
  469.4 3.2 convert_add_fusion.5
  474.2 10.6 %convolution_convert_fusion.5 = bf16[2048,1024]{1,0:T(8,128)(2,1)} fusion(bf16[2048,2048]{1,0:T(8,128)(2,1)S(1)} %bitcast.107, bf16[2048,1024]{1,0:T(8,128)(2,1)S(1)} %fusion.3), kind=kOutput, calls=%fused_computation.14 | convolution fusion | flops 8592031744 | bytes 16777216 | tf_op jit(solution)/shard_map/dot_general | solution.py:85
  491.8 10.9 %collective-permute-done.43 = bf16[128,2048]{1,0:T(8,128)(2,1)S(1)} collective-permute-done((bf16[128,2048]{1,0:T(8,128)(2,1)}, bf16[128,2048]{1,0:T(8,128)(2,1)S(1)}, u32[]{:S(2)}, u32[]{:S(2)}) %collective-permute-start.43) | collective-permute-done | bytes 524320 | tf_op jit(solution)/shard_map/ppermute | solution.py:89
  504.5 20.3 %collective-permute-done.47 = bf16[256,2048]{1,0:T(8,128)(2,1)S(1)} collective-permute-done((bf16[256,2048]{1,0:T(8,128)(2,1)S(1)}, bf16[256,2048]{1,0:T(8,128)(2,1)S(1)}, u32[]{:S(2)}, u32[]{:S(2)}) %collective-permute-start.47) | collective-permute-done | bytes 1048608 | tf_op jit(solution)/shard_map/ppermute | solution.py:89
  527.4 4.2 multiply_reduce_fusion
  531.7 4.2 multiply_reduce_fusion.1
  538.4 17.3 %all_to_all.61 = bf16[8,256,256]{2,1,0:T(8,128)(2,1)S(1)} all-to-all(bf16[8,256,256]{2,1,0:T(8,128)(2,1)S(1)} %bitcast.93), channel_id=1, replica_groups=mesh['z'=4,'x'=2,'y'=2,'c'=2] {'x','y','c'}, dimensions={0} | all-to-all | bytes 2097152 | tf_op jit(solution)/shard_map/all_to_all | solution.py:139
  555.7 20.6 %shard_map.247 = bf16[2048,768]{1,0:T(8,128)(2,1)} custom-call(s32[2]{0:T(128)S(1)} %pad_add_fusion.2.place_ref, s32[2,1024,1]{2,1,0:T(8,128)S(1)} %copy.56.start_ref, f32[1024,128]{1,0:T(8,128)S(1)} %get-tuple-element.87.cos_ref, f32[1024,128]{1,0:T(8,128)S(1)} %get-tuple-element.88.sin_ref, bf16[2048,768]{1,0:T(8,128)(2,1)} %get-tuple-element.16.rot_ref, ...), custom_call_target="tpu_custom_call" | custom-call | flops 5368709120 | bytes 16777216 | tf_op jit(solution)/shard_map/pallas_call | solution.py:277
  576.3 10.1 %convolution_convert_fusion.6 = bf16[2048,768]{1,0:T(8,128)(2,1)} fusion(bf16[2048,2048]{1,0:T(8,128)(2,1)S(1)} %bitcast.105, bf16[2048,768]{1,0:T(8,128)(2,1)} %shard_map.247), kind=kOutput, calls=%fused_computation.15 | convolution fusion | flops 6444023808 | bytes 14680064 | tf_op jit(solution)/shard_map/dot_general | solution.py:85
  586.7 17.2 %convolution_convert_fusion.4 = bf16[1024,2048]{1,0:T(8,128)(2,1)} fusion(bf16[2048,2048]{1,0:T(8,128)(2,1)} %constant_dynamic-update-slice_fusion.18, f32[2048]{0:T(1024)S(1)} %bitcast.125, f32[2048,1024]{1,0:T(8,128)} %fusion.121, s32[1024]{0:T(1024)S(1)} %fusion.62, s32[2048]{0:T(1024)S(1)} %bitcast.123), kind=kOutput, calls=%fused_computation.13 | convolution fusion | flops 8615100416 | bytes 20992000 | tf_op jit(solution)/shard_map/dot_general | solution.py:85
  605.5 7.1 convolution_convert_fusion
  612.6 9.8 %convolution_convert_fusion.1 = bf16[2048,2048]{1,0:T(8,128)(2,1)S(1)} fusion(bf16[2048,768]{1,0:T(8,128)(2,1)} %shard_map.247, bf16[2048,768]{1,0:T(8,128)(2,1)} %all-gather.7.cloned.1.call-done), kind=kOutput, calls=%fused_computation.10 | convolution fusion | flops 6446645248 | bytes 14680064 | tf_op jit(solution)/shard_map/dot_general | solution.py:81
  633.1 11.0 %collective-permute-done.54 = bf16[128,2048]{1,0:T(8,128)(2,1)S(1)} collective-permute-done((bf16[128,2048]{1,0:T(8,128)(2,1)S(1)}, bf16[128,2048]{1,0:T(8,128)(2,1)S(1)}, u32[]{:S(2)}, u32[]{:S(2)}) %collective-permute-start.54) | collective-permute-done | bytes 524320 | tf_op jit(solution)/shard_map/ppermute | solution.py:89
  649.0 21.3 %collective-permute-done.62 = f32[7,2048]{1,0:T(8,128)S(1)} collective-permute-done((f32[7,2048]{1,0:T(8,128)S(1)}, f32[7,2048]{1,0:T(8,128)S(1)}, u32[]{:S(2)}, u32[]{:S(2)}) %collective-permute-start.62) | collective-permute-done | bytes 57376 | tf_op jit(solution)/shard_map/ppermute | solution.py:89
  674.7 6.1 collective-permute-done.64
  682.4 8.8 collective-permute-done.65
  691.9 4.4 fusion.20
  703.3 4.3 all-to-all-start.5
  707.7 9.0 %collective-permute-done.59 = f32[6,2048]{1,0:T(8,128)S(1)} collective-permute-done((f32[6,2048]{1,0:T(8,128)S(1)}, f32[6,2048]{1,0:T(8,128)S(1)}, u32[]{:S(2)}, u32[]{:S(2)}) %collective-permute-start.59) | collective-permute-done | bytes 49184 | tf_op jit(solution)/shard_map/ppermute | solution.py:133
  716.8 3.7 fusion.19
  720.5 7.2 collective-permute-done.60
  727.7 3.9 all-to-all-start.4
  741.4 5.9 all-to-all-done.4
  750.7 130.7 %reduce-scatter.7.cloned.1.call-done = bf16[64,2048]{1,0:T(8,128)(2,1)} async-done(((bf16[2048,2048]{1,0:T(8,128)(2,1)}), bf16[64,2048]{1,0:T(8,128)(2,1)}) %reduce-scatter.7.cloned.1.call-update) | async-done | bytes 262160 | tf_op jit(solution)/shard_map/reduce_scatter | solution.py:437
  (379 shorter events, 174.6 us)
Async XLA Ops:
  7.2 104.8 %all-gather.7.cloned.1.call-start = ((), (), s32[]{:S(2)}) async-start(), calls=%async_computation.10 | async-start | bytes 3932160 | tf_op jit(solution)/shard_map/all_gather | solution.py:346
  26.8 154.3 %all-gather.9.cloned.1.call-start = ((), (), s32[]{:S(2)}) async-start(), calls=%async_computation.11 | async-start | bytes 8650752 | tf_op jit(solution)/shard_map/all_gather | solution.py:347
  27.5 234.5 %all-gather.11.cloned.1.call-start = ((), (), s32[]{:S(2)}) async-start(), calls=%async_computation.12 | async-start | bytes 5242880 | tf_op jit(solution)/shard_map/all_gather | solution.py:353
  46.9 295.9 %all-gather.13.cloned.1.call-start = ((), (), s32[]{:S(2)}) async-start(), calls=%async_computation.13 | async-start | bytes 5242880 | tf_op jit(solution)/shard_map/all_gather | solution.py:354
  49.5 33.4 %collective-permute-start.3 = (bf16[256,2048]{1,0:T(8,128)(2,1)}, bf16[256,2048]{1,0:T(8,128)(2,1)S(1)}, u32[]{:S(2)}, u32[]{:S(2)}) collective-permute-start(bf16[256,2048]{1,0:T(8,128)(2,1)} %get-tuple-element.40), channel_id=1, source_target_pairs={{0,4},{4,0},{1,5},{5,1},{2,6},{6,2},{3,7},{7,3},{8,12},{12,8},{9,1... | collective-permute-start | bytes 3145736 | tf_op jit(solution)/shard_map/ppermute | solution.py:89
  50.8 30.6 %collective-permute-start.1 = (bf16[256,2048]{1,0:T(8,128)(2,1)}, bf16[256,2048]{1,0:T(8,128)(2,1)}, u32[]{:S(2)}, u32[]{:S(2)}) collective-permute-start(bf16[256,2048]{1,0:T(8,128)(2,1)} %get-tuple-element.40), channel_id=1, source_target_pairs={{0,2},{2,0},{1,3},{3,1},{4,6},{6,4},{5,7},{7,5},{8,10},{10,8},{9,1... | collective-permute-start | bytes 3145736 | tf_op jit(solution)/shard_map/ppermute | solution.py:89
  51.6 36.8 %collective-permute-start = (bf16[256,2048]{1,0:T(8,128)(2,1)}, bf16[256,2048]{1,0:T(8,128)(2,1)}, u32[]{:S(2)}, u32[]{:S(2)}) collective-permute-start(bf16[256,2048]{1,0:T(8,128)(2,1)} %get-tuple-element.40), channel_id=1, source_target_pairs={{0,1},{1,0},{2,3},{3,2},{4,5},{5,4},{6,7},{7,6},{8,9},{9,8},{10,11... | collective-permute-start | bytes 3145736 | tf_op jit(solution)/shard_map/ppermute | solution.py:89
  81.4 21.3 %collective-permute-start.2 = (bf16[256,2048]{1,0:T(8,128)(2,1)}, bf16[256,2048]{1,0:T(8,128)(2,1)}, u32[]{:S(2)}, u32[]{:S(2)}) collective-permute-start(bf16[256,2048]{1,0:T(8,128)(2,1)} %collective-permute-done.1), channel_id=1, source_target_pairs={{0,1},{1,0},{2,3},{3,2},{4,5},{5,4},{6,7},{7,6},{8,9},{9,8},{10,11... | collective-permute-start | bytes 3145736 | tf_op jit(solution)/shard_map/ppermute | solution.py:89
  83.9 14.3 %collective-permute-start.6 = (bf16[128,2048]{1,0:T(8,128)(2,1)}, bf16[128,2048]{1,0:T(8,128)(2,1)}, u32[]{:S(2)}, u32[]{:S(2)}) collective-permute-start(bf16[128,2048]{1,0:T(8,128)(2,1)} %slice.251), channel_id=1, source_target_pairs={{0,2},{2,0},{1,3},{3,1},{4,6},{6,4},{5,7},{7,5},{8,10},{10,8},{9,1... | collective-permute-start | bytes 1572872 | tf_op jit(solution)/shard_map/ppermute | solution.py:89
  87.2 14.0 %collective-permute-start.5 = (bf16[128,2048]{1,0:T(8,128)(2,1)}, bf16[128,2048]{1,0:T(8,128)(2,1)}, u32[]{:S(2)}, u32[]{:S(2)}) collective-permute-start(bf16[128,2048]{1,0:T(8,128)(2,1)} %slice.250), channel_id=1, source_target_pairs={{0,4},{4,0},{1,5},{5,1},{2,6},{6,2},{3,7},{7,3},{8,12},{12,8},{9,1... | collective-permute-start | bytes 1572872 | tf_op jit(solution)/shard_map/ppermute | solution.py:89
  88.3 17.8 %collective-permute-start.4 = (bf16[256,2048]{1,0:T(8,128)(2,1)}, bf16[256,2048]{1,0:T(8,128)(2,1)S(1)}, u32[]{:S(2)}, u32[]{:S(2)}) collective-permute-start(bf16[256,2048]{1,0:T(8,128)(2,1)} %copy-done.19), channel_id=1, source_target_pairs={{0,1},{1,0},{2,3},{3,2},{4,5},{5,4},{6,7},{7,6},{8,9},{9,8},{10,11... | collective-permute-start | bytes 3145736 | tf_op jit(solution)/shard_map/ppermute | solution.py:89
  137.4 30.5 %all-to-all-start.1 = ((bf16[8,256,256]{2,1,0:T(8,128)(2,1)}), bf16[8,256,256]{2,1,0:T(8,128)(2,1)}, u32[]{:S(2)}, u32[]{:S(2)}) async-start(bf16[8,256,256]{2,1,0:T(8,128)(2,1)} %bitcast.6), calls=%async_computation.1 | async-start | bytes 2097152 | tf_op jit(solution)/shard_map/all_to_all | solution.py:139
  141.9 561.4 %reduce-scatter.9.cloned.1.call-start = ((), (), s32[]{:S(2)}) async-start(), calls=%async_computation.16 | async-start | bytes 5242880 | tf_op jit(solution)/shard_map/reduce_scatter | solution.py:411
  190.8 26.3 %collective-permute-start.9 = (bf16[256,2048]{1,0:T(8,128)(2,1)}, bf16[256,2048]{1,0:T(8,128)(2,1)}, u32[]{:S(2)}, u32[]{:S(2)}) collective-permute-start(bf16[256,2048]{1,0:T(8,128)(2,1)} %get-tuple-element.35), channel_id=1, source_target_pairs={{0,2},{2,0},{1,3},{3,1},{4,6},{6,4},{5,7},{7,5},{8,10},{10,8},{9,1... | collective-permute-start | bytes 3145736 | tf_op jit(solution)/shard_map/ppermute | solution.py:89
  192.3 25.3 %collective-permute-start.11 = (bf16[256,2048]{1,0:T(8,128)(2,1)}, bf16[256,2048]{1,0:T(8,128)(2,1)}, u32[]{:S(2)}, u32[]{:S(2)}) collective-permute-start(bf16[256,2048]{1,0:T(8,128)(2,1)} %get-tuple-element.35), channel_id=1, source_target_pairs={{0,4},{4,0},{1,5},{5,1},{2,6},{6,2},{3,7},{7,3},{8,12},{12,8},{9,1... | collective-permute-start | bytes 3145736 | tf_op jit(solution)/shard_map/ppermute | solution.py:89
  192.8 29.1 %collective-permute-start.8 = (bf16[256,2048]{1,0:T(8,128)(2,1)}, bf16[256,2048]{1,0:T(8,128)(2,1)}, u32[]{:S(2)}, u32[]{:S(2)}) collective-permute-start(bf16[256,2048]{1,0:T(8,128)(2,1)} %get-tuple-element.35), channel_id=1, source_target_pairs={{0,1},{1,0},{2,3},{3,2},{4,5},{5,4},{6,7},{7,6},{8,9},{9,8},{10,11... | collective-permute-start | bytes 3145736 | tf_op jit(solution)/shard_map/ppermute | solution.py:89
  192.9 167.0 %collective-permute-start.33 = (bf16[256,2048]{1,0:T(8,128)(2,1)}, bf16[256,2048]{1,0:T(8,128)(2,1)}, u32[]{:S(2)}, u32[]{:S(2)}) collective-permute-start(bf16[256,2048]{1,0:T(8,128)(2,1)} %param.29), channel_id=1, source_target_pairs={{0,2},{2,0},{1,3},{3,1},{4,6},{6,4},{5,7},{7,5},{8,10},{10,8},{9,1... | collective-permute-start | bytes 3145736 | tf_op jit(solution)/shard_map/ppermute | solution.py:89
  217.2 34.5 %collective-permute-start.10 = (bf16[256,2048]{1,0:T(8,128)(2,1)}, bf16[256,2048]{1,0:T(8,128)(2,1)S(1)}, u32[]{:S(2)}, u32[]{:S(2)}) collective-permute-start(bf16[256,2048]{1,0:T(8,128)(2,1)} %collective-permute-done.9), channel_id=1, source_target_pairs={{0,1},{1,0},{2,3},{3,2},{4,5},{5,4},{6,7},{7,6},{8,9},{9,8},{10,11... | collective-permute-start | bytes 3145736 | tf_op jit(solution)/shard_map/ppermute | solution.py:89
  218.7 31.3 %collective-permute-start.14 = (bf16[128,2048]{1,0:T(8,128)(2,1)S(1)}, bf16[128,2048]{1,0:T(8,128)(2,1)S(1)}, u32[]{:S(2)}, u32[]{:S(2)}) collective-permute-start(bf16[128,2048]{1,0:T(8,128)(2,1)S(1)} %slice.254), channel_id=1, source_target_pairs={{0,2},{2,0},{1,3},{3,1},{4,6},{6,4},{5,7},{7,5},{8,10},{10,8},{9,1... | collective-permute-start | bytes 1572872 | tf_op jit(solution)/shard_map/ppermute | solution.py:89
  220.9 30.6 %collective-permute-start.13 = (bf16[128,2048]{1,0:T(8,128)(2,1)S(1)}, bf16[128,2048]{1,0:T(8,128)(2,1)S(1)}, u32[]{:S(2)}, u32[]{:S(2)}) collective-permute-start(bf16[128,2048]{1,0:T(8,128)(2,1)S(1)} %slice.253), channel_id=1, source_target_pairs={{0,4},{4,0},{1,5},{5,1},{2,6},{6,2},{3,7},{7,3},{8,12},{12,8},{9,1... | collective-permute-start | bytes 1572872 | tf_op jit(solution)/shard_map/ppermute | solution.py:89
  222.0 33.2 %collective-permute-start.12 = (bf16[256,2048]{1,0:T(8,128)(2,1)}, bf16[256,2048]{1,0:T(8,128)(2,1)S(1)}, u32[]{:S(2)}, u32[]{:S(2)}) collective-permute-start(bf16[256,2048]{1,0:T(8,128)(2,1)} %collective-permute-done.11), channel_id=1, source_target_pairs={{0,1},{1,0},{2,3},{3,2},{4,5},{5,4},{6,7},{7,6},{8,9},{9,8},{10,11... | collective-permute-start | bytes 3145736 | tf_op jit(solution)/shard_map/ppermute | solution.py:89
  250.1 111.4 %collective-permute-start.35 = (bf16[256,2048]{1,0:T(8,128)(2,1)}, bf16[256,2048]{1,0:T(8,128)(2,1)}, u32[]{:S(2)}, u32[]{:S(2)}) collective-permute-start(bf16[256,2048]{1,0:T(8,128)(2,1)} %param.29), channel_id=1, source_target_pairs={{0,4},{4,0},{1,5},{5,1},{2,6},{6,2},{3,7},{7,3},{8,12},{12,8},{9,1... | collective-permute-start | bytes 3145736 | tf_op jit(solution)/shard_map/ppermute | solution.py:89
  361.4 14.8 %collective-permute-start.37 = (bf16[128,2048]{1,0:T(8,128)(2,1)S(1)}, bf16[128,2048]{1,0:T(8,128)(2,1)S(1)}, u32[]{:S(2)}, u32[]{:S(2)}) collective-permute-start(bf16[128,2048]{1,0:T(8,128)(2,1)S(1)} %slice.269), channel_id=1, source_target_pairs={{0,4},{4,0},{1,5},{5,1},{2,6},{6,2},{3,7},{7,3},{8,12},{12,8},{9,1... | collective-permute-start | bytes 1572872 | tf_op jit(solution)/shard_map/ppermute | solution.py:89
  364.1 13.7 %collective-permute-start.38 = (bf16[128,2048]{1,0:T(8,128)(2,1)S(1)}, bf16[128,2048]{1,0:T(8,128)(2,1)S(1)}, u32[]{:S(2)}, u32[]{:S(2)}) collective-permute-start(bf16[128,2048]{1,0:T(8,128)(2,1)S(1)} %slice.270), channel_id=1, source_target_pairs={{0,2},{2,0},{1,3},{3,1},{4,6},{6,4},{5,7},{7,5},{8,10},{10,8},{9,1... | collective-permute-start | bytes 1572872 | tf_op jit(solution)/shard_map/ppermute | solution.py:89
  365.6 35.8 %collective-permute-start.34 = (bf16[256,2048]{1,0:T(8,128)(2,1)}, bf16[256,2048]{1,0:T(8,128)(2,1)S(1)}, u32[]{:S(2)}, u32[]{:S(2)}) collective-permute-start(bf16[256,2048]{1,0:T(8,128)(2,1)} %collective-permute-done.33), channel_id=1, source_target_pairs={{0,1},{1,0},{2,3},{3,2},{4,5},{5,4},{6,7},{7,6},{8,9},{9,8},{10,11... | collective-permute-start | bytes 3145736 | tf_op jit(solution)/shard_map/ppermute | solution.py:89
  365.7 40.9 %collective-permute-start.36 = (bf16[256,2048]{1,0:T(8,128)(2,1)}, bf16[256,2048]{1,0:T(8,128)(2,1)S(1)}, u32[]{:S(2)}, u32[]{:S(2)}) collective-permute-start(bf16[256,2048]{1,0:T(8,128)(2,1)} %collective-permute-done.35), channel_id=1, source_target_pairs={{0,1},{1,0},{2,3},{3,2},{4,5},{5,4},{6,7},{7,6},{8,9},{9,8},{10,11... | collective-permute-start | bytes 3145736 | tf_op jit(solution)/shard_map/ppermute | solution.py:89
  367.5 19.1 %collective-permute-start.22 = (bf16[128,2048]{1,0:T(8,128)(2,1)S(1)}, bf16[128,2048]{1,0:T(8,128)(2,1)S(1)}, u32[]{:S(2)}, u32[]{:S(2)}) collective-permute-start(bf16[128,2048]{1,0:T(8,128)(2,1)S(1)} %get-tuple-element.68), channel_id=1, source_target_pairs={{0,4},{4,0},{1,5},{5,1},{2,6},{6,2},{3,7},{7,3},{8,12},{12,8},{9,1... | collective-permute-start | bytes 1572872 | tf_op jit(solution)/shard_map/ppermute | solution.py:89
  377.9 58.0 %collective-permute-start.39 = (bf16[256,2048]{1,0:T(8,128)(2,1)S(1)}, bf16[256,2048]{1,0:T(8,128)(2,1)S(1)}, u32[]{:S(2)}, u32[]{:S(2)}) collective-permute-start(bf16[256,2048]{1,0:T(8,128)(2,1)S(1)} %pad_maximum_fusion.4), channel_id=1, source_target_pairs={{0,1},{1,0},{2,3},{3,2},{4,5},{5,4},{6,7},{7,6},{8,9},{9,8},{10,11... | collective-permute-start | bytes 3145736 | tf_op jit(solution)/shard_map/ppermute | solution.py:89
  377.9 31.5 %collective-permute-start.16 = (bf16[256,2048]{1,0:T(8,128)(2,1)S(1)}, bf16[256,2048]{1,0:T(8,128)(2,1)S(1)}, u32[]{:S(2)}, u32[]{:S(2)}) collective-permute-start(bf16[256,2048]{1,0:T(8,128)(2,1)S(1)} %get-tuple-element.55), channel_id=1, source_target_pairs={{0,1},{1,0},{2,3},{3,2},{4,5},{5,4},{6,7},{7,6},{8,9},{9,8},{10,11... | collective-permute-start | bytes 3145736 | tf_op jit(solution)/shard_map/ppermute | solution.py:89
  399.7 23.4 %collective-permute-start.23 = (bf16[256,2048]{1,0:T(8,128)(2,1)S(1)}, bf16[256,2048]{1,0:T(8,128)(2,1)S(1)}, u32[]{:S(2)}, u32[]{:S(2)}) collective-permute-start(bf16[256,2048]{1,0:T(8,128)(2,1)S(1)} %pad_maximum_fusion.3), channel_id=1, source_target_pairs={{0,2},{2,0},{1,3},{3,1},{4,6},{6,4},{5,7},{7,5},{8,10},{10,8},{9,1... | collective-permute-start | bytes 3145736 | tf_op jit(solution)/shard_map/ppermute | solution.py:89
  401.5 23.1 %collective-permute-start.20 = (bf16[256,2048]{1,0:T(8,128)(2,1)S(1)}, bf16[256,2048]{1,0:T(8,128)(2,1)S(1)}, u32[]{:S(2)}, u32[]{:S(2)}) collective-permute-start(bf16[256,2048]{1,0:T(8,128)(2,1)S(1)} %pad_maximum_fusion.2), channel_id=1, source_target_pairs={{0,4},{4,0},{1,5},{5,1},{2,6},{6,2},{3,7},{7,3},{8,12},{12,8},{9,1... | collective-permute-start | bytes 3145736 | tf_op jit(solution)/shard_map/ppermute | solution.py:89
  473.6 15.7 %collective-permute-start.46 = (bf16[128,2048]{1,0:T(8,128)(2,1)}, bf16[128,2048]{1,0:T(8,128)(2,1)}, u32[]{:S(2)}, u32[]{:S(2)}) collective-permute-start(bf16[128,2048]{1,0:T(8,128)(2,1)} %get-tuple-element.66), channel_id=1, source_target_pairs={{0,4},{4,0},{1,5},{5,1},{2,6},{6,2},{3,7},{7,3},{8,12},{12,8},{9,1... | collective-permute-start | bytes 1572872 | tf_op jit(solution)/shard_map/ppermute | solution.py:89
  484.8 242.9 %reduce-scatter.5.cloned.1.call-start = ((), (), s32[]{:S(2)}) async-start(), calls=%async_computation.14 | async-start | bytes 3932160 | tf_op jit(solution)/shard_map/reduce_scatter | solution.py:450
  484.9 19.6 %collective-permute-start.40 = (bf16[256,2048]{1,0:T(8,128)(2,1)}, bf16[256,2048]{1,0:T(8,128)(2,1)S(1)}, u32[]{:S(2)}, u32[]{:S(2)}) collective-permute-start(bf16[256,2048]{1,0:T(8,128)(2,1)} %get-tuple-element.48), channel_id=1, source_target_pairs={{0,1},{1,0},{2,3},{3,2},{4,5},{5,4},{6,7},{7,6},{8,9},{9,8},{10,11... | collective-permute-start | bytes 3145736 | tf_op jit(solution)/shard_map/ppermute | solution.py:89
  487.7 15.0 %collective-permute-start.43 = (bf16[128,2048]{1,0:T(8,128)(2,1)}, bf16[128,2048]{1,0:T(8,128)(2,1)S(1)}, u32[]{:S(2)}, u32[]{:S(2)}) collective-permute-start(bf16[128,2048]{1,0:T(8,128)(2,1)} %get-tuple-element.65), channel_id=1, source_target_pairs={{0,2},{2,0},{1,3},{3,1},{4,6},{6,4},{5,7},{7,5},{8,10},{10,8},{9,1... | collective-permute-start | bytes 1572872 | tf_op jit(solution)/shard_map/ppermute | solution.py:89
  490.6 34.2 %collective-permute-start.47 = (bf16[256,2048]{1,0:T(8,128)(2,1)S(1)}, bf16[256,2048]{1,0:T(8,128)(2,1)S(1)}, u32[]{:S(2)}, u32[]{:S(2)}) collective-permute-start(bf16[256,2048]{1,0:T(8,128)(2,1)S(1)} %pad_maximum_fusion.6), channel_id=1, source_target_pairs={{0,2},{2,0},{1,3},{3,1},{4,6},{6,4},{5,7},{7,5},{8,10},{10,8},{9,1... | collective-permute-start | bytes 3145736 | tf_op jit(solution)/shard_map/ppermute | solution.py:89
  502.9 24.4 %collective-permute-start.44 = (bf16[256,2048]{1,0:T(8,128)(2,1)S(1)}, bf16[256,2048]{1,0:T(8,128)(2,1)S(1)}, u32[]{:S(2)}, u32[]{:S(2)}) collective-permute-start(bf16[256,2048]{1,0:T(8,128)(2,1)S(1)} %pad_maximum_fusion.5), channel_id=1, source_target_pairs={{0,4},{4,0},{1,5},{5,1},{2,6},{6,2},{3,7},{7,3},{8,12},{12,8},{9,1... | collective-permute-start | bytes 3145736 | tf_op jit(solution)/shard_map/ppermute | solution.py:89
  586.4 146.4 %reduce-scatter.11.cloned.1.call-start = ((), (), s32[]{:S(2)}) async-start(), calls=%async_computation.17 | async-start | bytes 5242880 | tf_op jit(solution)/shard_map/reduce_scatter | solution.py:404
  603.9 277.4 %reduce-scatter.7.cloned.1.call-start = ((), (), s32[]{:S(2)}) async-start(), calls=%async_computation.15 | async-start | bytes 8650752 | tf_op jit(solution)/shard_map/reduce_scatter | solution.py:437
  630.1 14.0 %collective-permute-start.54 = (bf16[128,2048]{1,0:T(8,128)(2,1)S(1)}, bf16[128,2048]{1,0:T(8,128)(2,1)S(1)}, u32[]{:S(2)}, u32[]{:S(2)}) collective-permute-start(bf16[128,2048]{1,0:T(8,128)(2,1)S(1)} %get-tuple-element.64), channel_id=1, source_target_pairs={{0,4},{4,0},{1,5},{5,1},{2,6},{6,2},{3,7},{7,3},{8,12},{12,8},{9,1... | collective-permute-start | bytes 1572872 | tf_op jit(solution)/shard_map/ppermute | solution.py:89
  631.6 15.7 %collective-permute-start.61 = (f32[7,2048]{1,0:T(8,128)S(1)}, f32[7,2048]{1,0:T(8,128)S(1)}, u32[]{:S(2)}, u32[]{:S(2)}) collective-permute-start(f32[7,2048]{1,0:T(8,128)S(1)} %pad_maximum_fusion.12), channel_id=1, source_target_pairs={{0,1},{1,0},{2,3},{3,2},{4,5},{5,4},{6,7},{7,6},{8,9},{9,8},{10,11... | collective-permute-start | bytes 172040 | tf_op jit(solution)/shard_map/ppermute | solution.py:89
  631.7 60.2 %collective-permute-start.48 = (bf16[256,2048]{1,0:T(8,128)(2,1)S(1)}, bf16[256,2048]{1,0:T(8,128)(2,1)S(1)}, u32[]{:S(2)}, u32[]{:S(2)}) collective-permute-start(bf16[256,2048]{1,0:T(8,128)(2,1)S(1)} %get-tuple-element.41), channel_id=1, source_target_pairs={{0,1},{1,0},{2,3},{3,2},{4,5},{5,4},{6,7},{7,6},{8,9},{9,8},{10,11... | collective-permute-start | bytes 3145736 | tf_op jit(solution)/shard_map/ppermute | solution.py:89
  632.4 14.0 %collective-permute-start.51 = (bf16[128,2048]{1,0:T(8,128)(2,1)S(1)}, bf16[128,2048]{1,0:T(8,128)(2,1)S(1)}, u32[]{:S(2)}, u32[]{:S(2)}) collective-permute-start(bf16[128,2048]{1,0:T(8,128)(2,1)S(1)} %get-tuple-element.63), channel_id=1, source_target_pairs={{0,2},{2,0},{1,3},{3,1},{4,6},{6,4},{5,7},{7,5},{8,10},{10,8},{9,1... | collective-permute-start | bytes 1572872 | tf_op jit(solution)/shard_map/ppermute | solution.py:89
  644.4 47.5 %collective-permute-start.55 = (bf16[256,2048]{1,0:T(8,128)(2,1)S(1)}, bf16[256,2048]{1,0:T(8,128)(2,1)S(1)}, u32[]{:S(2)}, u32[]{:S(2)}) collective-permute-start(bf16[256,2048]{1,0:T(8,128)(2,1)S(1)} %pad_maximum_fusion.8), channel_id=1, source_target_pairs={{0,2},{2,0},{1,3},{3,1},{4,6},{6,4},{5,7},{7,5},{8,10},{10,8},{9,1... | collective-permute-start | bytes 3145736 | tf_op jit(solution)/shard_map/ppermute | solution.py:89
  646.5 45.3 %collective-permute-start.52 = (bf16[256,2048]{1,0:T(8,128)(2,1)S(1)}, bf16[256,2048]{1,0:T(8,128)(2,1)S(1)}, u32[]{:S(2)}, u32[]{:S(2)}) collective-permute-start(bf16[256,2048]{1,0:T(8,128)(2,1)S(1)} %pad_maximum_fusion.7), channel_id=1, source_target_pairs={{0,4},{4,0},{1,5},{5,1},{2,6},{6,2},{3,7},{7,3},{8,12},{12,8},{9,1... | collective-permute-start | bytes 3145736 | tf_op jit(solution)/shard_map/ppermute | solution.py:89
  647.4 22.9 %collective-permute-start.62 = (f32[7,2048]{1,0:T(8,128)S(1)}, f32[7,2048]{1,0:T(8,128)S(1)}, u32[]{:S(2)}, u32[]{:S(2)}) collective-permute-start(f32[7,2048]{1,0:T(8,128)S(1)} %fusion.101), channel_id=1, source_target_pairs={{0,2},{2,0},{1,3},{3,1},{4,6},{6,4},{5,7},{7,5},{8,10},{10,8},{9,1... | collective-permute-start | bytes 172040 | tf_op jit(solution)/shard_map/ppermute | solution.py:89
  703.3 24.4 %all-to-all-start.5 = ((bf16[8,64,1024]{2,1,0:T(8,128)(2,1)}), bf16[8,64,1024]{2,1,0:T(8,128)(2,1)}, u32[]{:S(2)}, u32[]{:S(2)}) async-start(bf16[8,64,1024]{2,1,0:T(8,128)(2,1)} %bitcast.100), calls=%async_computation.8 | async-start | bytes 2097152 | tf_op jit(solution)/shard_map/all_to_all | solution.py:139
  727.7 19.5 %all-to-all-start.4 = ((bf16[8,64,768]{2,1,0:T(8,128)(2,1)}), bf16[8,64,768]{2,1,0:T(8,128)(2,1)S(1)}, u32[]{:S(2)}, u32[]{:S(2)}) async-start(bf16[8,64,768]{2,1,0:T(8,128)(2,1)} %bitcast.103), calls=%async_computation.5 | async-start | bytes 1572864 | tf_op jit(solution)/shard_map/all_to_all | solution.py:139
  (75 other events, 1320.8 us)
Sparse Core Ops, SparseCore 0:
  26.9 63.8 all-gather.6
  93.6 87.4 all-gather.8
  182.7 79.3 all-gather.10
  263.5 79.2 all-gather.12
  484.9 74.3 reduce-scatter.8
  586.5 57.9 reduce-scatter.4
  646.9 82.4 reduce-scatter.10
  731.7 149.6 reduce-scatter.6

commit v2 on v1

v2 whole, which is shorter than its diff:
```python
import functools

import jax
import jax.numpy as jnp
from jax import lax
from jax.experimental import pallas as pl
from jax.experimental.pallas import tpu as pltpu
from jax.sharding import Mesh, PartitionSpec as P

D = 2048
H = 16
HD = 128
FF = 8192
OPTIONS = 4
LONGEST = 512

PLANE = ("x", "y", "c")
ALL = ("z", "x", "y", "c")
GROUP = 8
SHARE = D // GROUP

highest = lax.Precision.HIGHEST
epsilon = 1e-05
masked_score = -1e30
f32 = jnp.float32
bf16 = jnp.bfloat16


def normalize(values, gain_vec, shift_vec):
    centre = values - jnp.mean(values, axis=1, keepdims=True)
    inv_scale = lax.rsqrt(jnp.mean(centre * centre, axis=1, keepdims=True) + epsilon)
    normed = centre * inv_scale
    return (normed * gain_vec + shift_vec, normed, inv_scale)


def normalize_back(grad_hidden, normed, inv_scale, gain_vec):
    grad_normed = grad_hidden * gain_vec
    inner = (
        grad_normed
        - jnp.mean(grad_normed, axis=1, keepdims=True)
        - normed * jnp.mean(grad_normed * normed, axis=1, keepdims=True)
    )
    return (inv_scale * inner, jnp.sum(grad_hidden * normed, axis=0), jnp.sum(grad_hidden, axis=0))


def route(hidden, router, picked):
    logits = jnp.dot(hidden, router, precision=highest)
    shifted = jnp.exp(logits - jnp.max(logits, axis=1, keepdims=True))
    prob_rows = shifted / jnp.sum(shifted, axis=1, keepdims=True)
    chosen = (jnp.arange(router.shape[1])[None, :] == picked[:, None]).astype(f32)
    return (router.shape[1] * jnp.sum(prob_rows * chosen, axis=1), prob_rows, chosen)


def route_back(grad_gate, prob_rows, chosen, hidden, router):
    grad_prob = router.shape[1] * grad_gate[:, None] * chosen
    grad_logits = prob_rows * (grad_prob - jnp.sum(grad_prob * prob_rows, axis=1, keepdims=True))
    grad_router = lax.dot_general(
        grad_logits, hidden, (((0,), (0,)), ((), ())), precision=highest
    )
    grad_hidden = jnp.dot(grad_logits, router.T, precision=highest)
    return (grad_router, grad_hidden)


def rope_tables(positions):
    half_width = HD // 2
    exponent = jnp.arange(half_width).astype(f32) * (-2.0 / HD)
    frequency = jnp.power(10000.0, exponent)
    angles = positions[:, None] * frequency[None, :]
    cos_half, sin_half = jnp.cos(angles), jnp.sin(angles)
    return (
        jnp.concatenate([cos_half, cos_half], axis=1),
        jnp.concatenate([-sin_half, sin_half], axis=1),
    )


def dot_plain(left, right):
    return jnp.dot(left, right, preferred_element_type=f32)


def contract_last(left, right):
    return lax.dot_general(left, right, (((1,), (1,)), ((), ())), preferred_element_type=f32)


def contract_first(left, right):
    return lax.dot_general(left, right, (((0,), (0,)), ((), ())), preferred_element_type=f32)


def flip(values, axis):
    return lax.ppermute(values, axis, [(0, 1), (1, 0)])


def gather_four(values):
    half = values.shape[0] // 2
    top, bottom = values[:half], values[half:]
    y_top, x_bottom = flip(top, "y"), flip(bottom, "x")
    y_bottom, x_top = flip(bottom, "y"), flip(top, "x")
    return [values, y_top, y_bottom, x_top, x_bottom, flip(y_top, "x"), flip(x_bottom, "y")]


def gather_eight(values):
    chunks = gather_four(values)
    return chunks + [flip(chunk, "c") for chunk in chunks]


def copies_in(pieces, whole, sem):
    copies, at = [], 0
    for i, piece in enumerate(pieces):
        count = piece.shape[0]
        copies.append(pltpu.make_async_copy(piece, whole.at[at : at + count, :], sem.at[i]))
        at += count
    return copies


def scatter_send(parts):
    half = parts[0].shape[0] // 2
    by_x, by_y = flip(parts[3][:half], "x"), flip(parts[3][half:], "y")
    x_top, y_bottom = flip(parts[2][:half], "x"), flip(parts[1][half:], "y")
    return by_x, by_y, x_top, y_bottom


def scatter_end(parts, sent):
    half = parts[0].shape[0] // 2
    by_x, by_y, x_top, y_bottom = sent
    y_top = flip((parts[1][:half].astype(f32) + by_x.astype(f32)).astype(bf16), "y")
    x_bottom = flip((parts[2][half:].astype(f32) + by_y.astype(f32)).astype(bf16), "x")
    own = parts[0].astype(f32)
    return jnp.concatenate(
        [
            own[:half] + x_top.astype(f32) + y_top.astype(f32),
            own[half:] + x_bottom.astype(f32) + y_bottom.astype(f32),
        ],
        axis=0,
    )


def scatter_four(parts):
    return scatter_end(parts, scatter_send(parts))


def add_cores(parts):
    other = [flip(part, "c") for part in parts[4:]]
    return [(a.astype(f32) + b.astype(f32)).astype(bf16) for a, b in zip(parts[:4], other)]


def send_four(values, d):
    return lax.ppermute(values, ("x", "y"), [(i, i ^ d) for i in range(4)])


def gather_small(values):
    return jnp.stack([values] + [send_four(values, d) for d in range(1, 4)])


def sum_small(values):
    return values[0] + sum(send_four(values[d], d) for d in range(1, 4))


def sum_everywhere(values, planes, before_last):
    for axis in ("c", "y", "x"):
        values = values + flip(values, axis)
    if planes & (planes - 1):
        return lax.psum(values, "z"), before_last
    step = 1
    while step < planes:
        if 2 * step == planes:
            values, before_last = lax.optimization_barrier((values, before_last))
        values = values + lax.ppermute(values, "z", [(i, i ^ step) for i in range(planes)])
        step *= 2
    return values, before_last


def after(values, *others):
    return lax.optimization_barrier((values, *others))[0]


def head_numbers():
    chip = lax.axis_index("x") * 2 + lax.axis_index("y")
    return [chip + 4 * (2 * lax.axis_index("c") + e) for e in range(2)]


def by_core(mine, other, axis):
    return jnp.where(
        lax.axis_index("c") == 0,
        jnp.concatenate([mine, other], axis=axis),
        jnp.concatenate([other, mine], axis=axis),
    )


def share_heads(blocks):
    weight_rows = blocks[0].shape[0]
    if len(blocks) == 1 or 2 * weight_rows != HD:
        full = lax.all_gather(blocks[0], ALL, axis=0, tiled=True)
        mine = [lax.dynamic_slice_in_dim(full, h * HD, HD, 0) for h in head_numbers()]
        mine = jnp.concatenate(mine, axis=0)
        return jnp.concatenate([mine, flip(mine, "c")], axis=0)
    halves = jnp.zeros((len(blocks), 1, weight_rows, D), bf16)
    for d, block in enumerate(blocks):
        at = lax.axis_index("z") ^ d
        halves = lax.dynamic_update_slice(halves, block[None, None], (at, 0, 0, 0))
    heads = by_core(halves, flip(halves, "c"), 1)
    core = lax.axis_index("c")
    return jnp.concatenate(
        [
            lax.dynamic_slice_in_dim(heads, 2 * core, 2, 0),
            lax.dynamic_slice_in_dim(heads, 2 - 2 * core, 2, 0),
        ],
        axis=0,
    ).reshape(2 * SHARE, D)


def sum_heads(part, planes, weight_rows):
    if 2 * weight_rows != HD:
        mine = part[:SHARE] + flip(part[SHARE:], "c")
        full = jnp.zeros((D, D), part.dtype)
        for e, h in enumerate(head_numbers()):
            full = lax.dynamic_update_slice(full, mine[e * HD : (e + 1) * HD], (h * HD, 0))
        return lax.psum_scatter(full, ALL, scatter_dimension=0, tiled=True)
    core = lax.axis_index("c")
    halves = part.reshape(4, 2, weight_rows, D)
    mine = lax.dynamic_slice_in_dim(halves, core, 1, 1)[:, 0]
    other = flip(lax.dynamic_slice_in_dim(halves, 1 - core, 1, 1)[:, 0], "c")
    first = (mine[:2].astype(f32) + other[2:].astype(f32)).astype(bf16)
    second = (mine[2:].astype(f32) + other[:2].astype(f32)).astype(bf16)
    return lax.psum_scatter(
        by_core(first, second, 0).reshape(planes * weight_rows, D),
        "z",
        scatter_dimension=0,
        tiled=True,
    )


def attention_columns():
    return [
        (part * D + (p // 2 + 4 * (2 * (p % 2) + e)) * HD, HD, p, (e * 3 + part) * HD)
        for p in range(GROUP)
        for part in range(3)
        for e in range(2)
    ]


def unit_columns(planes, unit_rows):
    return [
        ((k * GROUP + p) * unit_rows, unit_rows, p, k * unit_rows)
        for p in range(GROUP)
        for k in range(planes)
    ]


def deal_kernel(moves, whole_ref, dealt_ref):
    for first, width, p, at in moves:
        dealt_ref[p, :, at : at + width] = whole_ref[:, first : first + width]


def deal(whole, moves):
    rows, columns = whole.shape
    if any(width % 128 for _, width, _, _ in moves):
        parts = [[] for _ in range(GROUP)]
        for first, width, p, _ in moves:
            parts[p].append(whole[:, first : first + width])
        return jnp.concatenate([jnp.concatenate(part, axis=1) for part in parts], axis=0)
    dealt = pl.pallas_call(
        functools.partial(deal_kernel, moves),
        out_shape=jax.ShapeDtypeStruct((GROUP, rows, columns // GROUP), whole.dtype),
    )(whole)
    return dealt.reshape(GROUP * rows, columns // GROUP)


def undeal_kernel(moves, dealt_ref, whole_ref):
    for first, width, p, at in moves:
        whole_ref[:, first : first + width] = dealt_ref[p, :, at : at + width].astype(f32)


def undeal(dealt, moves):
    rows, columns = dealt.shape[0] // GROUP, dealt.shape[1] * GROUP
    dealt = dealt.reshape(GROUP, rows, columns // GROUP)
    if any(width % 128 for _, width, _, _ in moves):
        return jnp.concatenate(
            [dealt[p, :, at : at + width] for _, width, p, at in sorted(moves)], axis=1
        ).astype(f32)
    return pl.pallas_call(
        functools.partial(undeal_kernel, moves),
        out_shape=jax.ShapeDtypeStruct((rows, columns), f32),
    )(dealt)


def swap_plane(values):
    return lax.all_to_all(values, PLANE, 0, 0, tiled=True)


def chunk_at(block, quarter, rows):
    differs = block ^ quarter
    return differs % 2, pl.ds(pl.multiple_of(differs // 2 * rows, rows), rows)


def key_blocks(block, rows):
    return range(max(0, (block * rows - (LONGEST - 1)) // rows), block + 1)


def visible(start_col, block, key_block, rows):
    key_pos = key_block * rows + lax.broadcasted_iota(jnp.int32, (rows, rows), 1)
    seen = key_pos >= start_col
    if key_block == block:
        seen &= key_pos <= block * rows + lax.broadcasted_iota(jnp.int32, (rows, rows), 0)
    return seen


def softmax_blocks(query, rot_ref, start_col, block, rows, key_at):
    scores = []
    for key_block in key_blocks(block, rows):
        keys = rot_ref[key_block * rows : (key_block + 1) * rows, key_at : key_at + HD]
        piece = contract_last(query, keys) * HD ** (-0.5)
        scores.append(
            jnp.where(visible(start_col, block, key_block, rows), piece, masked_score)
        )
    top = functools.reduce(
        jnp.maximum, [jnp.max(piece, axis=1, keepdims=True) for piece in scores]
    )
    weights = [jnp.exp(piece - top) for piece in scores]
    total = functools.reduce(
        jnp.add, [jnp.sum(piece, axis=1, keepdims=True) for piece in weights]
    )
    inverse = 1.0 / total
    return [piece * inverse for piece in weights]


def attend_kernel(
    rows,
    blocks,
    head,
    place_ref,
    start_ref,
    level_ref,
    cos_ref,
    sin_ref,
    weight_ref,
    *others,
):
    pieces, others = others[:-6], others[-6:]
    rot_ref, out_ref, all_ref, hidden_ref, sem, out_sem = others
    quarter = place_ref[0]
    level_least = place_ref[1]
    sequence = pl.program_id(0)
    copies = copies_in(pieces, hidden_ref, sem)
    copy_out = pltpu.make_async_copy(hidden_ref, all_ref, out_sem)
    first = [copies[i] for i in (0, 1, 2, 7, 8, 9)]
    second = [copies[i] for i in (3, 4, 5, 6, 10, 11, 12, 13)]

    @pl.when(sequence == 0)
    def _():
        for copy in first + second:
            copy.start()
        for copy in first:
            copy.wait()

    @pl.when(sequence == 1)
    def _():
        for copy in second:
            copy.wait()
        copy_out.start()

    for block in range(blocks):
        here = slice(block * rows, (block + 1) * rows)
        other, there = chunk_at(block, quarter, rows)
        cos_rows, sin_rows = cos_ref[here, :], sin_ref[here, :]
        at = (other * 4 + sequence * 2 + (block ^ quarter) // 2) * rows
        hidden = hidden_ref[pl.ds(pl.multiple_of(at, rows), rows), :]
        projected = dot_plain(hidden, weight_ref[...])
        for col in range(0, 2 * HD, HD):
            piece = projected[:, col : col + HD]
            turned = piece * cos_rows + pltpu.roll(piece, HD // 2, 1) * sin_rows
            rot_ref[here, col : col + HD] = turned.astype(bf16)
        rot_ref[here, 2 * HD :] = projected[:, 2 * HD :].astype(bf16)
    for block in range(blocks):
        here = slice(block * rows, (block + 1) * rows)
        other, there = chunk_at(block, quarter, rows)
        query = rot_ref[here, :HD]
        probs = softmax_blocks(query, rot_ref, start_ref[here, :], block, rows, HD)
        total = None
        for key_block, piece in zip(key_blocks(block, rows), probs):
            values = rot_ref[key_block * rows : (key_block + 1) * rows, 2 * HD :]
            term = dot_plain(piece.astype(bf16), values)
            total = term if total is None else total + term
        kept = level_ref[other, there, :] >= level_least + head
        out_ref[other, there, :] = jnp.where(kept, total, 0.0).astype(bf16)

    @pl.when(sequence == 1)
    def _():
        copy_out.wait()


def attend_back_kernel(
    rows,
    blocks,
    place_ref,
    start_ref,
    level_ref,
    cos_ref,
    sin_ref,
    rot_refs_0,
    rot_refs_1,
    grad_ref,
    weight_0,
    weight_1,
    out_ref,
    hidden_ref,
    key_acc,
    value_acc,
):
    quarter = place_ref[0]
    level_least = place_ref[1]
    scale = HD ** (-0.5)

    def turn_back(piece, here):
        return piece * cos_ref[here, :] - pltpu.roll(piece, HD // 2, 1) * sin_ref[here, :]

    for head, rot_ref in ((0, rot_refs_0), (HD, rot_refs_1)):
        key_at, value_at = HD, 2 * HD
        out_at = head * 3
        key_acc[...] = jnp.zeros_like(key_acc)
        value_acc[...] = jnp.zeros_like(value_acc)
        for block in range(blocks):
            here = slice(block * rows, (block + 1) * rows)
            other, there = chunk_at(block, quarter, rows)
            query = rot_ref[here, :HD]
            kept = level_ref[other, there, :] >= level_least + head // HD
            grad = jnp.where(kept, grad_ref[other, there, head : head + HD], 0.0).astype(bf16)
            probs = softmax_blocks(query, rot_ref, start_ref[here, :], block, rows, key_at)
            grad_probs, inner = [], None
            for key_block, piece in zip(key_blocks(block, rows), probs):
                keys_at = slice(key_block * rows, (key_block + 1) * rows)
                grad_piece = contract_last(grad, rot_ref[keys_at, value_at : value_at + HD])
                grad_probs.append(grad_piece)
                term = jnp.sum(grad_piece * piece, axis=1, keepdims=True)
                inner = term if inner is None else inner + term
            query_grad = None
            for key_block, piece, grad_piece in zip(key_blocks(block, rows), probs, grad_probs):
                keys_at = slice(key_block * rows, (key_block + 1) * rows)
                grad_scores = (piece * (grad_piece - inner)).astype(bf16)
                term = dot_plain(grad_scores, rot_ref[keys_at, key_at : key_at + HD])
                query_grad = term if query_grad is None else query_grad + term
                key_acc[keys_at, :] += contract_first(grad_scores, query)
                value_acc[keys_at, :] += contract_first(piece.astype(bf16), grad)
            out_ref[other, there, out_at : out_at + HD] = turn_back(query_grad * scale, here).astype(bf16)
        for block in range(blocks):
            here = slice(block * rows, (block + 1) * rows)
            other, there = chunk_at(block, quarter, rows)
            out_ref[other, there, out_at + HD : out_at + 2 * HD] = turn_back(
                key_acc[here, :] * scale, here
            ).astype(bf16)
            out_ref[other, there, out_at + 2 * HD : out_at + 3 * HD] = value_acc[
                here, :
            ].astype(bf16)
    for block in range(blocks):
        other, there = chunk_at(block, quarter, rows)
        hidden_ref[other, there, :] = (
            contract_last(out_ref[other, there, : 3 * HD], weight_0[...])
            + contract_last(out_ref[other, there, 3 * HD :], weight_1[...])
        ).astype(bf16)


def chunked(seq_rows, columns):
    return pl.BlockSpec((2, None, seq_rows // 2, columns), lambda s, place: (0, s, 0, 0))


def attend(place, starts, levels, cos_table, sin_table, weight, pieces, rows, head):
    seq_rows = cos_table.shape[0]
    body = functools.partial(attend_kernel, rows, seq_rows // rows, head)
    return pl.pallas_call(
        body,
        grid_spec=pltpu.PrefetchScalarGridSpec(
            num_scalar_prefetch=1,
            grid=(2,),
            in_specs=[
                pl.BlockSpec((seq_rows, 1), lambda s, place: (s, 0)),
                chunked(seq_rows, 1),
                pl.BlockSpec((seq_rows, HD), lambda s, place: (0, 0)),
                pl.BlockSpec((seq_rows, HD), lambda s, place: (0, 0)),
                pl.BlockSpec((D, 3 * HD), lambda s, place: (0, 0)),
            ]
            + [pl.BlockSpec(memory_space=pl.ANY)] * len(pieces),
            out_specs=[
                pl.BlockSpec((seq_rows, 3 * HD), lambda s, place: (s, 0)),
                chunked(seq_rows, HD),
                pl.BlockSpec(memory_space=pl.ANY),
            ],
            scratch_shapes=[
                pltpu.VMEM((2 * seq_rows, D), bf16),
                pltpu.SemaphoreType.DMA((len(pieces),)),
                pltpu.SemaphoreType.DMA,
            ],
        ),
        out_shape=[
            jax.ShapeDtypeStruct((2 * seq_rows, 3 * HD), bf16),
            jax.ShapeDtypeStruct((2, 2, seq_rows // 2, HD), bf16),
            jax.ShapeDtypeStruct((2 * seq_rows, D), bf16),
        ],
        compiler_params=pltpu.CompilerParams(vmem_limit_bytes=48 * 1024 * 1024),
    )(
        place,
        starts,
        levels,
        cos_table,
        sin_table,
        weight,
        *pieces,
    )


def attend_back(place, starts, levels, cos_table, sin_table, rotated, grad, weights, rows):
    seq_rows = cos_table.shape[0]
    body = functools.partial(attend_back_kernel, rows, seq_rows // rows)
    grad_projected, grad_hidden = pl.pallas_call(
        body,
        grid_spec=pltpu.PrefetchScalarGridSpec(
            num_scalar_prefetch=1,
            grid=(2,),
            in_specs=[
                pl.BlockSpec((seq_rows, 1), lambda s, place: (s, 0)),
                chunked(seq_rows, 1),
                pl.BlockSpec((seq_rows, HD), lambda s, place: (0, 0)),
                pl.BlockSpec((seq_rows, HD), lambda s, place: (0, 0)),
                pl.BlockSpec((seq_rows, 3 * HD), lambda s, place: (s, 0)),
                pl.BlockSpec((seq_rows, 3 * HD), lambda s, place: (s, 0)),
                chunked(seq_rows, SHARE),
                pl.BlockSpec((D, 3 * HD), lambda s, place: (0, 0)),
                pl.BlockSpec((D, 3 * HD), lambda s, place: (0, 0)),
            ],
            out_specs=[chunked(seq_rows, 3 * SHARE), chunked(seq_rows, D)],
            scratch_shapes=[pltpu.VMEM((seq_rows, HD), f32), pltpu.VMEM((seq_rows, HD), f32)],
        ),
        out_shape=[
            jax.ShapeDtypeStruct((2, 2, seq_rows // 2, 3 * SHARE), bf16),
            jax.ShapeDtypeStruct((2, 2, seq_rows // 2, D), bf16),
        ],
        compiler_params=pltpu.CompilerParams(vmem_limit_bytes=48 * 1024 * 1024),
    )(
        place,
        starts,
        levels,
        cos_table,
        sin_table,
        *rotated,
        grad.reshape(2, 2, seq_rows // 2, SHARE),
        *weights,
    )
    return (
        grad_projected.reshape(2 * seq_rows, 3 * SHARE),
        grad_hidden.reshape(2 * seq_rows, D),
    )


BLOCK = 512
NARROW = 512


def narrower(block):
    wide = min(NARROW, block)
    return [slice(at, at + wide) for at in range(0, block, wide)]


def of_two(step, half, body, mine_ref, other_ref):
    @pl.when(step < half)
    def _():
        body(mine_ref)

    @pl.when(step >= half)
    def _():
        body(other_ref)


def lift_kernel(half, gate_ref, limit_ref, unit_ref, mine_ref, other_ref, *others):
    feed_pieces, upstream_pieces = others[:7], others[7:14]
    rectified_ref, activated_ref, grad_ref, feed_all, upstream_all = others[14:19]
    feed_ref, upstream_ref, feed_sem, upstream_sem, out_sem = others[19:]
    step = pl.program_id(0)
    wide = grad_ref.shape[1]
    feed_in = copies_in(feed_pieces, feed_ref, feed_sem)
    upstream_in = copies_in(upstream_pieces, upstream_ref, upstream_sem)
    feed_out = pltpu.make_async_copy(feed_ref, feed_all, out_sem.at[0])
    upstream_out = pltpu.make_async_copy(upstream_ref, upstream_all, out_sem.at[1])

    @pl.when(step == 0)
    def _():
        for copy in feed_in + upstream_in:
            copy.start()
        for copy in feed_in:
            copy.wait()
        feed_out.start()

    def body(up_ref):
        for at in narrower(rectified_ref.shape[1]):
            kept = unit_ref[:, at] < limit_ref[...]
            lifted = dot_plain(feed_ref[...], up_ref[:, at])
            rectified = jnp.where(kept, jnp.maximum(lifted, 0.0), 0.0)
            rectified_ref[:, at] = rectified
            activated_ref[:, at] = (rectified * rectified).astype(bf16)

    of_two(step, half, body, mine_ref, other_ref)

    @pl.when(step == 0)
    def _():
        for copy in upstream_in:
            copy.wait()
        upstream_out.start()

    upstream = upstream_ref[:, pl.ds(pl.multiple_of(step * wide, wide), wide)]
    grad_ref[...] = (gate_ref[...] * upstream.astype(f32)).astype(bf16)

    @pl.when(step == 2 * half - 1)
    def _():
        feed_out.wait()
        upstream_out.wait()


def lift(gate, limit, unit, up_mine, up_other, feed, upstream):
    count, units = gate.shape[0], up_mine.shape[1]
    block = min(BLOCK, units)
    half = units // block
    steps = 2 * half
    wide = D // steps
    return pl.pallas_call(
        functools.partial(lift_kernel, half),
        grid=(steps,),
        in_specs=[
            pl.BlockSpec((count, 1), lambda s: (0, 0)),
            pl.BlockSpec((count, 1), lambda s: (0, 0)),
            pl.BlockSpec((1, block), lambda s: (0, s)),
            pl.BlockSpec((D, block), lambda s: (0, jnp.minimum(s, half - 1))),
            pl.BlockSpec((D, block), lambda s: (0, jnp.maximum(s - half, 0))),
        ]
        + [pl.BlockSpec(memory_space=pl.ANY)] * 14,
        out_specs=[
            pl.BlockSpec((count, block), lambda s: (0, s)),
            pl.BlockSpec((count, block), lambda s: (0, s)),
            pl.BlockSpec((count, wide), lambda s: (0, s)),
            pl.BlockSpec(memory_space=pl.ANY),
            pl.BlockSpec(memory_space=pl.ANY),
        ],
        out_shape=[
            jax.ShapeDtypeStruct((count, 2 * units), f32),
            jax.ShapeDtypeStruct((count, 2 * units), bf16),
            jax.ShapeDtypeStruct((count, D), bf16),
            jax.ShapeDtypeStruct((count, D), bf16),
            jax.ShapeDtypeStruct((count, D), bf16),
        ],
        scratch_shapes=[
            pltpu.VMEM((count, D), bf16),
            pltpu.VMEM((count, D), bf16),
            pltpu.SemaphoreType.DMA((7,)),
            pltpu.SemaphoreType.DMA((7,)),
            pltpu.SemaphoreType.DMA((2,)),
        ],
        compiler_params=pltpu.CompilerParams(vmem_limit_bytes=56 * 1024 * 1024),
    )(gate, limit, unit, up_mine, up_other, *feed, *upstream)


def mixed_back_kernel(weight_ref, *others):
    pieces, (grad_ref, all_ref, whole_ref, sem, out_sem) = others[:7], others[7:]
    copies = copies_in(pieces, whole_ref, sem)
    copy_out = pltpu.make_async_copy(whole_ref, all_ref, out_sem)
    for copy in copies:
        copy.start()
    for copy in copies:
        copy.wait()
    copy_out.start()
    grad_ref[...] = contract_last(whole_ref[...], weight_ref[...]).astype(bf16)
    copy_out.wait()


def mixed_back(weight, pieces):
    count = sum(piece.shape[0] for piece in pieces)
    return pl.pallas_call(
        mixed_back_kernel,
        in_specs=[pl.BlockSpec(memory_space=pltpu.VMEM)]
        + [pl.BlockSpec(memory_space=pl.ANY)] * len(pieces),
        out_specs=[pl.BlockSpec(memory_space=pltpu.VMEM), pl.BlockSpec(memory_space=pl.ANY)],
        out_shape=[
            jax.ShapeDtypeStruct((count, weight.shape[0]), bf16),
            jax.ShapeDtypeStruct((count, D), bf16),
        ],
        scratch_shapes=[
            pltpu.VMEM((count, D), bf16),
            pltpu.SemaphoreType.DMA((len(pieces),)),
            pltpu.SemaphoreType.DMA,
        ],
        compiler_params=pltpu.CompilerParams(vmem_limit_bytes=48 * 1024 * 1024),
    )(weight, *pieces)


def lower_kernel(
    half,
    grad_ref,
    rectified_ref,
    down_mine_ref,
    down_other_ref,
    up_mine_ref,
    up_other_ref,
    lifted_ref,
    input_ref,
    kept_ref,
):
    step = pl.program_id(0)
    count, block = rectified_ref.shape
    units = half * block

    @pl.when(step < 2 * half)
    def _():
        columns = pl.ds(pl.multiple_of(step * block, block), block)

        def body(down_ref):
            for at in narrower(block):
                grad = contract_last(grad_ref[...], down_ref[at, :])
                lifted_ref[:, at] = (grad * 2.0 * rectified_ref[:, at]).astype(bf16)

        of_two(step, half, body, down_mine_ref, down_other_ref)
        kept_ref[:, columns] = lifted_ref[...]

    @pl.when(step >= 2 * half)
    def _():
        for at in narrower(input_ref.shape[1]):
            input_ref[:, at] = (
                contract_last(kept_ref[:, :units], up_mine_ref[at, :])
                + contract_last(kept_ref[:, units:], up_other_ref[at, :])
            ).astype(bf16)


def lower(grad, rectified, down_mine, down_other, up_mine, up_other):
    count, units = grad.shape[0], up_mine.shape[1]
    block = min(BLOCK, units)
    half = units // block
    first, second = 2 * half, D // BLOCK
    once = pl.Buffered(1)
    return pl.pallas_call(
        functools.partial(lower_kernel, half),
        grid=(first + second,),
        in_specs=[
            pl.BlockSpec((count, D), lambda s: (0, 0), pipeline_mode=once),
            pl.BlockSpec((count, block), lambda s: (0, jnp.minimum(s, first - 1))),
            pl.BlockSpec((block, D), lambda s: (jnp.minimum(s, half - 1), 0)),
            pl.BlockSpec((block, D), lambda s: (jnp.clip(s - half, 0, half - 1), 0)),
            pl.BlockSpec((BLOCK, units), lambda s: (jnp.maximum(s - first, 0), 0)),
            pl.BlockSpec((BLOCK, units), lambda s: (jnp.maximum(s - first, 0), 0)),
        ],
        out_specs=[
            pl.BlockSpec((count, block), lambda s: (0, jnp.minimum(s, first - 1))),
            pl.BlockSpec((count, BLOCK), lambda s: (0, jnp.maximum(s - first, 0))),
        ],
        out_shape=[
            jax.ShapeDtypeStruct((count, 2 * units), bf16),
            jax.ShapeDtypeStruct((count, D), bf16),
        ],
        scratch_shapes=[pltpu.VMEM((count, 2 * units), bf16)],
        compiler_params=pltpu.CompilerParams(vmem_limit_bytes=56 * 1024 * 1024),
    )(grad, rectified, down_mine, down_other, up_mine, up_other)


def branch_kernel(activated_ref, upstream_ref, mine_ref, other_ref, branch_ref, part_ref):
    units = mine_ref.shape[0]
    total = None
    for at in narrower(branch_ref.shape[1]):
        branch = dot_plain(activated_ref[:, :units], mine_ref[:, at]) + dot_plain(
            activated_ref[:, units:], other_ref[:, at]
        )
        branch_ref[:, at] = branch.astype(bf16)
        part = jnp.sum(branch * upstream_ref[:, at].astype(f32), axis=1, keepdims=True)
        total = part if total is None else total + part

    @pl.when(pl.program_id(0) == 0)
    def _():
        part_ref[...] = total

    @pl.when(pl.program_id(0) > 0)
    def _():
        part_ref[...] += total


def branch(activated, upstream, down_mine, down_other):
    count, units = activated.shape[0], down_mine.shape[0]
    once = pl.Buffered(1)
    return pl.pallas_call(
        branch_kernel,
        grid=(D // BLOCK,),
        in_specs=[
            pl.BlockSpec((count, 2 * units), lambda s: (0, 0), pipeline_mode=once),
            pl.BlockSpec((count, BLOCK), lambda s: (0, s)),
            pl.BlockSpec((units, BLOCK), lambda s: (0, s)),
            pl.BlockSpec((units, BLOCK), lambda s: (0, s)),
        ],
        out_specs=[
            pl.BlockSpec((count, BLOCK), lambda s: (0, s)),
            pl.BlockSpec((count, 1), lambda s: (0, 0)),
        ],
        out_shape=[
            jax.ShapeDtypeStruct((count, D), bf16),
            jax.ShapeDtypeStruct((count, 1), f32),
        ],
        compiler_params=pltpu.CompilerParams(vmem_limit_bytes=56 * 1024 * 1024),
    )(activated, upstream, down_mine, down_other)


def local(
    planes,
    tokens,
    documents,
    head_level,
    width_level,
    mixer_gain,
    mixer_bias,
    input_weight,
    output_weight,
    mixer_router,
    feed_gain,
    feed_bias,
    up_weight,
    down_weight,
    feed_router,
    cotangent,
):
    rows = tokens.shape[0]
    seq_rows = documents.shape[1]
    weight_rows = input_weight.shape[0]
    unit_rows = down_weight.shape[0]
    at_core = lax.axis_index("c")
    chip = lax.axis_index("x") * 2 + lax.axis_index("y")
    at_plane = chip * 2 + at_core
    quarter = at_plane % (seq_rows // rows)
    place = jnp.stack([quarter, 2 * at_core]).astype(jnp.int32)

    def pieces(values):
        return [values[at : at + rows] for at in range(0, values.shape[0], rows)]

    def both_cores(mine, other):
        return (mine.astype(f32) + flip(other, "c").astype(f32)).astype(bf16)

    levels = jnp.concatenate(
        [head_level.reshape(2, rows // 2), width_level.reshape(2, rows // 2)], axis=1
    )
    levels = levels.astype(f32)
    levels = gather_small(levels)
    plane_docs = jnp.concatenate([documents, flip(documents, "x")], axis=0)
    starts = jnp.sum(
        (plane_docs[:, None, :] < plane_docs[:, :, None]).astype(jnp.int32), axis=2
    ).reshape(2 * seq_rows, 1)
    level_range = jnp.arange(OPTIONS)
    head_counts = jnp.sum((head_level[:, None] == level_range[None, :]).astype(f32), axis=0)
    width_counts = jnp.sum((width_level[:, None] == level_range[None, :]).astype(f32), axis=0)

    output_blocks = [output_weight]
    if planes == 4:
        output_blocks += [
            lax.ppermute(output_weight, "z", [(i, i ^ d) for i in range(planes)])
            for d in range(1, planes)
        ]
    input_first = swap_plane(deal(input_weight, attention_columns()))
    weights = [lax.all_gather(input_first[:, : 3 * HD], "z", axis=0, tiled=True)]
    token_values = tokens.astype(f32)
    mixer_hidden, mixer_normed, mixer_scale = normalize(token_values, mixer_gain, mixer_bias)
    mixer_gate, mixer_probs, mixer_chosen = route(mixer_hidden, mixer_router, head_level)
    mixer_pieces = gather_eight(mixer_hidden.astype(bf16))
    (
        mixer_pieces[1:5],
        input_second,
        output_blocks,
        up_weight,
        cotangent_sent,
        levels,
        starts,
    ) = lax.optimization_barrier(
        (
            mixer_pieces[1:5],
            input_first[:, 3 * HD :],
            output_blocks,
            up_weight,
            cotangent,
            levels,
            starts,
        )
    )
    weights.append(lax.all_gather(input_second, "z", axis=0, tiled=True))
    output_share = share_heads(output_blocks)
    width_all = levels[:, :, rows // 2 :].reshape(4 * rows)
    limit = (width_all[:, None].astype(jnp.int32) + 1) * (FF // OPTIONS)
    head_all = levels[:, :, : rows // 2].reshape(4, rows)
    head_all = jnp.concatenate([head_all, flip(head_all, "c")], axis=0)
    head_all = head_all.reshape(2, 2, 2 * rows, 1)
    up_first = swap_plane(deal(up_weight, unit_columns(planes, unit_rows)))
    weights[1], up_first = lax.optimization_barrier((weights[1], up_first))
    up_mine = lax.all_gather(up_first, "z", axis=0, tiled=True)
    down_mine = lax.all_gather(after(down_weight, up_first), "z", axis=0, tiled=True)
    upstream_pieces = gather_four(cotangent_sent)

    cos_table, sin_table = rope_tables(jnp.arange(seq_rows).astype(f32))
    attending = functools.partial(attend, place, starts, head_all, cos_table, sin_table)
    rotated_0, mixed_0, mixer_all = attending(weights[0], mixer_pieces, rows, 0)
    weights[1], mixed_0, upstream_pieces[1:5] = lax.optimization_barrier(
        (weights[1], mixed_0, upstream_pieces[1:5])
    )
    rotated_1, mixed_1, _ = attending(weights[1], mixer_pieces, rows, 1)
    mixed = [m.reshape(2, 4 * rows, HD) for m in (mixed_0, mixed_1)]
    mixed_all = jnp.concatenate(
        [m[0] for m in mixed] + [flip(m[1], "c") for m in mixed], axis=1
    )
    mixed_all, upstream_pieces[5:] = lax.optimization_barrier((mixed_all, upstream_pieces[5:]))
    mixer_branch = scatter_four(pieces(dot_plain(mixed_all, output_share).astype(bf16)))
    middle = token_values + mixer_gate[:, None] * mixer_branch
    feed_hidden, feed_normed, feed_scale = normalize(middle, feed_gain, feed_bias)
    feed_gate, feed_probs, feed_chosen = route(feed_hidden, feed_router, width_level)
    upstream = cotangent.astype(f32)

    up_mine, feed_low = lax.optimization_barrier((up_mine, feed_hidden.astype(bf16)))
    up_other = flip(up_mine, "c")
    feed_pieces = gather_four(feed_low)
    gate_all = gather_small(feed_gate.reshape(2, rows // 2)).reshape(4 * rows, 1)
    units = planes * unit_rows
    unit = jnp.arange(units, dtype=jnp.int32)
    unit = jnp.concatenate(
        [
            (unit // unit_rows * GROUP + share) * unit_rows + unit % unit_rows
            for share in (at_plane, at_plane ^ 1)
        ]
    )
    rectified, activated, grad_branch_all, feed_all, upstream_all = lift(
        gate_all, limit, unit[None, :], up_mine, up_other, feed_pieces, upstream_pieces
    )
    down_part_other = contract_first(activated[:, units:], grad_branch_all).astype(bf16)
    down_part = both_cores(
        contract_first(activated[:, :units], grad_branch_all), down_part_other
    )
    down_mine, down_part_other = lax.optimization_barrier((down_mine, down_part_other))
    down_other = flip(down_mine, "c")
    down_sum = lax.psum_scatter(down_part, "z", scatter_dimension=0, tiled=True)
    lifted, input_pieces = lower(
        grad_branch_all, rectified, down_mine, down_other, up_mine, up_other
    )
    activated, input_pieces = lax.optimization_barrier((activated, input_pieces))
    input_pieces = pieces(input_pieces)
    input_sent = scatter_send(input_pieces)
    branch_pieces, gate_part = branch(activated, upstream_all, down_mine, down_other)
    lifted, gate_part, input_sent = lax.optimization_barrier((lifted, gate_part, input_sent))
    grad_feed_gate = sum_small(gate_part.reshape(4, 2, rows // 2)).reshape(rows)
    up_part_other = contract_first(feed_all, lifted[:, units:]).astype(bf16)
    up_part = both_cores(contract_first(feed_all, lifted[:, :units]), up_part_other)
    grad_feed_input = scatter_end(input_pieces, input_sent)

    feed_router_term, grad_feed_routed = route_back(
        grad_feed_gate, feed_probs, feed_chosen, feed_hidden, feed_router
    )
    grad_middle_norm, feed_gain_term, feed_bias_term = normalize_back(
        grad_feed_input + grad_feed_routed, feed_normed, feed_scale, feed_gain
    )
    grad_middle = upstream + grad_middle_norm
    grad_mixer_gate = jnp.sum(mixer_branch * grad_middle, axis=1)
    grad_mixer_branch = (mixer_gate[:, None] * grad_middle).astype(bf16)
    grad_mixer_branch, down_sum, up_part = lax.optimization_barrier(
        (grad_mixer_branch, down_sum, up_part)
    )
    up_sum = lax.psum_scatter(up_part, "z", scatter_dimension=0, tiled=True)
    grad_attended, grad_mixer_all = mixed_back(output_share, gather_four(grad_mixer_branch))
    grad_attended = jnp.concatenate(
        [grad_attended[:, :SHARE], flip(grad_attended[:, SHARE:], "c")], axis=0
    )

    branch_pieces, grad_attended = lax.optimization_barrier((branch_pieces, grad_attended))
    branch_pieces = pieces(branch_pieces)
    branch_sent = scatter_send(branch_pieces)
    output_part = contract_first(mixed_all, grad_mixer_all).astype(bf16)
    grad_projected, mixer_pieces = attend_back(
        place,
        starts,
        head_all,
        cos_table,
        sin_table,
        (rotated_0, rotated_1),
        grad_attended,
        weights,
        rows,
    )
    grad_projected, up_sum, branch_sent = lax.optimization_barrier(
        (grad_projected, up_sum, branch_sent)
    )
    feed_branch = scatter_end(branch_pieces, branch_sent)
    input_part = contract_first(mixer_all, grad_projected).astype(bf16)
    input_sum = lax.psum_scatter(input_part, "z", scatter_dimension=0, tiled=True)
    mixer_pieces, feed_branch = lax.optimization_barrier(
        (add_cores(pieces(mixer_pieces)), feed_branch)
    )
    outputs = (middle + feed_gate[:, None] * feed_branch).astype(bf16)
    grad_mixer_input = scatter_four(mixer_pieces)
    input_sum, output_part = lax.optimization_barrier((input_sum, output_part))
    grad_output_weight = sum_heads(output_part, planes, weight_rows).astype(f32)
    grad_mixer_input, up_sum = lax.optimization_barrier((grad_mixer_input, up_sum))
    up_back = swap_plane(up_sum)

    mixer_router_term, grad_mixer_routed = route_back(
        grad_mixer_gate, mixer_probs, mixer_chosen, mixer_hidden, mixer_router
    )
    grad_token_norm, mixer_gain_term, mixer_bias_term = normalize_back(
        grad_mixer_input + grad_mixer_routed, mixer_normed, mixer_scale, mixer_gain
    )
    grad_tokens = grad_middle + grad_token_norm
    counts = jnp.pad(jnp.concatenate([head_counts, width_counts]), (0, D - 2 * OPTIONS))
    rows_of = [mixer_gain_term, mixer_bias_term, feed_gain_term, feed_bias_term, counts]
    sums, input_back = sum_everywhere(
        jnp.concatenate([jnp.stack(rows_of), mixer_router_term, feed_router_term], axis=0),
        planes,
        swap_plane(input_sum),
    )
    grad_down_weight = down_sum.astype(f32)
    grad_up_weight = undeal(up_back, unit_columns(planes, unit_rows))
    grad_input_weight = undeal(input_back, attention_columns())
    return (
        outputs,
        grad_tokens,
        sums[0],
        sums[1],
        grad_input_weight,
        grad_output_weight,
        sums[5:9].T,
        sums[2],
        sums[3],
        grad_up_weight,
        grad_down_weight,
        sums[9:13].T,
        sums[4, : 2 * OPTIONS].reshape(2, OPTIONS),
    )


def solution(mesh):
    wide, narrow = mesh.shape["wide"], mesh.shape["narrow"]
    planes = wide // 2
    inner = Mesh(mesh.devices.reshape(planes, 2, narrow // 2, 2), ALL)
    rowwise = P(ALL, None)
    in_specs = (
        rowwise,
        P(("z", "x"), None),
        P(ALL),
        P(ALL),
        P(),
        P(),
        rowwise,
        rowwise,
        P(),
        P(),
        P(),
        rowwise,
        rowwise,
        P(),
        rowwise,
    )
    out_specs = (
        rowwise,
        rowwise,
        P(),
        P(),
        rowwise,
        rowwise,
        P(),
        P(),
        P(),
        rowwise,
        rowwise,
        P(),
        P(),
    )
    return jax.shard_map(
        functools.partial(local, planes),
        mesh=inner,
        in_specs=in_specs,
        out_specs=out_specs,
        check_vma=False,
    )
```

time: 895 us -> 629 us (0.70)
  waiting for transfers between devices: 450 us -> 221 us
  Pallas kernels: 34.3 us -> 139 us
  blocking collectives: 79.4 us -> 0 us
  matrix products: 143 us -> 66.3 us
  starting transfers between devices: 57.6 us -> 98.9 us
  local copies, waits for them, and re-layouts: 75.5 us -> 38.7 us
    reduce_scatter x4, waiting for transfers between devices: 131 us -> 13.1 us  [the longest x1 13.1 us: local(): lax.psum_scatter(input_part, 'z', scatter_dimension=0, tiled=True)]
    pallas_call x0 -> x8, Pallas kernels: none -> 76.3 us  [the longest x1 27.6 us: lower(): pl.pallas_call(functools.partial(lower_kernel, half), grid=(first + secon...]
    all_gather x4, waiting for transfers between devices: 80.3 us -> 14.7 us  [the longest x1 5.12 us: local(): weights = [lax.all_gather(input_first[:, :3 * HD], 'z', axis=0, tiled=True)]]
    all_to_all x3 -> x0, blocking collectives: 52 us -> none  [swap_plane(): return lax.all_to_all(values, PLANE, 0, 0, tiled=True)]
    dot_general x4 -> x1, matrix products: 45 us -> 2.34 us  [dot_plain(): return jnp.dot(left, right, preferred_element_type=f32)]
    dot_general x4 -> x0, matrix products: 37.5 us -> none  [contract_last(): lax.dot_general(left, right, (((1,), (1,)), ((), ())), preferred_element_...]
    unnamed x121 -> x105, local copies, waits for them, and re-layouts: 44.8 us -> 8.4 us
    ppermute x4 -> x2, waiting for transfers between devices: 31.1 us -> 0.01 us  [sum_everywhere(): lax.ppermute(values, 'z', [(i, i ^ step) for i in range(planes)])]
  transfers between devices with their start and end apart: 77 -> 99, of which waited for: 41 -> 41; matrix products, arithmetic and copies ran while one was open for 24% -> 20% of each run, Pallas kernels for 4% -> 22%
where the time goes in v2:
time: 629 us; the launch traced here: 622 us
  waiting for transfers between devices  221 us (35%)
  Pallas kernels  139 us (22%)
  starting transfers between devices  98.9 us (16%)
  matrix products  66.3 us (11%)
  other arithmetic  42.1 us (7%)
  local copies, waits for them, and re-layouts  38.7 us (6%)
  between operations  15.7 us (2%)
    ppermute x73, waiting for transfers between devices, flip(): return lax.ppermute(values, axis, [(0, 1), (1, 0)])  159 us
    ppermute x73, starting transfers between devices, flip(): return lax.ppermute(values, axis, [(0, 1), (1, 0)])  61.5 us
    dot_general x6, matrix products, contract_first(): lax.dot_general(left, right, (((0,), (0,)), ((), ())), preferred_element_...  49.4 us
    pallas_call x2, Pallas kernels, attend(): pl.pallas_call(body, grid_spec=pltpu.PrefetchScalarGridSpec(num_scalar_pr...  33.7 us
    pallas_call x1, Pallas kernels, attend_back(): pl.pallas_call(body, grid_spec=pltpu.PrefetchScalarGridSpec(num_scalar_pr...  29 us
    pallas_call x1, Pallas kernels, lower(): pl.pallas_call(functools.partial(lower_kernel, half), grid=(first + secon...  27.6 us
    pallas_call x1, Pallas kernels, lift(): pl.pallas_call(functools.partial(lift_kernel, half), grid=(steps,), in_sp...  19.8 us
    all_to_all x4, starting transfers between devices, swap_plane(): return lax.all_to_all(values, PLANE, 0, 0, tiled=True)  16.6 us
  transfers between devices with their start and end apart: 99, of which 41 were waited for; matrix products, arithmetic and copies ran while one was open for 20% of the time, Pallas kernels for 22%

profile of v2, /device:TPU:0, one launch (start us, length us, event | category | flops | bytes accessed | tf_op | source)
XLA Modules:
  0.0 621.8 jit_solution(7174847742697191447)
XLA Ops:
  7.2 3.1 collective-permute-start.4
  19.2 3.9 all-to-all-start
  28.6 17.5 %collective-permute-done.10 = s32[1,1024]{1,0:T(1,128)S(1)} collective-permute-done((s32[1,1024]{1,0:T(1,128)S(1)}, s32[1,1024]{1,0:T(1,128)S(1)}, u32[]{:S(2)}, u32[]{:S(2)}) %collective-permute-start.10) | collective-permute-done | bytes 4128 | tf_op jit(solution)/shard_map/ppermute | solution.py:89
  50.6 7.1 %collective-permute-done.6 = bf16[64,2048]{1,0:T(8,128)(2,1)} collective-permute-done((bf16[64,2048]{1,0:T(8,128)(2,1)}, bf16[64,2048]{1,0:T(8,128)(2,1)}, u32[]{:S(2)}, u32[]{:S(2)}) %collective-permute-start.6) | collective-permute-done | bytes 262176 | tf_op jit(solution)/shard_map/ppermute | solution.py:850
  61.0 3.2 fusion.47
  68.2 4.3 all-to-all-start.1
  86.3 3.3 fusion.118
  91.0 4.8 all-gather.5.cloned.1.call-done.weight_ref.weight_1
  107.6 16.9 %collective-permute-done.24.others_11_ = bf16[128,2048]{1,0:T(8,128)(2,1)} collective-permute-done((bf16[128,2048]{1,0:T(8,128)(2,1)}, bf16[128,2048]{1,0:T(8,128)(2,1)}, u32[]{:S(2)}, u32[]{:S(2)}) %collective-permute-start.24) | collective-permute-done | bytes 524320 | tf_op jit(solution)/shard_map/ppermute | solution.py:89
  128.2 5.1 all-gather.7.cloned.1.call-done.weight_ref.weight_0
  135.5 16.6 %shard_map.248 = (bf16[2048,384]{1,0:T(8,128)(2,1)}, bf16[2,2,512,128]{3,2,1,0:T(8,128)(2,1)S(1)}, bf16[2048,2048]{1,0:T(8,128)(2,1)}) custom-call(s32[2]{0:T(128)S(1)} %pad_add_fusion.2.place_ref, s32[2048,1]{1,0:T(8,128)} %copy.38.start_ref, f32[2,2,512,1]{3,2,1,0:T(8,128)} %reshape.275.level_ref, f32[1024,128]{1,0:T(8,128)S(1)} %get-tuple-element.269.cos_ref, ...), custom_call_target="tpu_custom_call" | custom-call | tf_op jit(solution)/shard_map/pallas_call | solution.py:467
  152.1 17.0 %shard_map.249 = (bf16[2048,384]{1,0:T(8,128)(2,1)}, bf16[2,2,512,128]{3,2,1,0:T(8,128)(2,1)S(1)}, bf16[2048,2048]{1,0:T(8,128)(2,1)}) custom-call(s32[2]{0:T(128)S(1)} %pad_add_fusion.2.place_ref, s32[2048,1]{1,0:T(8,128)} %copy.38.start_ref, f32[2,2,512,1]{3,2,1,0:T(8,128)} %reshape.275.level_ref, f32[1024,128]{1,0:T(8,128)S(1)} %get-tuple-element.269.cos_ref, ...), custom_call_target="tpu_custom_call" | custom-call | tf_op jit(solution)/shard_map/pallas_call | solution.py:467
  178.1 10.6 %collective-permute-done.31 = bf16[128,2048]{1,0:T(8,128)(2,1)S(1)} collective-permute-done((bf16[128,2048]{1,0:T(8,128)(2,1)S(1)}, bf16[128,2048]{1,0:T(8,128)(2,1)S(1)}, u32[]{:S(2)}, u32[]{:S(2)}) %collective-permute-start.31) | collective-permute-done | bytes 524320 | tf_op jit(solution)/shard_map/ppermute | solution.py:89
  193.0 7.0 %collective-permute-done.30 = bf16[128,2048]{1,0:T(8,128)(2,1)S(1)} collective-permute-done((bf16[128,2048]{1,0:T(8,128)(2,1)S(1)}, bf16[128,2048]{1,0:T(8,128)(2,1)S(1)}, u32[]{:S(2)}, u32[]{:S(2)}) %collective-permute-start.30) | collective-permute-done | bytes 524320 | tf_op jit(solution)/shard_map/ppermute | solution.py:89
  201.5 10.2 %collective-permute-done.32 = bf16[128,2048]{1,0:T(8,128)(2,1)S(1)} collective-permute-done((bf16[128,2048]{1,0:T(8,128)(2,1)S(1)}, bf16[128,2048]{1,0:T(8,128)(2,1)S(1)}, u32[]{:S(2)}, u32[]{:S(2)}) %collective-permute-start.32) | collective-permute-done | bytes 524320 | tf_op jit(solution)/shard_map/ppermute | solution.py:89
  222.7 11.2 %collective-permute-done.38 = f32[2,128]{1,0:T(2,128)S(1)} collective-permute-done((f32[2,128]{1,0:T(2,128)S(1)}, f32[2,128]{1,0:T(2,128)S(1)}, u32[]{:S(2)}, u32[]{:S(2)}) %collective-permute-start.38) | collective-permute-done | bytes 1056 | tf_op jit(solution)/shard_map/ppermute | solution.py:146
  243.6 6.9 %collective-permute-done.41.others_2_ = bf16[128,2048]{1,0:T(8,128)(2,1)} collective-permute-done((bf16[128,2048]{1,0:T(8,128)(2,1)}, bf16[128,2048]{1,0:T(8,128)(2,1)}, u32[]{:S(2)}, u32[]{:S(2)}) %collective-permute-start.41) | collective-permute-done | bytes 524320 | tf_op jit(solution)/shard_map/ppermute | solution.py:89
  252.6 8.9 %collective-permute-done.44.others_5_ = bf16[128,2048]{1,0:T(8,128)(2,1)} collective-permute-done((bf16[128,2048]{1,0:T(8,128)(2,1)}, bf16[128,2048]{1,0:T(8,128)(2,1)}, u32[]{:S(2)}, u32[]{:S(2)}) %collective-permute-start.44) | collective-permute-done | bytes 524320 | tf_op jit(solution)/shard_map/ppermute | solution.py:89
  261.5 19.8 %shard_map.250 = (f32[1024,2048]{1,0:T(8,128)}, bf16[1024,2048]{1,0:T(8,128)(2,1)}, bf16[1024,2048]{1,0:T(8,128)(2,1)}, bf16[1024,2048]{1,0:T(8,128)(2,1)}, bf16[1024,2048]{1,0:T(8,128)(2,1)}) custom-call(f32[1024,1]{1,0:T(8,128)} %copy.42.gate_ref, s32[1024,1]{1,0:T(8,128)} %copy.43.limit_ref, s32[1,2048]{1,0:T(1,128)} %bitcast.122, ...), custom_call_target="tpu_custom_call" | custom-call | tf_op jit(solution)/shard_map/pallas_call | solution.py:620
  281.3 9.3 %convolution_convert_fusion.2 = bf16[1024,2048]{1,0:T(8,128)(2,1)} fusion(bf16[1024,2048]{1,0:T(8,128)(2,1)} %get-tuple-element.120.grad_ref, bf16[1024,2048]{1,0:T(8,128)(2,1)} %get-tuple-element.125.activated_ref), kind=kOutput, calls=%fused_computation.5 | convolution fusion | flops 4297064448 | bytes 10485760 | tf_op jit(solution)/shard_map/dot_general | solution.py:85
  290.6 4.7 all-gather.11.cloned.1.call-done.down_mine_ref.mine_ref
  298.1 10.6 %add_convert_fusion.1 = bf16[1024,2048]{1,0:T(8,128)(2,1)} fusion(bf16[1024,2048]{1,0:T(8,128)(2,1)} %collective-permute-done.56, bf16[1024,2048]{1,0:T(8,128)(2,1)} %get-tuple-element.120.grad_ref, bf16[1024,2048]{1,0:T(8,128)(2,1)} %get-tuple-element.125.activated_ref), kind=kOutput, calls=%fused_computation.1 | convolution fusion | flops 4301258752 | bytes 14680064 | tf_op jit(solution)/shard_map/dot_general | solution.py:85
  308.8 27.6 %shard_map.251 = (bf16[1024,2048]{1,0:T(8,128)(2,1)}, bf16[1024,2048]{1,0:T(8,128)(2,1)}) custom-call(bf16[1024,2048]{1,0:T(8,128)(2,1)} %get-tuple-element.120.grad_ref, f32[1024,2048]{1,0:T(8,128)} %get-tuple-element.121.rectified_ref, bf16[1024,2048]{1,0:T(8,128)(2,1)} %all-gather.11.cloned.1.call-done.down_mine_ref.mine_ref, ...), custom_call_target="tpu_custom_call" | custom-call | tf_op jit(solution)/shard_map/pallas_call | solution.py:732
  342.3 14.9 %shard_map.252 = (bf16[1024,2048]{1,0:T(8,128)(2,1)}, f32[1024,1]{1,0:T(8,128)}) custom-call(bf16[1024,2048]{1,0:T(8,128)(2,1)} %get-tuple-element.125.activated_ref, bf16[1024,2048]{1,0:T(8,128)(2,1)} %get-tuple-element.126.upstream_ref, bf16[1024,2048]{1,0:T(8,128)(2,1)} %all-gather.11.cloned.1.call-done.down_mine_ref.mine_ref, ...), custom_call_target="tpu_custom_call" | custom-call | tf_op jit(solution)/shard_map/pallas_call | solution.py:779
  357.2 6.2 %collective-permute-done.49 = bf16[128,2048]{1,0:T(8,128)(2,1)S(1)} collective-permute-done((bf16[128,2048]{1,0:T(8,128)(2,1)S(1)}, bf16[128,2048]{1,0:T(8,128)(2,1)S(1)}, u32[]{:S(2)}, u32[]{:S(2)}) %collective-permute-start.49) | collective-permute-done | bytes 524320 | tf_op jit(solution)/shard_map/ppermute | solution.py:89
  364.0 7.6 %convolution_convert_fusion.1 = bf16[2048,1024]{1,0:T(8,128)(2,1)S(1)} fusion(bf16[1024,2048]{1,0:T(8,128)(2,1)} %get-tuple-element.136, bf16[1024,2048]{1,0:T(8,128)(2,1)} %get-tuple-element.137), kind=kOutput, calls=%fused_computation.4 | convolution fusion | flops 4297064448 | bytes 10485760 | tf_op jit(solution)/shard_map/dot_general | solution.py:85
  379.0 10.4 %collective-permute-done.51 = bf16[128,2048]{1,0:T(8,128)(2,1)S(1)} collective-permute-done((bf16[128,2048]{1,0:T(8,128)(2,1)S(1)}, bf16[128,2048]{1,0:T(8,128)(2,1)S(1)}, u32[]{:S(2)}, u32[]{:S(2)}) %collective-permute-start.51) | collective-permute-done | bytes 524320 | tf_op jit(solution)/shard_map/ppermute | solution.py:89
  398.0 6.5 %add_convert_fusion = bf16[2048,1024]{1,0:T(8,128)(2,1)} fusion(bf16[2048,1024]{1,0:T(8,128)(2,1)S(1)} %collective-permute-done.57, bf16[1024,2048]{1,0:T(8,128)(2,1)S(1)} %copy-done.48, bf16[1024,2048]{1,0:T(8,128)(2,1)S(1)} %copy-done.49), kind=kOutput, calls=%fused_computation | convolution fusion | flops 4301258752 | bytes 14680064 | tf_op jit(solution)/shard_map/dot_general | solution.py:85
  408.9 10.8 %collective-permute-done.58.others_1_ = bf16[128,2048]{1,0:T(8,128)(2,1)S(1)} collective-permute-done((bf16[128,2048]{1,0:T(8,128)(2,1)S(1)}, bf16[128,2048]{1,0:T(8,128)(2,1)S(1)}, u32[]{:S(2)}, u32[]{:S(2)}) %collective-permute-start.58) | collective-permute-done | bytes 524320 | tf_op jit(solution)/shard_map/ppermute | solution.py:89
  421.8 9.2 %collective-permute-done.59.others_2_ = bf16[128,2048]{1,0:T(8,128)(2,1)S(1)} collective-permute-done((bf16[128,2048]{1,0:T(8,128)(2,1)S(1)}, bf16[128,2048]{1,0:T(8,128)(2,1)S(1)}, u32[]{:S(2)}, u32[]{:S(2)}) %collective-permute-start.59) | collective-permute-done | bytes 524320 | tf_op jit(solution)/shard_map/ppermute | solution.py:89
  431.8 8.7 %collective-permute-done.62.others_5_ = bf16[128,2048]{1,0:T(8,128)(2,1)S(1)} collective-permute-done((bf16[128,2048]{1,0:T(8,128)(2,1)S(1)}, bf16[128,2048]{1,0:T(8,128)(2,1)S(1)}, u32[]{:S(2)}, u32[]{:S(2)}) %collective-permute-start.62) | collective-permute-done | bytes 524320 | tf_op jit(solution)/shard_map/ppermute | solution.py:89
  440.6 4.3 shard_map.253
  451.5 29.0 %shard_map.254 = (bf16[2,2,512,768]{3,2,1,0:T(8,128)(2,1)}, bf16[2,2,512,2048]{3,2,1,0:T(8,128)(2,1)}) custom-call(s32[2]{0:T(128)S(1)} %pad_add_fusion.2.place_ref, s32[2048,1]{1,0:T(8,128)S(1)} %copy-done.2, f32[2,2,512,1]{3,2,1,0:T(8,128)S(1)} %copy-done.3, f32[1024,128]{1,0:T(8,128)S(1)} %get-tuple-element.269.cos_ref, ...), custom_call_target="tpu_custom_call" | custom-call | tf_op jit(solution)/shard_map/pallas_call | solution.py:511
  480.6 11.7 %convolution_convert_fusion.3 = bf16[2048,768]{1,0:T(8,128)(2,1)} fusion(bf16[2048,2048]{1,0:T(8,128)(2,1)} %get-tuple-element.156, bf16[2048,768]{1,0:T(8,128)(2,1)} %bitcast.148), kind=kOutput, calls=%fused_computation.6 | convolution fusion | flops 6444023808 | bytes 14680064 | tf_op jit(solution)/shard_map/dot_general | solution.py:85
  492.3 2.8 fusion.104
  502.4 4.1 add_convert_fusion.3
  506.4 5.6 collective-permute-done.73
  522.1 7.4 %collective-permute-done.76 = bf16[128,2048]{1,0:T(8,128)(2,1)S(1)} collective-permute-done((bf16[128,2048]{1,0:T(8,128)(2,1)S(1)}, bf16[128,2048]{1,0:T(8,128)(2,1)S(1)}, u32[]{:S(2)}, u32[]{:S(2)}) %collective-permute-start.76) | collective-permute-done | bytes 524320 | tf_op jit(solution)/shard_map/ppermute | solution.py:89
  534.2 3.8 convolution_convert_fusion.4
  538.2 13.1 %reduce-scatter.9.cloned.1.call-done = bf16[512,768]{1,0:T(8,128)(2,1)} async-done(((bf16[2048,768]{1,0:T(8,128)(2,1)}), bf16[512,768]{1,0:T(8,128)(2,1)}) %reduce-scatter.9.cloned.1.call-update) | async-done | bytes 786448 | tf_op jit(solution)/shard_map/reduce_scatter | solution.py:982
  551.3 3.1 dynamic-slice_bitcast_fusion.1
  556.6 4.2 fusion.16
  565.8 2.8 collective-permute-done.82
  571.0 4.2 all-to-all-start.2
  580.4 6.5 %all-to-all-done.2 = bf16[8,64,768]{2,1,0:T(8,128)(2,1)} async-done(((bf16[8,64,768]{2,1,0:T(8,128)(2,1)}), bf16[8,64,768]{2,1,0:T(8,128)(2,1)}, u32[]{:S(2)}, u32[]{:S(2)}) %all-to-all-start.2) | async-done | bytes 786464 | tf_op jit(solution)/shard_map/all_to_all | solution.py:286
  586.9 4.2 all-to-all-start.3
  594.6 5.6 fusion.15
  600.3 5.3 all-to-all-done.3.dealt_ref
  (391 shorter events, 184.4 us)
Async XLA Ops:
  7.2 40.3 %collective-permute-start.4 = (bf16[64,2048]{1,0:T(8,128)(2,1)}, bf16[64,2048]{1,0:T(8,128)(2,1)}, u32[]{:S(2)}, u32[]{:S(2)}) collective-permute-start(bf16[64,2048]{1,0:T(8,128)(2,1)} %param.22), channel_id=1, source_target_pairs={{0,8},{8,0},{16,24},{24,16},{1,9},{9,1},{17,25},{25,17},{2,10},{10... | collective-permute-start | bytes 786440 | tf_op jit(solution)/shard_map/ppermute | solution.py:850
  10.3 37.8 %collective-permute-start.5 = (bf16[64,2048]{1,0:T(8,128)(2,1)}, bf16[64,2048]{1,0:T(8,128)(2,1)}, u32[]{:S(2)}, u32[]{:S(2)}) collective-permute-start(bf16[64,2048]{1,0:T(8,128)(2,1)} %param.22), channel_id=1, source_target_pairs={{0,16},{8,24},{16,0},{24,8},{1,17},{9,25},{17,1},{25,9},{2,18},{10... | collective-permute-start | bytes 786440 | tf_op jit(solution)/shard_map/ppermute | solution.py:850
  19.2 30.3 %all-to-all-start = ((bf16[8,64,768]{2,1,0:T(8,128)(2,1)}), bf16[8,64,768]{2,1,0:T(8,128)(2,1)S(1)}, u32[]{:S(2)}, u32[]{:S(2)}) async-start(bf16[8,64,768]{2,1,0:T(8,128)(2,1)} %shard_map.246), calls=%async_computation | async-start | bytes 1572864 | tf_op jit(solution)/shard_map/all_to_all | solution.py:286
  23.1 72.7 %all-gather.5.cloned.1.call-start = ((), (), s32[]{:S(2)}) async-start(), calls=%async_computation.8 | async-start | bytes 1966080 | tf_op jit(solution)/shard_map/all_gather | solution.py:878
  24.5 33.2 %collective-permute-start = (bf16[128,2048]{1,0:T(8,128)(2,1)S(1)}, bf16[128,2048]{1,0:T(8,128)(2,1)S(1)}, u32[]{:S(2)}, u32[]{:S(2)}) collective-permute-start(bf16[128,2048]{1,0:T(8,128)(2,1)S(1)} %get-tuple-element.242), channel_id=1, source_target_pairs={{0,2},{2,0},{1,3},{3,1},{4,6},{6,4},{5,7},{7,5},{8,10},{10,8},{9,1... | collective-permute-start | bytes 1572872 | tf_op jit(solution)/shard_map/ppermute | solution.py:89
  26.6 33.0 %collective-permute-start.2 = (bf16[128,2048]{1,0:T(8,128)(2,1)S(1)}, bf16[128,2048]{1,0:T(8,128)(2,1)S(1)}, u32[]{:S(2)}, u32[]{:S(2)}) collective-permute-start(bf16[128,2048]{1,0:T(8,128)(2,1)S(1)} %get-tuple-element.242), channel_id=1, source_target_pairs={{0,4},{4,0},{1,5},{5,1},{2,6},{6,2},{3,7},{7,3},{8,12},{12,8},{9,1... | collective-permute-start | bytes 1572872 | tf_op jit(solution)/shard_map/ppermute | solution.py:89
  60.8 22.3 %collective-permute-start.14 = (bf16[256,2048]{1,0:T(8,128)(2,1)}, bf16[256,2048]{1,0:T(8,128)(2,1)}, u32[]{:S(2)}, u32[]{:S(2)}) collective-permute-start(bf16[256,2048]{1,0:T(8,128)(2,1)} %copy-done.21), channel_id=1, source_target_pairs={{0,1},{1,0},{2,3},{3,2},{4,5},{5,4},{6,7},{7,6},{8,9},{9,8},{10,11... | collective-permute-start | bytes 3145736 | tf_op jit(solution)/shard_map/ppermute | solution.py:89
  68.2 22.8 %all-to-all-start.1 = ((bf16[8,64,1024]{2,1,0:T(8,128)(2,1)}), bf16[8,64,1024]{2,1,0:T(8,128)(2,1)}, u32[]{:S(2)}, u32[]{:S(2)}) async-start(bf16[8,64,1024]{2,1,0:T(8,128)(2,1)} %shard_map.247), calls=%async_computation.1 | async-start | bytes 2097152 | tf_op jit(solution)/shard_map/all_to_all | solution.py:286
  72.5 60.9 %all-gather.7.cloned.1.call-start = ((), (), s32[]{:S(2)}) async-start(), calls=%async_computation.9 | async-start | bytes 1966080 | tf_op jit(solution)/shard_map/all_gather | solution.py:854
  73.2 141.9 %all-gather.9.cloned.1.call-start = ((), (), s32[]{:S(2)}) async-start(), calls=%async_computation.10 | async-start | bytes 5242880 | tf_op jit(solution)/shard_map/all_gather | solution.py:887
  81.2 21.7 %collective-permute-start.29 = (bf16[4,1,64,2048]{3,2,1,0:T(8,128)(2,1)}, bf16[4,1,64,2048]{3,2,1,0:T(8,128)(2,1)}, u32[]{:S(2)}, u32[]{:S(2)}) collective-permute-start(bf16[4,1,64,2048]{3,2,1,0:T(8,128)(2,1)} %bitcast_dynamic-update-slice_fusion), channel_id=1, source_target_pairs={{0,1},{1,0},{2,3},{3,2},{4,5},{5,4},{6,7},{7,6},{8,9},{9,8},{10,11... | collective-permute-start | bytes 3145736 | tf_op jit(solution)/shard_map/ppermute | solution.py:89
  95.8 199.5 %all-gather.11.cloned.1.call-start = ((), (), s32[]{:S(2)}) async-start(), calls=%async_computation.11 | async-start | bytes 5242880 | tf_op jit(solution)/shard_map/all_gather | solution.py:888
  99.4 52.7 %collective-permute-start.23 = (bf16[128,2048]{1,0:T(8,128)(2,1)}, bf16[128,2048]{1,0:T(8,128)(2,1)}, u32[]{:S(2)}, u32[]{:S(2)}) collective-permute-start(bf16[128,2048]{1,0:T(8,128)(2,1)} %get-tuple-element.240), channel_id=1, source_target_pairs={{0,4},{4,0},{1,5},{5,1},{2,6},{6,2},{3,7},{7,3},{8,12},{12,8},{9,1... | collective-permute-start | bytes 1572872 | tf_op jit(solution)/shard_map/ppermute | solution.py:89
  100.9 51.2 %collective-permute-start.22 = (bf16[128,2048]{1,0:T(8,128)(2,1)}, bf16[128,2048]{1,0:T(8,128)(2,1)}, u32[]{:S(2)}, u32[]{:S(2)}) collective-permute-start(bf16[128,2048]{1,0:T(8,128)(2,1)} %get-tuple-element.239), channel_id=1, source_target_pairs={{0,2},{2,0},{1,3},{3,1},{4,6},{6,4},{5,7},{7,5},{8,10},{10,8},{9,1... | collective-permute-start | bytes 1572872 | tf_op jit(solution)/shard_map/ppermute | solution.py:89
  102.4 22.1 %collective-permute-start.24 = (bf16[128,2048]{1,0:T(8,128)(2,1)}, bf16[128,2048]{1,0:T(8,128)(2,1)}, u32[]{:S(2)}, u32[]{:S(2)}) collective-permute-start(bf16[128,2048]{1,0:T(8,128)(2,1)} %get-tuple-element.239), channel_id=1, source_target_pairs={{0,4},{4,0},{1,5},{5,1},{2,6},{6,2},{3,7},{7,3},{8,12},{12,8},{9,1... | collective-permute-start | bytes 1572872 | tf_op jit(solution)/shard_map/ppermute | solution.py:89
  102.9 23.1 %collective-permute-start.19 = (bf16[128,2048]{1,0:T(8,128)(2,1)S(1)}, bf16[128,2048]{1,0:T(8,128)(2,1)S(1)}, u32[]{:S(2)}, u32[]{:S(2)}) collective-permute-start(bf16[128,2048]{1,0:T(8,128)(2,1)S(1)} %collective-permute-done.12.others_5_), channel_id=1, source_target_pairs={{0,1},{1,0},{2,3},{3,2},{4,5},{5,4},{6,7},{7,6},{8,9},{9,8},{10,11... | collective-permute-start | bytes 1572872 | tf_op jit(solution)/shard_map/ppermute | solution.py:89
  102.9 25.3 %collective-permute-start.20 = (bf16[128,2048]{1,0:T(8,128)(2,1)}, bf16[128,2048]{1,0:T(8,128)(2,1)}, u32[]{:S(2)}, u32[]{:S(2)}) collective-permute-start(bf16[128,2048]{1,0:T(8,128)(2,1)} %copy-done.4), channel_id=1, source_target_pairs={{0,1},{1,0},{2,3},{3,2},{4,5},{5,4},{6,7},{7,6},{8,9},{9,8},{10,11... | collective-permute-start | bytes 1572872 | tf_op jit(solution)/shard_map/ppermute | solution.py:89
  124.5 46.8 %collective-permute-start.27 = (bf16[128,2048]{1,0:T(8,128)(2,1)}, bf16[128,2048]{1,0:T(8,128)(2,1)}, u32[]{:S(2)}, u32[]{:S(2)}) collective-permute-start(bf16[128,2048]{1,0:T(8,128)(2,1)} %collective-permute-done.21.others_8_), channel_id=1, source_target_pairs={{0,4},{4,0},{1,5},{5,1},{2,6},{6,2},{3,7},{7,3},{8,12},{12,8},{9,1... | collective-permute-start | bytes 1572872 | tf_op jit(solution)/shard_map/ppermute | solution.py:89
  126.8 44.6 %collective-permute-start.28 = (bf16[128,2048]{1,0:T(8,128)(2,1)}, bf16[128,2048]{1,0:T(8,128)(2,1)}, u32[]{:S(2)}, u32[]{:S(2)}) collective-permute-start(bf16[128,2048]{1,0:T(8,128)(2,1)} %collective-permute-done.24.others_11_), channel_id=1, source_target_pairs={{0,2},{2,0},{1,3},{3,1},{4,6},{6,4},{5,7},{7,5},{8,10},{10,8},{9,1... | collective-permute-start | bytes 1572872 | tf_op jit(solution)/shard_map/ppermute | solution.py:89
  177.0 23.0 %collective-permute-start.30 = (bf16[128,2048]{1,0:T(8,128)(2,1)S(1)}, bf16[128,2048]{1,0:T(8,128)(2,1)S(1)}, u32[]{:S(2)}, u32[]{:S(2)}) collective-permute-start(bf16[128,2048]{1,0:T(8,128)(2,1)S(1)} %get-tuple-element.209), channel_id=1, source_target_pairs={{0,4},{4,0},{1,5},{5,1},{2,6},{6,2},{3,7},{7,3},{8,12},{12,8},{9,1... | collective-permute-start | bytes 1572872 | tf_op jit(solution)/shard_map/ppermute | solution.py:89
  177.6 23.9 %collective-permute-start.35 = (bf16[128,2048]{1,0:T(8,128)(2,1)S(1)}, bf16[128,2048]{1,0:T(8,128)(2,1)S(1)}, u32[]{:S(2)}, u32[]{:S(2)}) collective-permute-start(bf16[128,2048]{1,0:T(8,128)(2,1)S(1)} %get-tuple-element.210), channel_id=1, source_target_pairs={{0,2},{2,0},{1,3},{3,1},{4,6},{6,4},{5,7},{7,5},{8,10},{10,8},{9,1... | collective-permute-start | bytes 1572872 | tf_op jit(solution)/shard_map/ppermute | solution.py:89
  190.7 21.1 %collective-permute-start.32 = (bf16[128,2048]{1,0:T(8,128)(2,1)S(1)}, bf16[128,2048]{1,0:T(8,128)(2,1)S(1)}, u32[]{:S(2)}, u32[]{:S(2)}) collective-permute-start(bf16[128,2048]{1,0:T(8,128)(2,1)S(1)} %get-tuple-element.213), channel_id=1, source_target_pairs={{0,2},{2,0},{1,3},{3,1},{4,6},{6,4},{5,7},{7,5},{8,10},{10,8},{9,1... | collective-permute-start | bytes 1572872 | tf_op jit(solution)/shard_map/ppermute | solution.py:89
  192.2 19.6 %collective-permute-start.34 = (bf16[128,2048]{1,0:T(8,128)(2,1)S(1)}, bf16[128,2048]{1,0:T(8,128)(2,1)S(1)}, u32[]{:S(2)}, u32[]{:S(2)}) collective-permute-start(bf16[128,2048]{1,0:T(8,128)(2,1)S(1)} %get-tuple-element.214), channel_id=1, source_target_pairs={{0,4},{4,0},{1,5},{5,1},{2,6},{6,2},{3,7},{7,3},{8,12},{12,8},{9,1... | collective-permute-start | bytes 1572872 | tf_op jit(solution)/shard_map/ppermute | solution.py:89
  215.1 46.3 %collective-permute-start.39 = (bf16[2048,1024]{1,0:T(8,128)(2,1)}, bf16[2048,1024]{1,0:T(8,128)(2,1)}, u32[]{:S(2)}, u32[]{:S(2)}) collective-permute-start(bf16[2048,1024]{1,0:T(8,128)(2,1)} %all-gather.9.cloned.1.call-done.mine_ref.up_mine_ref), channel_id=1, source_target_pairs={{0,1},{1,0},{2,3},{3,2},{4,5},{5,4},{6,7},{7,6},{8,9},{9,8},{10,11... | collective-permute-start | bytes 12582920 | tf_op jit(solution)/shard_map/ppermute | solution.py:89
  215.2 189.3 %reduce-scatter.5.cloned.1.call-start = ((), (), s32[]{:S(2)}) async-start(), calls=%async_computation.12 | async-start | bytes 5242880 | tf_op jit(solution)/shard_map/reduce_scatter | solution.py:930
  218.2 20.2 %collective-permute-start.40 = (bf16[128,2048]{1,0:T(8,128)(2,1)}, bf16[128,2048]{1,0:T(8,128)(2,1)}, u32[]{:S(2)}, u32[]{:S(2)}) collective-permute-start(bf16[128,2048]{1,0:T(8,128)(2,1)} %get-tuple-element.238), channel_id=1, source_target_pairs={{0,2},{2,0},{1,3},{3,1},{4,6},{6,4},{5,7},{7,5},{8,10},{10,8},{9,1... | collective-permute-start | bytes 1572872 | tf_op jit(solution)/shard_map/ppermute | solution.py:89
  219.6 19.8 %collective-permute-start.43 = (bf16[128,2048]{1,0:T(8,128)(2,1)}, bf16[128,2048]{1,0:T(8,128)(2,1)}, u32[]{:S(2)}, u32[]{:S(2)}) collective-permute-start(bf16[128,2048]{1,0:T(8,128)(2,1)} %get-tuple-element.237), channel_id=1, source_target_pairs={{0,4},{4,0},{1,5},{5,1},{2,6},{6,2},{3,7},{7,3},{8,12},{12,8},{9,1... | collective-permute-start | bytes 1572872 | tf_op jit(solution)/shard_map/ppermute | solution.py:89
  238.4 23.1 %collective-permute-start.44 = (bf16[128,2048]{1,0:T(8,128)(2,1)}, bf16[128,2048]{1,0:T(8,128)(2,1)}, u32[]{:S(2)}, u32[]{:S(2)}) collective-permute-start(bf16[128,2048]{1,0:T(8,128)(2,1)} %collective-permute-done.40.others_1_), channel_id=1, source_target_pairs={{0,4},{4,0},{1,5},{5,1},{2,6},{6,2},{3,7},{7,3},{8,12},{12,8},{9,1... | collective-permute-start | bytes 1572872 | tf_op jit(solution)/shard_map/ppermute | solution.py:89
  239.5 22.0 %collective-permute-start.45 = (bf16[128,2048]{1,0:T(8,128)(2,1)}, bf16[128,2048]{1,0:T(8,128)(2,1)}, u32[]{:S(2)}, u32[]{:S(2)}) collective-permute-start(bf16[128,2048]{1,0:T(8,128)(2,1)} %collective-permute-done.43.others_4_), channel_id=1, source_target_pairs={{0,2},{2,0},{1,3},{3,1},{4,6},{6,4},{5,7},{7,5},{8,10},{10,8},{9,1... | collective-permute-start | bytes 1572872 | tf_op jit(solution)/shard_map/ppermute | solution.py:89
  308.7 171.8 %reduce-scatter.7.cloned.1.call-start = ((), (), s32[]{:S(2)}) async-start(), calls=%async_computation.13 | async-start | bytes 5242880 | tf_op jit(solution)/shard_map/reduce_scatter | solution.py:956
  340.5 22.9 %collective-permute-start.49 = (bf16[128,2048]{1,0:T(8,128)(2,1)S(1)}, bf16[128,2048]{1,0:T(8,128)(2,1)S(1)}, u32[]{:S(2)}, u32[]{:S(2)}) collective-permute-start(bf16[128,2048]{1,0:T(8,128)(2,1)S(1)} %get-tuple-element.206), channel_id=1, source_target_pairs={{0,4},{4,0},{1,5},{5,1},{2,6},{6,2},{3,7},{7,3},{8,12},{12,8},{9,1... | collective-permute-start | bytes 1572872 | tf_op jit(solution)/shard_map/ppermute | solution.py:89
  341.7 22.3 %collective-permute-start.50 = (bf16[128,2048]{1,0:T(8,128)(2,1)S(1)}, bf16[128,2048]{1,0:T(8,128)(2,1)S(1)}, u32[]{:S(2)}, u32[]{:S(2)}) collective-permute-start(bf16[128,2048]{1,0:T(8,128)(2,1)S(1)} %get-tuple-element.205), channel_id=1, source_target_pairs={{0,2},{2,0},{1,3},{3,1},{4,6},{6,4},{5,7},{7,5},{8,10},{10,8},{9,1... | collective-permute-start | bytes 1572872 | tf_op jit(solution)/shard_map/ppermute | solution.py:89
  371.5 24.6 %collective-permute-start.57 = (bf16[2048,1024]{1,0:T(8,128)(2,1)S(1)}, bf16[2048,1024]{1,0:T(8,128)(2,1)S(1)}, u32[]{:S(2)}, u32[]{:S(2)}) collective-permute-start(bf16[2048,1024]{1,0:T(8,128)(2,1)S(1)} %convolution_convert_fusion.1), channel_id=1, source_target_pairs={{0,1},{1,0},{2,3},{3,2},{4,5},{5,4},{6,7},{7,6},{8,9},{9,8},{10,11... | collective-permute-start | bytes 12582920 | tf_op jit(solution)/shard_map/ppermute | solution.py:89
  404.5 146.8 %reduce-scatter.9.cloned.1.call-start = ((), (), s32[]{:S(2)}) async-start(), calls=%async_computation.14 | async-start | bytes 3932160 | tf_op jit(solution)/shard_map/reduce_scatter | solution.py:982
  406.9 24.0 %collective-permute-start.59 = (bf16[128,2048]{1,0:T(8,128)(2,1)S(1)}, bf16[128,2048]{1,0:T(8,128)(2,1)S(1)}, u32[]{:S(2)}, u32[]{:S(2)}) collective-permute-start(bf16[128,2048]{1,0:T(8,128)(2,1)S(1)} %get-tuple-element.235), channel_id=1, source_target_pairs={{0,2},{2,0},{1,3},{3,1},{4,6},{6,4},{5,7},{7,5},{8,10},{10,8},{9,1... | collective-permute-start | bytes 1572872 | tf_op jit(solution)/shard_map/ppermute | solution.py:89
  408.1 23.8 %collective-permute-start.60 = (bf16[128,2048]{1,0:T(8,128)(2,1)S(1)}, bf16[128,2048]{1,0:T(8,128)(2,1)S(1)}, u32[]{:S(2)}, u32[]{:S(2)}) collective-permute-start(bf16[128,2048]{1,0:T(8,128)(2,1)S(1)} %get-tuple-element.236), channel_id=1, source_target_pairs={{0,4},{4,0},{1,5},{5,1},{2,6},{6,2},{3,7},{7,3},{8,12},{12,8},{9,1... | collective-permute-start | bytes 1572872 | tf_op jit(solution)/shard_map/ppermute | solution.py:89
  419.7 20.8 %collective-permute-start.62 = (bf16[128,2048]{1,0:T(8,128)(2,1)S(1)}, bf16[128,2048]{1,0:T(8,128)(2,1)S(1)}, u32[]{:S(2)}, u32[]{:S(2)}) collective-permute-start(bf16[128,2048]{1,0:T(8,128)(2,1)S(1)} %collective-permute-done.58.others_1_), channel_id=1, source_target_pairs={{0,4},{4,0},{1,5},{5,1},{2,6},{6,2},{3,7},{7,3},{8,12},{12,8},{9,1... | collective-permute-start | bytes 1572872 | tf_op jit(solution)/shard_map/ppermute | solution.py:89
  420.9 19.6 %collective-permute-start.63 = (bf16[128,2048]{1,0:T(8,128)(2,1)S(1)}, bf16[128,2048]{1,0:T(8,128)(2,1)S(1)}, u32[]{:S(2)}, u32[]{:S(2)}) collective-permute-start(bf16[128,2048]{1,0:T(8,128)(2,1)S(1)} %collective-permute-done.61.others_4_), channel_id=1, source_target_pairs={{0,2},{2,0},{1,3},{3,1},{4,6},{6,4},{5,7},{7,5},{8,10},{10,8},{9,1... | collective-permute-start | bytes 1572872 | tf_op jit(solution)/shard_map/ppermute | solution.py:89
  447.3 33.2 %collective-permute-start.69 = (bf16[128,2048]{1,0:T(8,128)(2,1)S(1)}, bf16[128,2048]{1,0:T(8,128)(2,1)S(1)}, u32[]{:S(2)}, u32[]{:S(2)}) collective-permute-start(bf16[128,2048]{1,0:T(8,128)(2,1)S(1)} %get-tuple-element.202), channel_id=1, source_target_pairs={{0,4},{4,0},{1,5},{5,1},{2,6},{6,2},{3,7},{7,3},{8,12},{12,8},{9,1... | collective-permute-start | bytes 1572872 | tf_op jit(solution)/shard_map/ppermute | solution.py:89
  448.5 32.0 %collective-permute-start.70 = (bf16[128,2048]{1,0:T(8,128)(2,1)S(1)}, bf16[128,2048]{1,0:T(8,128)(2,1)S(1)}, u32[]{:S(2)}, u32[]{:S(2)}) collective-permute-start(bf16[128,2048]{1,0:T(8,128)(2,1)S(1)} %get-tuple-element.201), channel_id=1, source_target_pairs={{0,2},{2,0},{1,3},{3,1},{4,6},{6,4},{5,7},{7,5},{8,10},{10,8},{9,1... | collective-permute-start | bytes 1572872 | tf_op jit(solution)/shard_map/ppermute | solution.py:89
  449.4 31.1 %collective-permute-start.71 = (bf16[128,2048]{1,0:T(8,128)(2,1)S(1)}, bf16[128,2048]{1,0:T(8,128)(2,1)S(1)}, u32[]{:S(2)}, u32[]{:S(2)}) collective-permute-start(bf16[128,2048]{1,0:T(8,128)(2,1)S(1)} %get-tuple-element.200), channel_id=1, source_target_pairs={{0,4},{4,0},{1,5},{5,1},{2,6},{6,2},{3,7},{7,3},{8,12},{12,8},{9,1... | collective-permute-start | bytes 1572872 | tf_op jit(solution)/shard_map/ppermute | solution.py:89
  450.2 30.3 %collective-permute-start.72 = (bf16[128,2048]{1,0:T(8,128)(2,1)S(1)}, bf16[128,2048]{1,0:T(8,128)(2,1)S(1)}, u32[]{:S(2)}, u32[]{:S(2)}) collective-permute-start(bf16[128,2048]{1,0:T(8,128)(2,1)S(1)} %get-tuple-element.199), channel_id=1, source_target_pairs={{0,2},{2,0},{1,3},{3,1},{4,6},{6,4},{5,7},{7,5},{8,10},{10,8},{9,1... | collective-permute-start | bytes 1572872 | tf_op jit(solution)/shard_map/ppermute | solution.py:89
  519.5 34.9 %collective-permute-start.75 = (bf16[128,2048]{1,0:T(8,128)(2,1)}, bf16[128,2048]{1,0:T(8,128)(2,1)}, u32[]{:S(2)}, u32[]{:S(2)}) collective-permute-start(bf16[128,2048]{1,0:T(8,128)(2,1)} %slice.339), channel_id=1, source_target_pairs={{0,4},{4,0},{1,5},{5,1},{2,6},{6,2},{3,7},{7,3},{8,12},{12,8},{9,1... | collective-permute-start | bytes 1572872 | tf_op jit(solution)/shard_map/ppermute | solution.py:89
  521.3 33.2 %collective-permute-start.80 = (bf16[128,2048]{1,0:T(8,128)(2,1)}, bf16[128,2048]{1,0:T(8,128)(2,1)}, u32[]{:S(2)}, u32[]{:S(2)}) collective-permute-start(bf16[128,2048]{1,0:T(8,128)(2,1)} %slice.345), channel_id=1, source_target_pairs={{0,2},{2,0},{1,3},{3,1},{4,6},{6,4},{5,7},{7,5},{8,10},{10,8},{9,1... | collective-permute-start | bytes 1572872 | tf_op jit(solution)/shard_map/ppermute | solution.py:89
  530.4 24.0 %collective-permute-start.77 = (bf16[128,2048]{1,0:T(8,128)(2,1)}, bf16[128,2048]{1,0:T(8,128)(2,1)}, u32[]{:S(2)}, u32[]{:S(2)}) collective-permute-start(bf16[128,2048]{1,0:T(8,128)(2,1)} %add_convert_fusion.8), channel_id=1, source_target_pairs={{0,2},{2,0},{1,3},{3,1},{4,6},{6,4},{5,7},{7,5},{8,10},{10,8},{9,1... | collective-permute-start | bytes 1572872 | tf_op jit(solution)/shard_map/ppermute | solution.py:89
  533.3 21.2 %collective-permute-start.79 = (bf16[128,2048]{1,0:T(8,128)(2,1)}, bf16[128,2048]{1,0:T(8,128)(2,1)}, u32[]{:S(2)}, u32[]{:S(2)}) collective-permute-start(bf16[128,2048]{1,0:T(8,128)(2,1)} %add_convert_fusion.7), channel_id=1, source_target_pairs={{0,4},{4,0},{1,5},{5,1},{2,6},{6,2},{3,7},{7,3},{8,12},{12,8},{9,1... | collective-permute-start | bytes 1572872 | tf_op jit(solution)/shard_map/ppermute | solution.py:89
  554.4 20.9 %collective-permute-start.86 = (bf16[4,64,2048]{2,1,0:T(8,128)(2,1)}, bf16[4,64,2048]{2,1,0:T(8,128)(2,1)}, u32[]{:S(2)}, u32[]{:S(2)}) collective-permute-start(bf16[4,64,2048]{2,1,0:T(8,128)(2,1)} %get-tuple-element.216), channel_id=1, source_target_pairs={{0,1},{1,0},{2,3},{3,2},{4,5},{5,4},{6,7},{7,6},{8,9},{9,8},{10,11... | collective-permute-start | bytes 3145736 | tf_op jit(solution)/shard_map/ppermute | solution.py:89
  575.3 37.5 %reduce-scatter.11.cloned.1.call-start = ((), (), s32[]{:S(2)}) async-start(), calls=%async_computation.15 | async-start | bytes 1310720 | tf_op jit(solution)/shard_map/reduce_scatter | solution.py:223
  (102 other events, 1294.4 us)
Sparse Core Ops, SparseCore 0:
  61.0 34.8 all-gather.4
  97.4 35.9 all-gather.6
  134.9 79.6 all-gather.8
  216.0 79.2 all-gather.10
  308.8 74.7 reduce-scatter.4
  404.6 74.0 reduce-scatter.6
  492.4 58.8 reduce-scatter.8
  578.4 30.4 reduce-scatter.10

commit v3 on v2

--- a/solution.py
+++ b/solution.py
@@ -851,28 +851,17 @@
             for d in range(1, planes)
         ]
     input_first = swap_plane(deal(input_weight, attention_columns()))
+    input_first, output_blocks, levels, starts = lax.optimization_barrier(
+        (input_first, output_blocks, levels, starts)
+    )
     weights = [lax.all_gather(input_first[:, : 3 * HD], "z", axis=0, tiled=True)]
     token_values = tokens.astype(f32)
     mixer_hidden, mixer_normed, mixer_scale = normalize(token_values, mixer_gain, mixer_bias)
     mixer_gate, mixer_probs, mixer_chosen = route(mixer_hidden, mixer_router, head_level)
     mixer_pieces = gather_eight(mixer_hidden.astype(bf16))
-    (
-        mixer_pieces[1:5],
-        input_second,
-        output_blocks,
-        up_weight,
-        cotangent_sent,
-        levels,
-        starts,
-    ) = lax.optimization_barrier(
-        (
-            mixer_pieces[1:5],
-            input_first[:, 3 * HD :],
-            output_blocks,
-            up_weight,
-            cotangent,
-            levels,
-            starts,
+    mixer_pieces[1:5], input_second, up_weight, cotangent_sent, weights[0] = (
+        lax.optimization_barrier(
+            (mixer_pieces[1:5], input_first[:, 3 * HD :], up_weight, cotangent, weights[0])
         )
     )
     weights.append(lax.all_gather(input_second, "z", axis=0, tiled=True))

time: 629 us -> 619 us (0.984)
    all_gather x1, waiting for transfers between devices: 4.81 us -> 12.8 us  [local(): weights.append(lax.all_gather(input_second, 'z', axis=0, tiled=True))]
    ppermute x3, waiting for transfers between devices: 7.11 us -> 0.01 us  [local(): lax.ppermute(output_weight, 'z', [(i, i ^ d) for i in range(planes)])]
    ppermute x73, waiting for transfers between devices: 159 us -> 153 us  [flip(): return lax.ppermute(values, axis, [(0, 1), (1, 0)])]
  transfers between devices with their start and end apart: 99 -> 99, of which waited for: 41 -> 42; matrix products, arithmetic and copies ran while one was open for 20% -> 20% of each run, Pallas kernels for 22% -> 23%
where the time goes in v3:
time: 619 us; the launch traced here: 612 us
  waiting for transfers between devices  217 us (35%)
  Pallas kernels  140 us (23%)
  starting transfers between devices  96.6 us (16%)
  matrix products  65.2 us (11%)
  other arithmetic  44.6 us (7%)
  local copies, waits for them, and re-layouts  32.8 us (5%)
  between operations  15.9 us (3%)
    ppermute x73, waiting for transfers between devices, flip(): return lax.ppermute(values, axis, [(0, 1), (1, 0)])  153 us
    ppermute x73, starting transfers between devices, flip(): return lax.ppermute(values, axis, [(0, 1), (1, 0)])  58.6 us
    dot_general x6, matrix products, contract_first(): lax.dot_general(left, right, (((0,), (0,)), ((), ())), preferred_element_...  49.5 us
    pallas_call x2, Pallas kernels, attend(): pl.pallas_call(body, grid_spec=pltpu.PrefetchScalarGridSpec(num_scalar_pr...  34.2 us
    pallas_call x1, Pallas kernels, attend_back(): pl.pallas_call(body, grid_spec=pltpu.PrefetchScalarGridSpec(num_scalar_pr...  29.3 us
    pallas_call x1, Pallas kernels, lower(): pl.pallas_call(functools.partial(lower_kernel, half), grid=(first + secon...  27.6 us
    pallas_call x1, Pallas kernels, lift(): pl.pallas_call(functools.partial(lift_kernel, half), grid=(steps,), in_sp...  19.8 us
    all_to_all x4, waiting for transfers between devices, swap_plane(): return lax.all_to_all(values, PLANE, 0, 0, tiled=True)  17.2 us
  transfers between devices with their start and end apart: 99, of which 42 were waited for; matrix products, arithmetic and copies ran while one was open for 20% of the time, Pallas kernels for 23%

profile of v3, /device:TPU:0, one launch (start us, length us, event | category | flops | bytes accessed | tf_op | source)
XLA Modules:
  0.0 612.1 jit_solution(1511697589699205245)
XLA Ops:
  7.2 3.1 collective-permute-start.4
  19.3 3.7 all-to-all-start
  25.7 9.1 %collective-permute-done.10 = s32[1,1024]{1,0:T(1,128)S(1)} collective-permute-done((s32[1,1024]{1,0:T(1,128)S(1)}, s32[1,1024]{1,0:T(1,128)S(1)}, u32[]{:S(2)}, u32[]{:S(2)}) %collective-permute-start.10) | collective-permute-done | bytes 4128 | tf_op jit(solution)/shard_map/ppermute | solution.py:89
  44.5 3.1 fusion.47
  47.6 7.7 %collective-permute-done.others_1_ = bf16[128,2048]{1,0:T(8,128)(2,1)S(1)} collective-permute-done((bf16[128,2048]{1,0:T(8,128)(2,1)S(1)}, bf16[128,2048]{1,0:T(8,128)(2,1)S(1)}, u32[]{:S(2)}, u32[]{:S(2)}) %collective-permute-start) | collective-permute-done | bytes 524320 | tf_op jit(solution)/shard_map/ppermute | solution.py:89
  55.6 9.5 %collective-permute-done.1.others_2_ = bf16[128,2048]{1,0:T(8,128)(2,1)S(1)} collective-permute-done((bf16[128,2048]{1,0:T(8,128)(2,1)S(1)}, bf16[128,2048]{1,0:T(8,128)(2,1)S(1)}, u32[]{:S(2)}, u32[]{:S(2)}) %collective-permute-start.1) | collective-permute-done | bytes 524320 | tf_op jit(solution)/shard_map/ppermute | solution.py:89
  65.1 3.0 collective-permute-done.3.others_4_
  68.6 5.6 all-gather.5.cloned.1.call-done.weight_ref.weight_0
  80.8 4.2 all-to-all-start.1
  94.2 5.3 all-to-all-done.1
  99.5 12.8 %all-gather.7.cloned.1.call-done.weight_ref.weight_1 = bf16[2048,384]{1,0:T(8,128)(2,1)} async-done(((bf16[512,384]{1,0:T(8,128)(2,1)}), bf16[2048,384]{1,0:T(8,128)(2,1)}) %all-gather.7.cloned.1.call-update) | async-done | bytes 1572880 | tf_op jit(solution)/shard_map/all_gather | solution.py:867
  122.1 16.9 %shard_map.248 = (bf16[2048,384]{1,0:T(8,128)(2,1)}, bf16[2,2,512,128]{3,2,1,0:T(8,128)(2,1)S(1)}, bf16[2048,2048]{1,0:T(8,128)(2,1)}) custom-call(s32[2]{0:T(128)S(1)} %pad_add_fusion.2.place_ref, s32[2048,1]{1,0:T(8,128)} %copy.38.start_ref, f32[2,2,512,1]{3,2,1,0:T(8,128)} %reshape.275.level_ref, f32[1024,128]{1,0:T(8,128)S(1)} %get-tuple-element.273.cos_ref, ...), custom_call_target="tpu_custom_call" | custom-call | tf_op jit(solution)/shard_map/pallas_call | solution.py:467
  142.9 17.2 %shard_map.249 = (bf16[2048,384]{1,0:T(8,128)(2,1)}, bf16[2,2,512,128]{3,2,1,0:T(8,128)(2,1)S(1)}, bf16[2048,2048]{1,0:T(8,128)(2,1)}) custom-call(s32[2]{0:T(128)S(1)} %pad_add_fusion.2.place_ref, s32[2048,1]{1,0:T(8,128)} %copy.38.start_ref, f32[2,2,512,1]{3,2,1,0:T(8,128)} %reshape.275.level_ref, f32[1024,128]{1,0:T(8,128)S(1)} %get-tuple-element.273.cos_ref, ...), custom_call_target="tpu_custom_call" | custom-call | tf_op jit(solution)/shard_map/pallas_call | solution.py:467
  169.1 10.6 %collective-permute-done.31 = bf16[128,2048]{1,0:T(8,128)(2,1)S(1)} collective-permute-done((bf16[128,2048]{1,0:T(8,128)(2,1)S(1)}, bf16[128,2048]{1,0:T(8,128)(2,1)S(1)}, u32[]{:S(2)}, u32[]{:S(2)}) %collective-permute-start.31) | collective-permute-done | bytes 524320 | tf_op jit(solution)/shard_map/ppermute | solution.py:89
  183.3 7.7 %collective-permute-done.30 = bf16[128,2048]{1,0:T(8,128)(2,1)S(1)} collective-permute-done((bf16[128,2048]{1,0:T(8,128)(2,1)S(1)}, bf16[128,2048]{1,0:T(8,128)(2,1)S(1)}, u32[]{:S(2)}, u32[]{:S(2)}) %collective-permute-start.30) | collective-permute-done | bytes 524320 | tf_op jit(solution)/shard_map/ppermute | solution.py:89
  191.8 10.2 %collective-permute-done.32 = bf16[128,2048]{1,0:T(8,128)(2,1)S(1)} collective-permute-done((bf16[128,2048]{1,0:T(8,128)(2,1)S(1)}, bf16[128,2048]{1,0:T(8,128)(2,1)S(1)}, u32[]{:S(2)}, u32[]{:S(2)}) %collective-permute-start.32) | collective-permute-done | bytes 524320 | tf_op jit(solution)/shard_map/ppermute | solution.py:89
  213.3 10.8 %collective-permute-done.38 = f32[2,128]{1,0:T(2,128)S(1)} collective-permute-done((f32[2,128]{1,0:T(2,128)S(1)}, f32[2,128]{1,0:T(2,128)S(1)}, u32[]{:S(2)}, u32[]{:S(2)}) %collective-permute-start.38) | collective-permute-done | bytes 1056 | tf_op jit(solution)/shard_map/ppermute | solution.py:146
  233.9 6.9 %collective-permute-done.41.others_2_ = bf16[128,2048]{1,0:T(8,128)(2,1)} collective-permute-done((bf16[128,2048]{1,0:T(8,128)(2,1)}, bf16[128,2048]{1,0:T(8,128)(2,1)}, u32[]{:S(2)}, u32[]{:S(2)}) %collective-permute-start.41) | collective-permute-done | bytes 524320 | tf_op jit(solution)/shard_map/ppermute | solution.py:89
  242.8 8.9 %collective-permute-done.44.others_5_ = bf16[128,2048]{1,0:T(8,128)(2,1)} collective-permute-done((bf16[128,2048]{1,0:T(8,128)(2,1)}, bf16[128,2048]{1,0:T(8,128)(2,1)}, u32[]{:S(2)}, u32[]{:S(2)}) %collective-permute-start.44) | collective-permute-done | bytes 524320 | tf_op jit(solution)/shard_map/ppermute | solution.py:89
  251.7 19.8 %shard_map.250 = (f32[1024,2048]{1,0:T(8,128)}, bf16[1024,2048]{1,0:T(8,128)(2,1)}, bf16[1024,2048]{1,0:T(8,128)(2,1)}, bf16[1024,2048]{1,0:T(8,128)(2,1)}, bf16[1024,2048]{1,0:T(8,128)(2,1)}) custom-call(f32[1024,1]{1,0:T(8,128)} %copy.42.gate_ref, s32[1024,1]{1,0:T(8,128)} %copy.43.limit_ref, s32[1,2048]{1,0:T(1,128)} %bitcast.122, ...), custom_call_target="tpu_custom_call" | custom-call | tf_op jit(solution)/shard_map/pallas_call | solution.py:620
  271.5 9.3 %convolution_convert_fusion.2 = bf16[1024,2048]{1,0:T(8,128)(2,1)} fusion(bf16[1024,2048]{1,0:T(8,128)(2,1)} %get-tuple-element.124.grad_ref, bf16[1024,2048]{1,0:T(8,128)(2,1)} %get-tuple-element.129.activated_ref), kind=kOutput, calls=%fused_computation.5 | convolution fusion | flops 4297064448 | bytes 10485760 | tf_op jit(solution)/shard_map/dot_general | solution.py:85
  280.9 3.6 all-gather.11.cloned.1.call-done.down_mine_ref.mine_ref
  284.5 3.9 collective-permute-done.56
  288.4 10.6 %add_convert_fusion.1 = bf16[1024,2048]{1,0:T(8,128)(2,1)} fusion(bf16[1024,2048]{1,0:T(8,128)(2,1)} %collective-permute-done.56, bf16[1024,2048]{1,0:T(8,128)(2,1)} %get-tuple-element.124.grad_ref, bf16[1024,2048]{1,0:T(8,128)(2,1)} %get-tuple-element.129.activated_ref), kind=kOutput, calls=%fused_computation.1 | convolution fusion | flops 4301258752 | bytes 14680064 | tf_op jit(solution)/shard_map/dot_general | solution.py:85
  299.1 27.6 %shard_map.251 = (bf16[1024,2048]{1,0:T(8,128)(2,1)}, bf16[1024,2048]{1,0:T(8,128)(2,1)}) custom-call(bf16[1024,2048]{1,0:T(8,128)(2,1)} %get-tuple-element.124.grad_ref, f32[1024,2048]{1,0:T(8,128)} %get-tuple-element.125.rectified_ref, bf16[1024,2048]{1,0:T(8,128)(2,1)} %all-gather.11.cloned.1.call-done.down_mine_ref.mine_ref, ...), custom_call_target="tpu_custom_call" | custom-call | tf_op jit(solution)/shard_map/pallas_call | solution.py:732
  332.6 14.9 %shard_map.252 = (bf16[1024,2048]{1,0:T(8,128)(2,1)}, f32[1024,1]{1,0:T(8,128)}) custom-call(bf16[1024,2048]{1,0:T(8,128)(2,1)} %get-tuple-element.129.activated_ref, bf16[1024,2048]{1,0:T(8,128)(2,1)} %get-tuple-element.130.upstream_ref, bf16[1024,2048]{1,0:T(8,128)(2,1)} %all-gather.11.cloned.1.call-done.down_mine_ref.mine_ref, ...), custom_call_target="tpu_custom_call" | custom-call | tf_op jit(solution)/shard_map/pallas_call | solution.py:779
  347.5 6.2 %collective-permute-done.49 = bf16[128,2048]{1,0:T(8,128)(2,1)S(1)} collective-permute-done((bf16[128,2048]{1,0:T(8,128)(2,1)S(1)}, bf16[128,2048]{1,0:T(8,128)(2,1)S(1)}, u32[]{:S(2)}, u32[]{:S(2)}) %collective-permute-start.49) | collective-permute-done | bytes 524320 | tf_op jit(solution)/shard_map/ppermute | solution.py:89
  354.6 7.6 %convolution_convert_fusion.1 = bf16[2048,1024]{1,0:T(8,128)(2,1)S(1)} fusion(bf16[1024,2048]{1,0:T(8,128)(2,1)} %get-tuple-element.140, bf16[1024,2048]{1,0:T(8,128)(2,1)} %get-tuple-element.141), kind=kOutput, calls=%fused_computation.4 | convolution fusion | flops 4297064448 | bytes 10485760 | tf_op jit(solution)/shard_map/dot_general | solution.py:85
  369.3 10.8 %collective-permute-done.51 = bf16[128,2048]{1,0:T(8,128)(2,1)S(1)} collective-permute-done((bf16[128,2048]{1,0:T(8,128)(2,1)S(1)}, bf16[128,2048]{1,0:T(8,128)(2,1)S(1)}, u32[]{:S(2)}, u32[]{:S(2)}) %collective-permute-start.51) | collective-permute-done | bytes 524320 | tf_op jit(solution)/shard_map/ppermute | solution.py:89
  388.0 6.5 %add_convert_fusion = bf16[2048,1024]{1,0:T(8,128)(2,1)} fusion(bf16[2048,1024]{1,0:T(8,128)(2,1)S(1)} %collective-permute-done.57, bf16[1024,2048]{1,0:T(8,128)(2,1)S(1)} %copy-done.51, bf16[1024,2048]{1,0:T(8,128)(2,1)S(1)} %copy-done.52), kind=kOutput, calls=%fused_computation | convolution fusion | flops 4301258752 | bytes 14680064 | tf_op jit(solution)/shard_map/dot_general | solution.py:85
  399.0 10.8 %collective-permute-done.58.others_1_ = bf16[128,2048]{1,0:T(8,128)(2,1)S(1)} collective-permute-done((bf16[128,2048]{1,0:T(8,128)(2,1)S(1)}, bf16[128,2048]{1,0:T(8,128)(2,1)S(1)}, u32[]{:S(2)}, u32[]{:S(2)}) %collective-permute-start.58) | collective-permute-done | bytes 524320 | tf_op jit(solution)/shard_map/ppermute | solution.py:89
  412.1 8.9 %collective-permute-done.59.others_2_ = bf16[128,2048]{1,0:T(8,128)(2,1)S(1)} collective-permute-done((bf16[128,2048]{1,0:T(8,128)(2,1)S(1)}, bf16[128,2048]{1,0:T(8,128)(2,1)S(1)}, u32[]{:S(2)}, u32[]{:S(2)}) %collective-permute-start.59) | collective-permute-done | bytes 524320 | tf_op jit(solution)/shard_map/ppermute | solution.py:89
  422.2 8.4 %collective-permute-done.62.others_5_ = bf16[128,2048]{1,0:T(8,128)(2,1)S(1)} collective-permute-done((bf16[128,2048]{1,0:T(8,128)(2,1)S(1)}, bf16[128,2048]{1,0:T(8,128)(2,1)S(1)}, u32[]{:S(2)}, u32[]{:S(2)}) %collective-permute-start.62) | collective-permute-done | bytes 524320 | tf_op jit(solution)/shard_map/ppermute | solution.py:89
  430.6 4.3 shard_map.253
  441.5 29.3 %shard_map.254 = (bf16[2,2,512,768]{3,2,1,0:T(8,128)(2,1)}, bf16[2,2,512,2048]{3,2,1,0:T(8,128)(2,1)}) custom-call(s32[2]{0:T(128)S(1)} %pad_add_fusion.2.place_ref, s32[2048,1]{1,0:T(8,128)S(1)} %copy-done.2, f32[2,2,512,1]{3,2,1,0:T(8,128)S(1)} %copy-done.3, f32[1024,128]{1,0:T(8,128)S(1)} %get-tuple-element.273.cos_ref, ...), custom_call_target="tpu_custom_call" | custom-call | tf_op jit(solution)/shard_map/pallas_call | solution.py:511
  470.9 11.7 %convolution_convert_fusion.3 = bf16[2048,768]{1,0:T(8,128)(2,1)} fusion(bf16[2048,2048]{1,0:T(8,128)(2,1)} %get-tuple-element.160, bf16[2048,768]{1,0:T(8,128)(2,1)} %bitcast.148), kind=kOutput, calls=%fused_computation.6 | convolution fusion | flops 6444023808 | bytes 14680064 | tf_op jit(solution)/shard_map/dot_general | solution.py:85
  492.6 4.1 add_convert_fusion.3
  496.7 5.6 collective-permute-done.73
  512.7 7.4 %collective-permute-done.76 = bf16[128,2048]{1,0:T(8,128)(2,1)S(1)} collective-permute-done((bf16[128,2048]{1,0:T(8,128)(2,1)S(1)}, bf16[128,2048]{1,0:T(8,128)(2,1)S(1)}, u32[]{:S(2)}, u32[]{:S(2)}) %collective-permute-start.76) | collective-permute-done | bytes 524320 | tf_op jit(solution)/shard_map/ppermute | solution.py:89
  524.8 3.8 convolution_convert_fusion.4
  528.8 12.8 %reduce-scatter.9.cloned.1.call-done = bf16[512,768]{1,0:T(8,128)(2,1)} async-done(((bf16[2048,768]{1,0:T(8,128)(2,1)}), bf16[512,768]{1,0:T(8,128)(2,1)}) %reduce-scatter.9.cloned.1.call-update) | async-done | bytes 786448 | tf_op jit(solution)/shard_map/reduce_scatter | solution.py:971
  541.6 3.1 dynamic-slice_bitcast_fusion.1
  546.9 4.2 fusion.16
  561.4 4.2 all-to-all-start.2
  570.7 6.5 %all-to-all-done.2 = bf16[8,64,768]{2,1,0:T(8,128)(2,1)} async-done(((bf16[8,64,768]{2,1,0:T(8,128)(2,1)}), bf16[8,64,768]{2,1,0:T(8,128)(2,1)}, u32[]{:S(2)}, u32[]{:S(2)}) %all-to-all-start.2) | async-done | bytes 786464 | tf_op jit(solution)/shard_map/all_to_all | solution.py:286
  577.2 4.3 all-to-all-start.3
  584.9 5.6 fusion.15
  590.6 5.4 all-to-all-done.3.dealt_ref
  (397 shorter events, 178.7 us)
Async XLA Ops:
  7.2 28.7 %collective-permute-start.4 = (bf16[64,2048]{1,0:T(8,128)(2,1)}, bf16[64,2048]{1,0:T(8,128)(2,1)S(1)}, u32[]{:S(2)}, u32[]{:S(2)}) collective-permute-start(bf16[64,2048]{1,0:T(8,128)(2,1)} %param.22), channel_id=1, source_target_pairs={{0,8},{8,0},{16,24},{24,16},{1,9},{9,1},{17,25},{25,17},{2,10},{10... | collective-permute-start | bytes 786440 | tf_op jit(solution)/shard_map/ppermute | solution.py:850
  10.3 25.7 %collective-permute-start.5 = (bf16[64,2048]{1,0:T(8,128)(2,1)}, bf16[64,2048]{1,0:T(8,128)(2,1)S(1)}, u32[]{:S(2)}, u32[]{:S(2)}) collective-permute-start(bf16[64,2048]{1,0:T(8,128)(2,1)} %param.22), channel_id=1, source_target_pairs={{0,16},{8,24},{16,0},{24,8},{1,17},{9,25},{17,1},{25,9},{2,18},{10... | collective-permute-start | bytes 786440 | tf_op jit(solution)/shard_map/ppermute | solution.py:850
  23.0 51.2 %all-gather.5.cloned.1.call-start = ((), (), s32[]{:S(2)}) async-start(), calls=%async_computation.8 | async-start | bytes 1966080 | tf_op jit(solution)/shard_map/all_gather | solution.py:857
  37.1 75.2 %all-gather.7.cloned.1.call-start = ((), (), s32[]{:S(2)}) async-start(), calls=%async_computation.9 | async-start | bytes 1966080 | tf_op jit(solution)/shard_map/all_gather | solution.py:867
  41.9 26.8 %collective-permute-start.2 = (bf16[128,2048]{1,0:T(8,128)(2,1)S(1)}, bf16[128,2048]{1,0:T(8,128)(2,1)S(1)}, u32[]{:S(2)}, u32[]{:S(2)}) collective-permute-start(bf16[128,2048]{1,0:T(8,128)(2,1)S(1)} %get-tuple-element.246), channel_id=1, source_target_pairs={{0,4},{4,0},{1,5},{5,1},{2,6},{6,2},{3,7},{7,3},{8,12},{12,8},{9,1... | collective-permute-start | bytes 1572872 | tf_op jit(solution)/shard_map/ppermute | solution.py:89
  42.4 22.7 %collective-permute-start.1 = (bf16[128,2048]{1,0:T(8,128)(2,1)S(1)}, bf16[128,2048]{1,0:T(8,128)(2,1)S(1)}, u32[]{:S(2)}, u32[]{:S(2)}) collective-permute-start(bf16[128,2048]{1,0:T(8,128)(2,1)S(1)} %get-tuple-element.245), channel_id=1, source_target_pairs={{0,2},{2,0},{1,3},{3,1},{4,6},{6,4},{5,7},{7,5},{8,10},{10,8},{9,1... | collective-permute-start | bytes 1572872 | tf_op jit(solution)/shard_map/ppermute | solution.py:89
  42.8 25.2 %collective-permute-start.3 = (bf16[128,2048]{1,0:T(8,128)(2,1)S(1)}, bf16[128,2048]{1,0:T(8,128)(2,1)}, u32[]{:S(2)}, u32[]{:S(2)}) collective-permute-start(bf16[128,2048]{1,0:T(8,128)(2,1)S(1)} %get-tuple-element.245), channel_id=1, source_target_pairs={{0,4},{4,0},{1,5},{5,1},{2,6},{6,2},{3,7},{7,3},{8,12},{12,8},{9,1... | collective-permute-start | bytes 1572872 | tf_op jit(solution)/shard_map/ppermute | solution.py:89
  44.5 47.4 %collective-permute-start.14 = (bf16[256,2048]{1,0:T(8,128)(2,1)}, bf16[256,2048]{1,0:T(8,128)(2,1)}, u32[]{:S(2)}, u32[]{:S(2)}) collective-permute-start(bf16[256,2048]{1,0:T(8,128)(2,1)} %fusion.9.others_0_), channel_id=1, source_target_pairs={{0,1},{1,0},{2,3},{3,2},{4,5},{5,4},{6,7},{7,6},{8,9},{9,8},{10,11... | collective-permute-start | bytes 3145736 | tf_op jit(solution)/shard_map/ppermute | solution.py:89
  55.2 36.1 %collective-permute-start.12 = (bf16[128,2048]{1,0:T(8,128)(2,1)S(1)}, bf16[128,2048]{1,0:T(8,128)(2,1)}, u32[]{:S(2)}, u32[]{:S(2)}) collective-permute-start(bf16[128,2048]{1,0:T(8,128)(2,1)S(1)} %collective-permute-done.others_1_), channel_id=1, source_target_pairs={{0,4},{4,0},{1,5},{5,1},{2,6},{6,2},{3,7},{7,3},{8,12},{12,8},{9,1... | collective-permute-start | bytes 1572872 | tf_op jit(solution)/shard_map/ppermute | solution.py:89
  65.1 27.0 %collective-permute-start.15 = (bf16[128,2048]{1,0:T(8,128)(2,1)S(1)}, bf16[128,2048]{1,0:T(8,128)(2,1)}, u32[]{:S(2)}, u32[]{:S(2)}) collective-permute-start(bf16[128,2048]{1,0:T(8,128)(2,1)S(1)} %collective-permute-done.others_1_), channel_id=1, source_target_pairs={{0,1},{1,0},{2,3},{3,2},{4,5},{5,4},{6,7},{7,6},{8,9},{9,8},{10,11... | collective-permute-start | bytes 1572872 | tf_op jit(solution)/shard_map/ppermute | solution.py:89
  68.1 23.5 %collective-permute-start.13 = (bf16[128,2048]{1,0:T(8,128)(2,1)}, bf16[128,2048]{1,0:T(8,128)(2,1)}, u32[]{:S(2)}, u32[]{:S(2)}) collective-permute-start(bf16[128,2048]{1,0:T(8,128)(2,1)} %collective-permute-done.3.others_4_), channel_id=1, source_target_pairs={{0,2},{2,0},{1,3},{3,1},{4,6},{6,4},{5,7},{7,5},{8,10},{10,8},{9,1... | collective-permute-start | bytes 1572872 | tf_op jit(solution)/shard_map/ppermute | solution.py:89
  85.0 120.3 %all-gather.9.cloned.1.call-start = ((), (), s32[]{:S(2)}) async-start(), calls=%async_computation.10 | async-start | bytes 5242880 | tf_op jit(solution)/shard_map/all_gather | solution.py:876
  85.8 31.8 %collective-permute-start.29 = (bf16[4,1,64,2048]{3,2,1,0:T(8,128)(2,1)}, bf16[4,1,64,2048]{3,2,1,0:T(8,128)(2,1)}, u32[]{:S(2)}, u32[]{:S(2)}) collective-permute-start(bf16[4,1,64,2048]{3,2,1,0:T(8,128)(2,1)} %bitcast_dynamic-update-slice_fusion), channel_id=1, source_target_pairs={{0,1},{1,0},{2,3},{3,2},{4,5},{5,4},{6,7},{7,6},{8,9},{9,8},{10,11... | collective-permute-start | bytes 3145736 | tf_op jit(solution)/shard_map/ppermute | solution.py:89
  91.4 22.6 %collective-permute-start.16 = (bf16[128,2048]{1,0:T(8,128)(2,1)S(1)}, bf16[128,2048]{1,0:T(8,128)(2,1)}, u32[]{:S(2)}, u32[]{:S(2)}) collective-permute-start(bf16[128,2048]{1,0:T(8,128)(2,1)S(1)} %collective-permute-done.1.others_2_), channel_id=1, source_target_pairs={{0,1},{1,0},{2,3},{3,2},{4,5},{5,4},{6,7},{7,6},{8,9},{9,8},{10,11... | collective-permute-start | bytes 1572872 | tf_op jit(solution)/shard_map/ppermute | solution.py:89
  91.6 22.5 %collective-permute-start.17 = (bf16[128,2048]{1,0:T(8,128)(2,1)S(1)}, bf16[128,2048]{1,0:T(8,128)(2,1)S(1)}, u32[]{:S(2)}, u32[]{:S(2)}) collective-permute-start(bf16[128,2048]{1,0:T(8,128)(2,1)S(1)} %collective-permute-done.2.others_3_), channel_id=1, source_target_pairs={{0,1},{1,0},{2,3},{3,2},{4,5},{5,4},{6,7},{7,6},{8,9},{9,8},{10,11... | collective-permute-start | bytes 1572872 | tf_op jit(solution)/shard_map/ppermute | solution.py:89
  91.9 23.7 %collective-permute-start.18 = (bf16[128,2048]{1,0:T(8,128)(2,1)}, bf16[128,2048]{1,0:T(8,128)(2,1)}, u32[]{:S(2)}, u32[]{:S(2)}) collective-permute-start(bf16[128,2048]{1,0:T(8,128)(2,1)} %collective-permute-done.3.others_4_), channel_id=1, source_target_pairs={{0,1},{1,0},{2,3},{3,2},{4,5},{5,4},{6,7},{7,6},{8,9},{9,8},{10,11... | collective-permute-start | bytes 1572872 | tf_op jit(solution)/shard_map/ppermute | solution.py:89
  92.1 25.0 %collective-permute-start.19 = (bf16[128,2048]{1,0:T(8,128)(2,1)}, bf16[128,2048]{1,0:T(8,128)(2,1)}, u32[]{:S(2)}, u32[]{:S(2)}) collective-permute-start(bf16[128,2048]{1,0:T(8,128)(2,1)} %collective-permute-done.12.others_5_), channel_id=1, source_target_pairs={{0,1},{1,0},{2,3},{3,2},{4,5},{5,4},{6,7},{7,6},{8,9},{9,8},{10,11... | collective-permute-start | bytes 1572872 | tf_op jit(solution)/shard_map/ppermute | solution.py:89
  112.4 172.1 %all-gather.11.cloned.1.call-start = ((), (), s32[]{:S(2)}) async-start(), calls=%async_computation.11 | async-start | bytes 5242880 | tf_op jit(solution)/shard_map/all_gather | solution.py:877
  114.0 25.0 %collective-permute-start.21 = (bf16[128,2048]{1,0:T(8,128)(2,1)S(1)}, bf16[128,2048]{1,0:T(8,128)(2,1)S(1)}, u32[]{:S(2)}, u32[]{:S(2)}) collective-permute-start(bf16[128,2048]{1,0:T(8,128)(2,1)S(1)} %get-tuple-element.244), channel_id=1, source_target_pairs={{0,2},{2,0},{1,3},{3,1},{4,6},{6,4},{5,7},{7,5},{8,10},{10,8},{9,1... | collective-permute-start | bytes 1572872 | tf_op jit(solution)/shard_map/ppermute | solution.py:89
  115.6 26.4 %collective-permute-start.23 = (bf16[128,2048]{1,0:T(8,128)(2,1)S(1)}, bf16[128,2048]{1,0:T(8,128)(2,1)S(1)}, u32[]{:S(2)}, u32[]{:S(2)}) collective-permute-start(bf16[128,2048]{1,0:T(8,128)(2,1)S(1)} %get-tuple-element.244), channel_id=1, source_target_pairs={{0,4},{4,0},{1,5},{5,1},{2,6},{6,2},{3,7},{7,3},{8,12},{12,8},{9,1... | collective-permute-start | bytes 1572872 | tf_op jit(solution)/shard_map/ppermute | solution.py:89
  117.1 25.0 %collective-permute-start.22 = (bf16[128,2048]{1,0:T(8,128)(2,1)S(1)}, bf16[128,2048]{1,0:T(8,128)(2,1)S(1)}, u32[]{:S(2)}, u32[]{:S(2)}) collective-permute-start(bf16[128,2048]{1,0:T(8,128)(2,1)S(1)} %get-tuple-element.243), channel_id=1, source_target_pairs={{0,2},{2,0},{1,3},{3,1},{4,6},{6,4},{5,7},{7,5},{8,10},{10,8},{9,1... | collective-permute-start | bytes 1572872 | tf_op jit(solution)/shard_map/ppermute | solution.py:89
  117.6 23.2 %collective-permute-start.24 = (bf16[128,2048]{1,0:T(8,128)(2,1)S(1)}, bf16[128,2048]{1,0:T(8,128)(2,1)S(1)}, u32[]{:S(2)}, u32[]{:S(2)}) collective-permute-start(bf16[128,2048]{1,0:T(8,128)(2,1)S(1)} %get-tuple-element.243), channel_id=1, source_target_pairs={{0,4},{4,0},{1,5},{5,1},{2,6},{6,2},{3,7},{7,3},{8,12},{12,8},{9,1... | collective-permute-start | bytes 1572872 | tf_op jit(solution)/shard_map/ppermute | solution.py:89
  139.0 23.3 %collective-permute-start.27 = (bf16[128,2048]{1,0:T(8,128)(2,1)S(1)}, bf16[128,2048]{1,0:T(8,128)(2,1)S(1)}, u32[]{:S(2)}, u32[]{:S(2)}) collective-permute-start(bf16[128,2048]{1,0:T(8,128)(2,1)S(1)} %collective-permute-done.21.others_8_), channel_id=1, source_target_pairs={{0,4},{4,0},{1,5},{5,1},{2,6},{6,2},{3,7},{7,3},{8,12},{12,8},{9,1... | collective-permute-start | bytes 1572872 | tf_op jit(solution)/shard_map/ppermute | solution.py:89
  140.8 21.5 %collective-permute-start.28 = (bf16[128,2048]{1,0:T(8,128)(2,1)S(1)}, bf16[128,2048]{1,0:T(8,128)(2,1)S(1)}, u32[]{:S(2)}, u32[]{:S(2)}) collective-permute-start(bf16[128,2048]{1,0:T(8,128)(2,1)S(1)} %collective-permute-done.24.others_11_), channel_id=1, source_target_pairs={{0,2},{2,0},{1,3},{3,1},{4,6},{6,4},{5,7},{7,5},{8,10},{10,8},{9,1... | collective-permute-start | bytes 1572872 | tf_op jit(solution)/shard_map/ppermute | solution.py:89
  167.3 23.7 %collective-permute-start.30 = (bf16[128,2048]{1,0:T(8,128)(2,1)S(1)}, bf16[128,2048]{1,0:T(8,128)(2,1)S(1)}, u32[]{:S(2)}, u32[]{:S(2)}) collective-permute-start(bf16[128,2048]{1,0:T(8,128)(2,1)S(1)} %get-tuple-element.213), channel_id=1, source_target_pairs={{0,4},{4,0},{1,5},{5,1},{2,6},{6,2},{3,7},{7,3},{8,12},{12,8},{9,1... | collective-permute-start | bytes 1572872 | tf_op jit(solution)/shard_map/ppermute | solution.py:89
  167.9 23.9 %collective-permute-start.35 = (bf16[128,2048]{1,0:T(8,128)(2,1)S(1)}, bf16[128,2048]{1,0:T(8,128)(2,1)S(1)}, u32[]{:S(2)}, u32[]{:S(2)}) collective-permute-start(bf16[128,2048]{1,0:T(8,128)(2,1)S(1)} %get-tuple-element.214), channel_id=1, source_target_pairs={{0,2},{2,0},{1,3},{3,1},{4,6},{6,4},{5,7},{7,5},{8,10},{10,8},{9,1... | collective-permute-start | bytes 1572872 | tf_op jit(solution)/shard_map/ppermute | solution.py:89
  180.9 21.1 %collective-permute-start.32 = (bf16[128,2048]{1,0:T(8,128)(2,1)S(1)}, bf16[128,2048]{1,0:T(8,128)(2,1)S(1)}, u32[]{:S(2)}, u32[]{:S(2)}) collective-permute-start(bf16[128,2048]{1,0:T(8,128)(2,1)S(1)} %get-tuple-element.217), channel_id=1, source_target_pairs={{0,2},{2,0},{1,3},{3,1},{4,6},{6,4},{5,7},{7,5},{8,10},{10,8},{9,1... | collective-permute-start | bytes 1572872 | tf_op jit(solution)/shard_map/ppermute | solution.py:89
  205.4 46.3 %collective-permute-start.39 = (bf16[2048,1024]{1,0:T(8,128)(2,1)}, bf16[2048,1024]{1,0:T(8,128)(2,1)}, u32[]{:S(2)}, u32[]{:S(2)}) collective-permute-start(bf16[2048,1024]{1,0:T(8,128)(2,1)} %all-gather.9.cloned.1.call-done.mine_ref.up_mine_ref), channel_id=1, source_target_pairs={{0,1},{1,0},{2,3},{3,2},{4,5},{5,4},{6,7},{7,6},{8,9},{9,8},{10,11... | collective-permute-start | bytes 12582920 | tf_op jit(solution)/shard_map/ppermute | solution.py:89
  205.4 189.2 %reduce-scatter.5.cloned.1.call-start = ((), (), s32[]{:S(2)}) async-start(), calls=%async_computation.12 | async-start | bytes 5242880 | tf_op jit(solution)/shard_map/reduce_scatter | solution.py:919
  228.9 22.8 %collective-permute-start.44 = (bf16[128,2048]{1,0:T(8,128)(2,1)}, bf16[128,2048]{1,0:T(8,128)(2,1)}, u32[]{:S(2)}, u32[]{:S(2)}) collective-permute-start(bf16[128,2048]{1,0:T(8,128)(2,1)} %collective-permute-done.40.others_1_), channel_id=1, source_target_pairs={{0,4},{4,0},{1,5},{5,1},{2,6},{6,2},{3,7},{7,3},{8,12},{12,8},{9,1... | collective-permute-start | bytes 1572872 | tf_op jit(solution)/shard_map/ppermute | solution.py:89
  229.7 22.0 %collective-permute-start.45 = (bf16[128,2048]{1,0:T(8,128)(2,1)}, bf16[128,2048]{1,0:T(8,128)(2,1)}, u32[]{:S(2)}, u32[]{:S(2)}) collective-permute-start(bf16[128,2048]{1,0:T(8,128)(2,1)} %collective-permute-done.43.others_4_), channel_id=1, source_target_pairs={{0,2},{2,0},{1,3},{3,1},{4,6},{6,4},{5,7},{7,5},{8,10},{10,8},{9,1... | collective-permute-start | bytes 1572872 | tf_op jit(solution)/shard_map/ppermute | solution.py:89
  299.0 171.8 %reduce-scatter.7.cloned.1.call-start = ((), (), s32[]{:S(2)}) async-start(), calls=%async_computation.13 | async-start | bytes 5242880 | tf_op jit(solution)/shard_map/reduce_scatter | solution.py:945
  330.1 23.7 %collective-permute-start.49 = (bf16[128,2048]{1,0:T(8,128)(2,1)S(1)}, bf16[128,2048]{1,0:T(8,128)(2,1)S(1)}, u32[]{:S(2)}, u32[]{:S(2)}) collective-permute-start(bf16[128,2048]{1,0:T(8,128)(2,1)S(1)} %get-tuple-element.210), channel_id=1, source_target_pairs={{0,4},{4,0},{1,5},{5,1},{2,6},{6,2},{3,7},{7,3},{8,12},{12,8},{9,1... | collective-permute-start | bytes 1572872 | tf_op jit(solution)/shard_map/ppermute | solution.py:89
  332.0 22.6 %collective-permute-start.50 = (bf16[128,2048]{1,0:T(8,128)(2,1)S(1)}, bf16[128,2048]{1,0:T(8,128)(2,1)S(1)}, u32[]{:S(2)}, u32[]{:S(2)}) collective-permute-start(bf16[128,2048]{1,0:T(8,128)(2,1)S(1)} %get-tuple-element.209), channel_id=1, source_target_pairs={{0,2},{2,0},{1,3},{3,1},{4,6},{6,4},{5,7},{7,5},{8,10},{10,8},{9,1... | collective-permute-start | bytes 1572872 | tf_op jit(solution)/shard_map/ppermute | solution.py:89
  362.3 23.9 %collective-permute-start.57 = (bf16[2048,1024]{1,0:T(8,128)(2,1)S(1)}, bf16[2048,1024]{1,0:T(8,128)(2,1)S(1)}, u32[]{:S(2)}, u32[]{:S(2)}) collective-permute-start(bf16[2048,1024]{1,0:T(8,128)(2,1)S(1)} %convolution_convert_fusion.1), channel_id=1, source_target_pairs={{0,1},{1,0},{2,3},{3,2},{4,5},{5,4},{6,7},{7,6},{8,9},{9,8},{10,11... | collective-permute-start | bytes 12582920 | tf_op jit(solution)/shard_map/ppermute | solution.py:89
  394.6 147.0 %reduce-scatter.9.cloned.1.call-start = ((), (), s32[]{:S(2)}) async-start(), calls=%async_computation.14 | async-start | bytes 3932160 | tf_op jit(solution)/shard_map/reduce_scatter | solution.py:971
  397.2 23.8 %collective-permute-start.59 = (bf16[128,2048]{1,0:T(8,128)(2,1)S(1)}, bf16[128,2048]{1,0:T(8,128)(2,1)S(1)}, u32[]{:S(2)}, u32[]{:S(2)}) collective-permute-start(bf16[128,2048]{1,0:T(8,128)(2,1)S(1)} %get-tuple-element.239), channel_id=1, source_target_pairs={{0,2},{2,0},{1,3},{3,1},{4,6},{6,4},{5,7},{7,5},{8,10},{10,8},{9,1... | collective-permute-start | bytes 1572872 | tf_op jit(solution)/shard_map/ppermute | solution.py:89
  398.4 23.8 %collective-permute-start.60 = (bf16[128,2048]{1,0:T(8,128)(2,1)S(1)}, bf16[128,2048]{1,0:T(8,128)(2,1)S(1)}, u32[]{:S(2)}, u32[]{:S(2)}) collective-permute-start(bf16[128,2048]{1,0:T(8,128)(2,1)S(1)} %get-tuple-element.240), channel_id=1, source_target_pairs={{0,4},{4,0},{1,5},{5,1},{2,6},{6,2},{3,7},{7,3},{8,12},{12,8},{9,1... | collective-permute-start | bytes 1572872 | tf_op jit(solution)/shard_map/ppermute | solution.py:89
  437.3 33.4 %collective-permute-start.69 = (bf16[128,2048]{1,0:T(8,128)(2,1)S(1)}, bf16[128,2048]{1,0:T(8,128)(2,1)S(1)}, u32[]{:S(2)}, u32[]{:S(2)}) collective-permute-start(bf16[128,2048]{1,0:T(8,128)(2,1)S(1)} %get-tuple-element.206), channel_id=1, source_target_pairs={{0,4},{4,0},{1,5},{5,1},{2,6},{6,2},{3,7},{7,3},{8,12},{12,8},{9,1... | collective-permute-start | bytes 1572872 | tf_op jit(solution)/shard_map/ppermute | solution.py:89
  438.9 31.9 %collective-permute-start.70 = (bf16[128,2048]{1,0:T(8,128)(2,1)S(1)}, bf16[128,2048]{1,0:T(8,128)(2,1)S(1)}, u32[]{:S(2)}, u32[]{:S(2)}) collective-permute-start(bf16[128,2048]{1,0:T(8,128)(2,1)S(1)} %get-tuple-element.205), channel_id=1, source_target_pairs={{0,2},{2,0},{1,3},{3,1},{4,6},{6,4},{5,7},{7,5},{8,10},{10,8},{9,1... | collective-permute-start | bytes 1572872 | tf_op jit(solution)/shard_map/ppermute | solution.py:89
  439.7 31.1 %collective-permute-start.71 = (bf16[128,2048]{1,0:T(8,128)(2,1)S(1)}, bf16[128,2048]{1,0:T(8,128)(2,1)S(1)}, u32[]{:S(2)}, u32[]{:S(2)}) collective-permute-start(bf16[128,2048]{1,0:T(8,128)(2,1)S(1)} %get-tuple-element.204), channel_id=1, source_target_pairs={{0,4},{4,0},{1,5},{5,1},{2,6},{6,2},{3,7},{7,3},{8,12},{12,8},{9,1... | collective-permute-start | bytes 1572872 | tf_op jit(solution)/shard_map/ppermute | solution.py:89
  440.6 30.2 %collective-permute-start.72 = (bf16[128,2048]{1,0:T(8,128)(2,1)S(1)}, bf16[128,2048]{1,0:T(8,128)(2,1)S(1)}, u32[]{:S(2)}, u32[]{:S(2)}) collective-permute-start(bf16[128,2048]{1,0:T(8,128)(2,1)S(1)} %get-tuple-element.203), channel_id=1, source_target_pairs={{0,2},{2,0},{1,3},{3,1},{4,6},{6,4},{5,7},{7,5},{8,10},{10,8},{9,1... | collective-permute-start | bytes 1572872 | tf_op jit(solution)/shard_map/ppermute | solution.py:89
  510.1 34.6 %collective-permute-start.75 = (bf16[128,2048]{1,0:T(8,128)(2,1)}, bf16[128,2048]{1,0:T(8,128)(2,1)}, u32[]{:S(2)}, u32[]{:S(2)}) collective-permute-start(bf16[128,2048]{1,0:T(8,128)(2,1)} %slice.339), channel_id=1, source_target_pairs={{0,4},{4,0},{1,5},{5,1},{2,6},{6,2},{3,7},{7,3},{8,12},{12,8},{9,1... | collective-permute-start | bytes 1572872 | tf_op jit(solution)/shard_map/ppermute | solution.py:89
  511.9 32.8 %collective-permute-start.80 = (bf16[128,2048]{1,0:T(8,128)(2,1)}, bf16[128,2048]{1,0:T(8,128)(2,1)}, u32[]{:S(2)}, u32[]{:S(2)}) collective-permute-start(bf16[128,2048]{1,0:T(8,128)(2,1)} %slice.345), channel_id=1, source_target_pairs={{0,2},{2,0},{1,3},{3,1},{4,6},{6,4},{5,7},{7,5},{8,10},{10,8},{9,1... | collective-permute-start | bytes 1572872 | tf_op jit(solution)/shard_map/ppermute | solution.py:89
  521.1 23.7 %collective-permute-start.77 = (bf16[128,2048]{1,0:T(8,128)(2,1)}, bf16[128,2048]{1,0:T(8,128)(2,1)}, u32[]{:S(2)}, u32[]{:S(2)}) collective-permute-start(bf16[128,2048]{1,0:T(8,128)(2,1)} %add_convert_fusion.8), channel_id=1, source_target_pairs={{0,2},{2,0},{1,3},{3,1},{4,6},{6,4},{5,7},{7,5},{8,10},{10,8},{9,1... | collective-permute-start | bytes 1572872 | tf_op jit(solution)/shard_map/ppermute | solution.py:89
  523.8 20.9 %collective-permute-start.79 = (bf16[128,2048]{1,0:T(8,128)(2,1)}, bf16[128,2048]{1,0:T(8,128)(2,1)}, u32[]{:S(2)}, u32[]{:S(2)}) collective-permute-start(bf16[128,2048]{1,0:T(8,128)(2,1)} %add_convert_fusion.7), channel_id=1, source_target_pairs={{0,4},{4,0},{1,5},{5,1},{2,6},{6,2},{3,7},{7,3},{8,12},{12,8},{9,1... | collective-permute-start | bytes 1572872 | tf_op jit(solution)/shard_map/ppermute | solution.py:89
  544.7 20.9 %collective-permute-start.86 = (bf16[4,64,2048]{2,1,0:T(8,128)(2,1)}, bf16[4,64,2048]{2,1,0:T(8,128)(2,1)}, u32[]{:S(2)}, u32[]{:S(2)}) collective-permute-start(bf16[4,64,2048]{2,1,0:T(8,128)(2,1)} %get-tuple-element.220), channel_id=1, source_target_pairs={{0,1},{1,0},{2,3},{3,2},{4,5},{5,4},{6,7},{7,6},{8,9},{9,8},{10,11... | collective-permute-start | bytes 3145736 | tf_op jit(solution)/shard_map/ppermute | solution.py:89
  565.6 37.5 %reduce-scatter.11.cloned.1.call-start = ((), (), s32[]{:S(2)}) async-start(), calls=%async_computation.15 | async-start | bytes 1310720 | tf_op jit(solution)/shard_map/reduce_scatter | solution.py:223
  (105 other events, 1356.6 us)
Sparse Core Ops, SparseCore 0:
  37.2 36.9 all-gather.4
  76.3 35.9 all-gather.6
  113.9 79.6 all-gather.8
  205.5 78.8 all-gather.10
  299.1 74.7 reduce-scatter.4
  394.7 74.2 reduce-scatter.6
  482.7 58.8 reduce-scatter.8
  568.7 30.3 reduce-scatter.10
